TPU v7x, 32 devices: a whole 2x2x4 slice. The times are simulated.
32 devices in a mesh: group: 2 (over x), row: 8 (over z, y), expert: 2 (over core).
Axes of the slice: x: 2, y: 2, z: 4, core: 2. Of those that a mesh axis runs over, the one named last changes fastest.
Arguments:
- tokens: bfloat16 [2, 128, 128, 1024], P('group', ('row', 'expert')), parts along dimension 0, may hold values from -30 to 30
- ln_first: float32 [1024], replicated, may hold values from 0.5 to 1.5
- spec_first: bfloat16 [2, 8, 128, 128], replicated, may hold values from -0.375 to 0.375
- spec_second: bfloat16 [2, 8, 128, 128], replicated, may hold values from -0.375 to 0.375
- spec_bias: float32 [2, 1024], replicated, may hold values from -3 to 3
- ln_second: float32 [1024], replicated, may hold values from 0.5 to 1.5
- routing: int32 [2, 128, 128, 4], P('group', ('row', 'expert')), parts along dimension 0, may hold values from 0 to 3, as said below
- combine: float32 [2, 128, 128, 4], P('group', ('row', 'expert')), parts along dimension 0, may hold values from 0.1 to 0.6
- up_weight: bfloat16 [8, 1024, 1536], P('row'), may hold values from -0.1875 to 0.1875
- down_weight: bfloat16 [8, 1536, 1024], P('row'), may hold values from -0.109375 to 0.109375
Outputs:
- block_out: bfloat16 [2, 128, 128, 1024], P('group', ('row', 'expert')), parts along dimension 0
There are 2 independent parts, one for each index of `group`. A program takes and returns all parts, laid end to end along the dimension named above; an argument that names none is the same for every part. Nothing has to cross between parts.
Inputs may be any that keep to these rules, and one draw needn't show every extreme that they name: `routing`: each token names 4 different experts, and the 1024 tokens held by each index of row+expert name every expert exactly 1024 times.
All inputs are finite; a program needn't handle non-finite values.
Results may differ from a plain program's by a relative error of at most 0.006.
Values may be sent and summed in bfloat16 or wider, within the bound.
No kernel may reach another device: no remote copies, remote signals or barrier semaphores. Data moves between devices by JAX's collectives and lax.ppermute only.
A program may use at most 128 MiB of HBM per device.

v0:
```python
import math

import jax
import jax.numpy as jnp
from jax import lax
from jax.sharding import PartitionSpec as P


def from_partner(value, axis, stride):
    mask = 2**stride
    pairs = [(source, source ^ mask) for source in range(lax.axis_size(axis))]
    return lax.ppermute(value, axis, pairs)


def twiddle(length):
    counter = jnp.arange(length, dtype=jnp.float32)
    angle = 2.0 * math.pi / length * jnp.mod(jnp.outer(counter, counter), float(length))
    return (jnp.cos(angle), jnp.sin(angle))


def layer_norm(values, gain):
    values = values.astype(jnp.float32)
    center = values - jnp.mean(values, axis=-1, keepdims=True)
    spread = jnp.mean(center * center, axis=-1, keepdims=True)
    return center * lax.rsqrt(spread + 1e-05) * gain


def product(left, right, form):
    return jnp.einsum(form, left, right, preferred_element_type=jnp.float32)


def complex_blocks(real_in, imag_in, weight):
    form = "ghkbi,bio->ghkbo"
    real_out = product(real_in, weight[0], form) - product(imag_in, weight[1], form)
    imag_out = product(real_in, weight[1], form) + product(imag_in, weight[0], form)
    return (real_out, imag_out)


def block_mlp(modes, first, second, bias):
    dims = modes.shape
    nblocks = first.shape[1]
    bwidth = first.shape[2]
    real_part = modes[:, 0].reshape(dims[0], dims[2], dims[3], nblocks, bwidth)
    imag_part = modes[:, 1].reshape(dims[0], dims[2], dims[3], nblocks, bwidth)
    hid_real, hid_imag = complex_blocks(real_part, imag_part, first)
    hid_real = jax.nn.relu(hid_real + bias[0].reshape(nblocks, bwidth)).astype(jnp.bfloat16)
    hid_imag = jax.nn.relu(hid_imag + bias[1].reshape(nblocks, bwidth)).astype(jnp.bfloat16)
    out_real, out_imag = complex_blocks(hid_real, hid_imag, second)
    return jnp.stack([out_real, out_imag], axis=1).reshape(dims).astype(jnp.bfloat16)


def run_expert(arrived, up_full, down_full):
    in_shape = arrived.shape
    width = arrived.shape[2]
    hidden = jax.nn.gelu(
        jnp.dot(arrived.reshape(-1, width), up_full, preferred_element_type=jnp.float32),
        approximate=True,
    ).astype(jnp.bfloat16)
    partial_out = jnp.dot(hidden, down_full, preferred_element_type=jnp.float32).reshape(
        in_shape[0], in_shape[1], width
    )
    return lax.all_to_all(
        partial_out.astype(jnp.bfloat16), "row", split_axis=0, concat_axis=0, tiled=True
    ).astype(partial_out.dtype)


def per_device(
    tokens,
    ln_first,
    spec_first,
    spec_second,
    spec_bias,
    ln_second,
    routing,
    combine,
    up_weight,
    down_weight,
):
    grid_len = tokens.shape[2]
    width = tokens.shape[3]
    cosine, sine = twiddle(grid_len)
    forward_cols = jnp.stack([cosine, -sine], axis=1).astype(jnp.bfloat16)
    forward_rows = jnp.stack(
        [jnp.stack([cosine, sine], axis=1), jnp.stack([-sine, cosine], axis=1)], axis=0
    ).astype(jnp.bfloat16)
    inverse_rows = jnp.stack(
        [jnp.stack([cosine, -sine], axis=1), jnp.stack([sine, cosine], axis=1)], axis=0
    ).astype(jnp.bfloat16)
    inverse_cols = jnp.stack([cosine, -sine], axis=0).astype(jnp.bfloat16)
    normed_first = layer_norm(tokens, ln_first).astype(jnp.bfloat16)
    col_spec = product(normed_first, forward_cols, "ghwd,wck->gchkd").astype(jnp.bfloat16)
    by_column = lax.all_to_all(col_spec, ("row", "expert"), split_axis=3, concat_axis=2, tiled=True)
    modes = (product(forward_rows, by_column, "amch,gchkd->gamkd") * (1.0 / grid_len)).astype(
        jnp.bfloat16
    )
    mixed_modes = block_mlp(modes, spec_first, spec_second, spec_bias)
    row_back = product(inverse_rows, mixed_modes, "amch,gchkd->gamkd").astype(jnp.bfloat16)
    by_row = lax.all_to_all(row_back, ("row", "expert"), split_axis=2, concat_axis=3, tiled=True)
    mixing = product(by_row, inverse_cols, "gchkd,ckw->ghwd") * (1.0 / grid_len)
    residual = (tokens.astype(jnp.float32) + mixing).astype(jnp.bfloat16)
    normed = layer_norm(residual, ln_second).astype(jnp.bfloat16).reshape(-1, width)
    n_tokens = normed.shape[0]
    top_count = routing.shape[-1]
    experts = lax.axis_size("row") // 2
    capacity = n_tokens * top_count // experts
    flat_route = routing.reshape(-1)
    one_hot = (flat_route[:, None] == jnp.arange(experts, dtype=jnp.int32)[None, :]).astype(
        jnp.int32
    )
    earlier = jnp.cumsum(one_hot, axis=0) - one_hot
    slot_index = flat_route * capacity + jnp.sum(earlier * one_hot, axis=1)
    token_of = jnp.arange(n_tokens * top_count, dtype=jnp.int32) // top_count
    source_row = jnp.zeros((experts * capacity,), jnp.int32).at[slot_index].set(token_of)
    send_rows = normed[source_row].reshape(experts, capacity, width)
    partner_up, partner_down = from_partner((up_weight, down_weight), "row", 0)
    up_full = jnp.concatenate([up_weight[0], partner_up[0]], axis=1)
    down_full = jnp.concatenate([down_weight[0], partner_down[0]], axis=0)
    outgoing = send_rows.reshape(experts * 2, capacity // 2, width)
    returned = run_expert(
        lax.all_to_all(outgoing, "row", split_axis=0, concat_axis=0, tiled=True), up_full, down_full
    )
    results = returned.reshape(experts, capacity, width)
    gathered = results.reshape(-1, width)[slot_index].reshape(n_tokens, top_count, width)
    moe_out = jnp.sum(gathered * combine.reshape(n_tokens, top_count, 1), axis=1)
    final = residual.reshape(-1, width).astype(jnp.float32) + moe_out
    return final.reshape(tokens.shape).astype(jnp.bfloat16)


def solution(mesh):
    placed = (
        P("group", ("row", "expert"), None, None),
        P(),
        P(),
        P(),
        P(),
        P(),
        P("group", ("row", "expert"), None, None),
        P("group", ("row", "expert"), None, None),
        P("row", None, None),
        P("row", None, None),
    )
    return jax.shard_map(
        per_device,
        mesh=mesh,
        in_specs=placed,
        out_specs=P("group", ("row", "expert"), None, None),
        check_vma=False,
    )
```

profile of v0, /device:TPU:0, one launch (start us, length us, event | category | flops | bytes accessed | tf_op | source)
XLA Modules:
  0.0 795.2 jit_solution(12745327477111533011)
XLA Ops:
  2.4 2.3 fusion.22
  6.1 4.3 copy.64
  10.4 7.7 all-to-all-start
  18.8 76.9 %all-to-all-done = bf16[1,2,8,128,1024]{4,2,1,0,3:T(8,128)(2,1)} async-done(((bf16[1,2,8,128,1024]{4,2,1,0,3:T(8,128)(2,1)}), bf16[1,2,8,128,1024]{4,2,1,0,3:T(8,128)(2,1)}, u32[]{:S(2)}, u32[]{:S(2)}) %all-to-all-start) | async-done | bytes 4194336 | tf_op jit(solution)/shard_map/all_to_all | solution.py:92
  95.7 4.5 copy.137
  100.7 5.6 fusion.27
  115.0 3.2 fusion.28
  118.2 11.2 %copy.80 = bf16[1,2,128,8,1024]{4,1,3,0,2:T(2,128)(2,1)} copy(bf16[1,2,128,8,1024]{2,4,1,3,0:T(8,128)(2,1)} %fusion.28) | data formatting | bytes 8388608 | tf_op jit(solution)/shard_map/convert_element_type | solution.py:97
  129.4 19.8 %all-to-all-start.1 = ((bf16[1,2,128,8,1024]{4,1,3,0,2:T(2,128)(2,1)}), bf16[1,2,128,8,1024]{4,1,3,0,2:T(2,128)(2,1)}, u32[]{:S(2)}, u32[]{:S(2)}) async-start(bf16[1,2,128,8,1024]{4,1,3,0,2:T(2,128)(2,1)} %copy.80), calls=%async_computation.1 | async-start | bytes 8388608 | tf_op jit(solution)/shard_map/all_to_all | solution.py:98
  152.5 15.5 %scatter_custom_fusion = s32[4096]{0:T(1024)S(1)} fusion(s32[4096]{0:T(1024)S(1)} %bitcast.233, s32[4096]{0:T(1024)S(1)} %add_select_fusion.2, s32[]{:T(128)} %constant.50.clone.1), kind=kCustom, calls=%fused_computation.156 | custom fusion | bytes 16388 | tf_op jit(solution)/shard_map/scatter | solution.py:113
  168.4 58.6 %all-to-all-done.1 = bf16[1,2,128,8,1024]{4,1,3,0,2:T(2,128)(2,1)} async-done(((bf16[1,2,128,8,1024]{4,1,3,0,2:T(2,128)(2,1)}), bf16[1,2,128,8,1024]{4,1,3,0,2:T(2,128)(2,1)}, u32[]{:S(2)}, u32[]{:S(2)}) %all-to-all-start.1) | async-done | bytes 4194336 | tf_op jit(solution)/shard_map/all_to_all | solution.py:98
  227.0 3.5 copy.81
  233.7 18.3 %gather_fusion = bf16[4096,1024]{1,0:T(8,128)(2,1)} fusion(bf16[1024,1024]{1,0:T(8,128)(2,1)S(1)} %bitcast.220, s32[4096]{0:T(1024)S(1)} %fusion.113), kind=kCustom, calls=%fused_computation | custom fusion | bytes 16793600 | tf_op jit(solution)/shard_map/gather | solution.py:114
  252.0 19.8 %all-to-all-start.2 = ((bf16[8,512,1024]{2,1,0:T(8,128)(2,1)}), bf16[8,512,1024]{2,1,0:T(8,128)(2,1)}, u32[]{:S(2)}, u32[]{:S(2)}) async-start(bf16[8,512,1024]{2,1,0:T(8,128)(2,1)} %bitcast.221), calls=%async_computation.2 | async-start | bytes 16777216 | tf_op jit(solution)/shard_map/all_to_all | solution.py:120
  273.9 159.1 %collective-permute-done = bf16[1,1024,1536]{2,1,0:T(8,128)(2,1)} collective-permute-done((bf16[1,1024,1536]{2,1,0:T(8,128)(2,1)S(1)}, bf16[1,1024,1536]{2,1,0:T(8,128)(2,1)}, u32[]{:S(2)}, u32[]{:S(2)}) %collective-permute-start) | collective-permute-done | bytes 3145760 | tf_op jit(solution)/shard_map/ppermute | solution.py:12
  433.0 22.6 %all-to-all-done.2 = bf16[8,512,1024]{2,1,0:T(8,128)(2,1)} async-done(((bf16[8,512,1024]{2,1,0:T(8,128)(2,1)}), bf16[8,512,1024]{2,1,0:T(8,128)(2,1)}, u32[]{:S(2)}, u32[]{:S(2)}) %all-to-all-start.2) | async-done | bytes 8388640 | tf_op jit(solution)/shard_map/all_to_all | solution.py:120
  455.6 45.2 %fusion.7 = bf16[4096,3072]{1,0:T(8,128)(2,1)} fusion(bf16[4096,1024]{1,0:T(8,128)(2,1)} %bitcast.80, bf16[1024,1536]{1,0:T(8,128)(2,1)} %bitcast.82, bf16[1024,1536]{1,0:T(8,128)(2,1)S(1)} %bitcast.240), kind=kOutput, calls=%fused_computation.11 | convolution fusion | flops 25895632896 | bytes 39845888 | tf_op jit(solution)/shard_map/dot_general | solution.py:56
  500.8 32.6 %convolution_convert_fusion = bf16[4096,1024]{1,0:T(8,128)(2,1)} fusion(bf16[4096,3072]{1,0:T(8,128)(2,1)} %fusion.7, bf16[1536,1024]{1,0:T(8,128)(2,1)} %bitcast.84, bf16[1536,1024]{1,0:T(8,128)(2,1)} %bitcast.241), kind=kOutput, calls=%fused_computation.17 | convolution fusion | flops 25786580992 | bytes 39845888 | tf_op jit(solution)/shard_map/dot_general | solution.py:59
  533.4 5.1 all-to-all-start.3
  538.8 182.3 %all-to-all-done.3 = bf16[8,512,1024]{2,1,0:T(8,128)(2,1)} async-done(((bf16[8,512,1024]{2,1,0:T(8,128)(2,1)}), bf16[8,512,1024]{2,1,0:T(8,128)(2,1)}, u32[]{:S(2)}, u32[]{:S(2)}) %all-to-all-start.3) | async-done | bytes 8388640 | tf_op jit(solution)/shard_map/all_to_all | solution.py:62
  721.1 11.3 %bitcast_convert_fusion = f32[4096,1024]{1,0:T(8,128)} fusion(bf16[8,512,1024]{2,1,0:T(8,128)(2,1)} %all-to-all-done.3), kind=kLoop, calls=%fused_computation.13 | loop fusion | flops 4194304 | bytes 25165824 | tf_op jit(solution)/shard_map/reshape;reshape | solution.py:123
  732.3 28.1 %gather_fusion.1 = f32[4096,1024]{1,0:T(8,128)} fusion(f32[4096,1024]{1,0:T(8,128)} %bitcast_convert_fusion, s32[4096]{0:T(1024)S(1)} %broadcast_clamp_fusion), kind=kCustom, calls=%fused_computation.1 | custom fusion | bytes 33570816 | tf_op jit(solution)/shard_map/gather | solution.py:123
  760.4 19.0 %reshape.316 = f32[1024,4,1024]{2,1,0:T(4,128)} reshape(f32[4096,1024]{1,0:T(8,128)} %gather_fusion.1) | data formatting | bytes 33554432 | tf_op jit(solution)/shard_map/reshape | solution.py:123
  779.4 13.4 %multiply_reduce_fusion = f32[1024,1024]{1,0:T(8,128)S(1)} fusion(f32[1024,4,1024]{2,1,0:T(4,128)} %reshape.316, f32[1024,4]{1,0:T(8,128)S(1)} %copy.87), kind=kLoop, calls=%fused_computation.12 | loop fusion | flops 7340032 | bytes 20987904 | tf_op jit(solution)/shard_map/reduce_sum | solution.py:124
  (75 shorter events, 24.7 us)
Async XLA Ops:
  0.0 4.7 copy-start
  0.0 4.7 copy-start.11
  10.4 8.4 %copy-start.9 = (f32[2,1024]{1,0:T(2,128)S(1)}, f32[2,1024]{1,0:T(2,128)}, u32[]{:S(2)}) copy-start(f32[2,1024]{1,0:T(2,128)} %param.14) | copy-start | bytes 24580
  10.4 85.3 %all-to-all-start = ((bf16[1,2,8,128,1024]{4,2,1,0,3:T(8,128)(2,1)}), bf16[1,2,8,128,1024]{4,2,1,0,3:T(8,128)(2,1)}, u32[]{:S(2)}, u32[]{:S(2)}) async-start(bf16[1,2,8,128,1024]{4,2,1,0,3:T(8,128)(2,1)} %copy.64), calls=%async_computation | async-start | bytes 8388608 | tf_op jit(solution)/shard_map/all_to_all | solution.py:92
  106.2 1.0 copy-start.3
  108.9 1.2 copy-start.4
  129.4 19.8 %copy-start.5 = (s32[1,8,128,4]{2,3,1,0:T(4,128)S(1)}, s32[1,8,128,4]{2,3,1,0:T(4,128)}, u32[]{:S(2)}) copy-start(s32[1,8,128,4]{2,3,1,0:T(4,128)} %param.16) | copy-start | bytes 49156
  129.4 97.5 %all-to-all-start.1 = ((bf16[1,2,128,8,1024]{4,1,3,0,2:T(2,128)(2,1)}), bf16[1,2,128,8,1024]{4,1,3,0,2:T(2,128)(2,1)}, u32[]{:S(2)}, u32[]{:S(2)}) async-start(bf16[1,2,128,8,1024]{4,1,3,0,2:T(2,128)(2,1)} %copy.80), calls=%async_computation.1 | async-start | bytes 8388608 | tf_op jit(solution)/shard_map/all_to_all | solution.py:98
  152.5 15.5 %copy-start.6 = (s32[4096,1]{0,1:T(1,128)}, s32[4096,1]{0,1:T(1,128)S(1)}, u32[]{:S(2)}) copy-start(s32[4096,1]{0,1:T(1,128)S(1)} %compare_select_fusion) | copy-start | bytes 49156
  230.5 2.6 copy-start.10
  231.7 1.3 copy-start.1
  252.0 19.8 %copy-start.12 = (bf16[1,1024,1536]{2,1,0:T(8,128)(2,1)S(1)}, bf16[1,1024,1536]{2,1,0:T(8,128)(2,1)}, u32[]{:S(2)}) copy-start(bf16[1,1024,1536]{2,1,0:T(8,128)(2,1)} %param.18) | copy-start | bytes 9437188
  252.0 203.6 %all-to-all-start.2 = ((bf16[8,512,1024]{2,1,0:T(8,128)(2,1)}), bf16[8,512,1024]{2,1,0:T(8,128)(2,1)}, u32[]{:S(2)}, u32[]{:S(2)}) async-start(bf16[8,512,1024]{2,1,0:T(8,128)(2,1)} %bitcast.221), calls=%async_computation.2 | async-start | bytes 16777216 | tf_op jit(solution)/shard_map/all_to_all | solution.py:120
  271.8 161.1 %collective-permute-start = (bf16[1,1024,1536]{2,1,0:T(8,128)(2,1)S(1)}, bf16[1,1024,1536]{2,1,0:T(8,128)(2,1)}, u32[]{:S(2)}, u32[]{:S(2)}) collective-permute-start(bf16[1,1024,1536]{2,1,0:T(8,128)(2,1)S(1)} %copy-done.12), channel_id=1, source_target_pairs={{0,2},{2,0},{4,6},{6,4},{8,10},{10,8},{12,14},{14,12},{1,3},{3,1},... | collective-permute-start | bytes 9437192 | tf_op jit(solution)/shard_map/ppermute | solution.py:12
  273.8 227.0 %collective-permute-start.1 = (bf16[1,1536,1024]{2,1,0:T(8,128)(2,1)}, bf16[1,1536,1024]{2,1,0:T(8,128)(2,1)}, u32[]{:S(2)}, u32[]{:S(2)}) collective-permute-start(bf16[1,1536,1024]{2,1,0:T(8,128)(2,1)} %param.19), channel_id=1, source_target_pairs={{0,2},{2,0},{4,6},{6,4},{8,10},{10,8},{12,14},{14,12},{1,3},{3,1},... | collective-permute-start | bytes 9437192 | tf_op jit(solution)/shard_map/ppermute | solution.py:12
  533.4 5.1 copy-start.8
  533.4 5.3 copy-start.7
  533.4 187.7 %all-to-all-start.3 = ((bf16[8,512,1024]{2,1,0:T(8,128)(2,1)}), bf16[8,512,1024]{2,1,0:T(8,128)(2,1)}, u32[]{:S(2)}, u32[]{:S(2)}) async-start(bf16[8,512,1024]{2,1,0:T(8,128)(2,1)} %bitcast.228), calls=%async_computation.3 | async-start | bytes 16777216 | tf_op jit(solution)/shard_map/all_to_all | solution.py:62
  779.4 13.4 %copy-start.2 = (bf16[1,8,128,1024]{3,2,1,0:T(8,128)(2,1)S(1)}, bf16[1,8,128,1024]{3,2,1,0:T(8,128)(2,1)}, u32[]{:S(2)}) copy-start(bf16[1,8,128,1024]{3,2,1,0:T(8,128)(2,1)} %copy-done.1) | copy-start | bytes 6291460
where the time goes:
time: 801 us; the launch traced here: 795 us
  waiting for transfers between devices  499 us (62%)
  local copies, waits for them, and re-layouts  109 us (14%)
  matrix products  96.5 us (12%)
  starting transfers between devices  54.6 us (7%)
  other arithmetic  35.4 us (4%)
    all_to_all x1, waiting for transfers between devices, run_expert(): lax.all_to_all(partial_out.astype(jnp.bfloat16), 'row', split_axis=0, con...  182 us
    ppermute x2, waiting for transfers between devices, from_partner(): return lax.ppermute(value, axis, pairs)  159 us
    all_to_all x1, waiting for transfers between devices, per_device(): lax.all_to_all(col_spec, ('row', 'expert'), split_axis=3, concat_axis=2,...  76.9 us
    all_to_all x1, waiting for transfers between devices, per_device(): lax.all_to_all(row_back, ('row', 'expert'), split_axis=2, concat_axis=3,...  58.6 us
    dot_general x1, matrix products, run_expert(): jnp.dot(arrived.reshape(-1, width), up_full, preferred_element_type=jnp.f...  45.2 us
    dot_general x1, matrix products, run_expert(): jnp.dot(hidden, down_full, preferred_element_type=jnp.float32)  32.6 us
    gather x1, local copies, waits for them, and re-layouts, per_device(): results.reshape(-1, width)[slot_index].reshape(n_tokens, top_count, width)  28.1 us
    all_to_all x1, waiting for transfers between devices, per_device(): lax.all_to_all(outgoing, 'row', split_axis=0, concat_axis=0, tiled=True)  22.6 us
  transfers between devices with their start and end apart: 6, of which 5 were waited for; matrix products, arithmetic and copies ran while one was open for 8% of the time, Pallas kernels for 0%

commit v1 on v0

v1 whole, which is shorter than its diff:
```python
import functools
import math

import jax
import jax.numpy as jnp
import ml_dtypes
import numpy as np
from jax import lax
from jax.experimental import pallas as pl
from jax.experimental.pallas import tpu as pltpu
from jax.sharding import PartitionSpec as P

MIB = 1 << 20


def exchange(value, axis, mask):
    pairs = [(source, source ^ mask) for source in range(lax.axis_size(axis))]
    return lax.ppermute(value, axis, pairs)


def mxu(left, right):
    return jnp.dot(left, right, preferred_element_type=jnp.float32)


def normalize(values, gain):
    center = values - jnp.mean(values, axis=-1, keepdims=True)
    spread = jnp.mean(center * center, axis=-1, keepdims=True)
    return center * lax.rsqrt(spread + 1e-05) * gain


def trig(grid_len):
    counter = np.arange(grid_len)
    angle = 2.0 * math.pi / grid_len * (np.outer(counter, counter) % grid_len)
    cosine = np.round(np.cos(angle), 12).astype(ml_dtypes.bfloat16).astype(np.float64)
    sine = np.round(np.sin(angle), 12).astype(ml_dtypes.bfloat16).astype(np.float64)
    return cosine, sine


def column_tables(grid_len, n_dev, rows_local):
    cosine, sine = trig(grid_len)
    packed = grid_len // 2
    per_dev = packed // n_dev
    part = np.stack([cosine[:packed], -sine[:packed]], axis=1)
    part[0, 1] = cosine[packed]
    part = part.reshape(n_dev, per_dev, 2, grid_len)
    forward = np.zeros((per_dev, n_dev, rows_local, 2, rows_local, grid_len))
    for row in range(rows_local):
        forward[:, :, row, :, row, :] = part.transpose(1, 0, 2, 3)
    forward = forward.reshape(per_dev, n_dev * rows_local * 2, rows_local * grid_len)
    inverse = forward.transpose(0, 2, 1) / grid_len
    return forward.astype(ml_dtypes.bfloat16), inverse.astype(ml_dtypes.bfloat16)


def row_tables(grid_len):
    c, s = trig(grid_len)
    z = np.zeros_like(c)

    def assemble(blocks):
        array = np.array(blocks)
        return array.transpose(0, 1, 3, 4, 2).reshape(4 * grid_len, 2 * grid_len)

    plain_fwd = assemble([[[c, s], [-s, c]], [[c, -s], [-s, -c]]]) / grid_len
    first_fwd = assemble([[[c, z], [-s, z]], [[z, c], [z, -s]]]) / grid_len
    plain_inv = assemble([[[c, s], [-s, c]], [[c, -s], [-s, -c]]]).T
    first_inv = assemble([[[c, z], [-s, z]], [[z, c], [z, -s]]]).T
    kinds = lambda first, plain: np.stack([first, plain]).astype(ml_dtypes.bfloat16)
    return kinds(first_fwd, plain_fwd), kinds(first_inv, plain_inv)


def spectra_kernel(tokens, gain, table, out, normed):
    tile = 128
    width = tokens.shape[1]

    def norm_tile(index, carry):
        rows = pl.ds(pl.multiple_of(index * tile, tile), tile)
        values = tokens[rows, :].astype(jnp.float32)
        normed[rows, :] = normalize(values, gain[...]).astype(normed.dtype)
        return carry

    lax.fori_loop(0, tokens.shape[0] // tile, norm_tile, 0)
    for column in range(table.shape[0]):
        out[:, column * width : (column + 1) * width] = mxu(table[column], normed[...]).astype(out.dtype)


def column_spectra(tokens, gain, table):
    per_dev, rows_out, rows_in = table.shape
    width = tokens.shape[1]
    return pl.pallas_call(
        spectra_kernel,
        out_shape=jax.ShapeDtypeStruct((rows_out, per_dev * width), jnp.bfloat16),
        in_specs=[pl.BlockSpec(memory_space=pltpu.VMEM)] * 3,
        out_specs=pl.BlockSpec(memory_space=pltpu.VMEM),
        scratch_shapes=[pltpu.VMEM((rows_in, width), jnp.bfloat16)],
        compiler_params=pltpu.CompilerParams(vmem_limit_bytes=32 * MIB),
        cost_estimate=pl.CostEstimate(
            flops=2 * per_dev * rows_out * rows_in * width,
            bytes_accessed=2 * (rows_in * width + rows_out * per_dev * width + table.size),
            transcendentals=0,
        ),
        name="column_spectra",
    )(tokens, gain, table)


def modes_kernel(spectra, forward, first, second, bias, inverse, out, mixed):
    n_blocks, pair, _ = first.shape
    block = pair // 2
    grid_len = spectra.shape[0] // 2
    modes = mxu(forward[0], spectra[...]).astype(jnp.bfloat16)
    for index in range(n_blocks):
        lanes = slice(index * block, (index + 1) * block)
        sides = [
            jnp.concatenate(
                [
                    modes[2 * sign * grid_len : (2 * sign + 1) * grid_len, lanes],
                    modes[(2 * sign + 1) * grid_len : (2 * sign + 2) * grid_len, lanes],
                ],
                axis=1,
            )
            for sign in range(2)
        ]
        hid = mxu(jnp.concatenate(sides, axis=0), first[index])
        hid = jnp.maximum(hid + bias[index : index + 1, :], 0.0).astype(jnp.bfloat16)
        result = mxu(hid, second[index]).astype(jnp.bfloat16)
        for sign in range(2):
            for part in range(2):
                base = (2 * sign + part) * grid_len
                mixed[base : base + grid_len, lanes] = result[
                    sign * grid_len : (sign + 1) * grid_len, part * block : (part + 1) * block
                ]
    out[...] = mxu(inverse[0], mixed[...]).astype(out.dtype)


def mix_modes(spectra, forward, first, second, bias, inverse, width):
    rows, lanes = spectra.shape
    per_dev = lanes // width
    modes_rows = forward.shape[1]
    kind = lambda k: (jnp.minimum(k, 1), 0, 0)
    whole3 = lambda k: (0, 0, 0)
    return pl.pallas_call(
        modes_kernel,
        grid=(per_dev,),
        out_shape=jax.ShapeDtypeStruct((rows, lanes), jnp.bfloat16),
        in_specs=[
            pl.BlockSpec((rows, width), lambda k: (0, k)),
            pl.BlockSpec((1,) + forward.shape[1:], kind),
            pl.BlockSpec(first.shape, whole3),
            pl.BlockSpec(second.shape, whole3),
            pl.BlockSpec(bias.shape, lambda k: (0, 0)),
            pl.BlockSpec((1,) + inverse.shape[1:], kind),
        ],
        out_specs=pl.BlockSpec((rows, width), lambda k: (0, k)),
        scratch_shapes=[pltpu.VMEM((modes_rows, width), jnp.bfloat16)],
        compiler_params=pltpu.CompilerParams(vmem_limit_bytes=32 * MIB),
        cost_estimate=pl.CostEstimate(
            flops=2 * lanes * (2 * rows * modes_rows + modes_rows * 512),
            bytes_accessed=4 * (rows * lanes + first.size),
            transcendentals=0,
        ),
        name="mix_modes",
    )(spectra, forward, first, second, bias, inverse)


def residual_kernel(spectra, table, tokens, gain, residual, normed):
    width = tokens.shape[1]
    total = tokens[...].astype(jnp.float32)
    mixing = None
    for column in range(table.shape[0]):
        term = mxu(table[column], spectra[:, column * width : (column + 1) * width])
        mixing = term if mixing is None else mixing + term
    rounded = (total + mixing).astype(jnp.bfloat16)
    residual[...] = rounded
    normed[...] = normalize(rounded.astype(jnp.float32), gain[...]).astype(jnp.bfloat16)


def add_mixing(spectra, table, tokens, gain):
    per_dev, rows_out, rows_in = table.shape
    width = tokens.shape[1]
    tile = math.gcd(rows_out, 256)
    out = jax.ShapeDtypeStruct((rows_out, width), jnp.bfloat16)
    row_tile = pl.BlockSpec((tile, width), lambda i: (i, 0))
    return pl.pallas_call(
        residual_kernel,
        grid=(rows_out // tile,),
        out_shape=(out, out),
        in_specs=[
            pl.BlockSpec(spectra.shape, lambda i: (0, 0)),
            pl.BlockSpec((per_dev, tile, rows_in), lambda i: (0, i, 0)),
            row_tile,
            pl.BlockSpec(gain.shape, lambda i: (0, 0)),
        ],
        out_specs=(row_tile, row_tile),
        compiler_params=pltpu.CompilerParams(vmem_limit_bytes=32 * MIB),
        cost_estimate=pl.CostEstimate(
            flops=2 * per_dev * rows_out * rows_in * width,
            bytes_accessed=2 * (3 * rows_out * width + spectra.size + table.size),
            transcendentals=0,
        ),
        name="add_mixing",
    )(spectra, table, tokens, gain)


def experts_kernel(n_blocks, n_parts, tile, chunk, normed, weights, *refs):
    per_block = [1] + [n_parts] * (n_blocks - 1)
    n_pieces = sum(per_block)
    ups, downs = refs[:n_pieces], refs[n_pieces : 2 * n_pieces]
    out, up_all, down_all, up_sem, down_sem = refs[2 * n_pieces :]
    hidden = up_all.shape[2]
    copies = []
    piece = 0
    for block, parts in enumerate(per_block):
        size = hidden // parts
        for part in range(parts):
            units = pl.ds(part * size, size)
            copies.append(
                (
                    block,
                    pltpu.make_async_copy(ups[piece], up_all.at[block, :, units], up_sem.at[piece]),
                    pltpu.make_async_copy(downs[piece], down_all.at[block, units, :], down_sem.at[piece]),
                )
            )
            piece += 1
    for _, up_copy, down_copy in copies:
        up_copy.start()
        down_copy.start()
    for block in range(n_blocks):
        for owner, up_copy, down_copy in copies:
            if owner == block:
                up_copy.wait()
                down_copy.wait()

        def token_tile(index, carry, block=block):
            rows = pl.ds(pl.multiple_of(index * tile, tile), tile)
            values = normed[rows, :]
            total = None
            for start in range(0, hidden, chunk):
                units = slice(start, start + chunk)
                act = jax.nn.gelu(mxu(values, up_all[block, :, units]), approximate=True)
                term = mxu(act.astype(jnp.bfloat16), down_all[block, units, :])
                total = term if total is None else total + term
            column = block // 2
            total = total * weights[rows, column : column + 1]
            if block > 0:
                total = total + out[rows, :]
            out[rows, :] = total
            return carry

        lax.fori_loop(0, normed.shape[0] // tile, token_tile, 0)


def run_experts(normed, weights, blocks, tile=256, chunk=512):
    rows, width = normed.shape
    ups = [up for block in blocks for up, _ in block]
    downs = [down for block in blocks for _, down in block]
    n_blocks = len(blocks)
    hidden = blocks[0][0][0].shape[1]
    chunk = math.gcd(chunk, hidden)
    n_parts = len(blocks[-1])
    vmem = pl.BlockSpec(memory_space=pltpu.VMEM)
    return pl.pallas_call(
        functools.partial(experts_kernel, n_blocks, n_parts, tile, chunk),
        out_shape=jax.ShapeDtypeStruct((rows, width), jnp.float32),
        in_specs=[vmem, vmem] + [pl.BlockSpec(memory_space=pl.ANY)] * (2 * len(ups)),
        out_specs=vmem,
        scratch_shapes=[
            pltpu.VMEM((n_blocks, width, hidden), jnp.bfloat16),
            pltpu.VMEM((n_blocks, hidden, width), jnp.bfloat16),
            pltpu.SemaphoreType.DMA((len(ups),)),
            pltpu.SemaphoreType.DMA((len(ups),)),
        ],
        compiler_params=pltpu.CompilerParams(vmem_limit_bytes=56 * MIB),
        cost_estimate=pl.CostEstimate(
            flops=4 * rows * width * hidden * n_blocks,
            bytes_accessed=4 * width * hidden * n_blocks + 8 * rows * width,
            transcendentals=rows * hidden * n_blocks,
        ),
        name="experts",
    )(normed, weights, *ups, *downs)


def expert_weights(routing, combine, experts):
    return jnp.stack(
        [jnp.sum(jnp.where(routing == expert, combine, 0.0), axis=-1) for expert in experts], axis=-1
    )


def gather_blocks(up, down):
    n_parts = lax.axis_size("group") * lax.axis_size("expert")
    part = lax.axis_index("group") * lax.axis_size("expert") + lax.axis_index("expert")
    size = up.shape[1] // n_parts
    mine = (
        lax.dynamic_slice_in_dim(up, part * size, size, axis=1),
        lax.dynamic_slice_in_dim(down, part * size, size, axis=0),
    )
    far = exchange(mine, "row", 4)
    near = exchange(mine, "row", 1)
    far_near = exchange(far, "row", 1)
    blocks = [[(up, down)]]
    for piece in (near, far, far_near):
        other = exchange(piece, "group", 1)
        blocks.append([piece, other, exchange(piece, "expert", 1), exchange(other, "expert", 1)])
    return blocks


def all_experts(residual, normed, routing, combine, up_weight, down_weight):
    mine = lax.axis_index("row") // 2
    flat = lambda value: value.reshape(-1, value.shape[-1])
    weights = lambda first: expert_weights(flat(routing), flat(combine), (first, first ^ 2))
    other_weights = exchange(weights(mine ^ 1).T, "row", 2).T
    blocks = gather_blocks(up_weight[0], down_weight[0])
    other = exchange(normed, "row", 2)
    own_out = run_experts(normed, weights(mine), blocks)
    other_out = run_experts(other, other_weights, blocks).astype(jnp.bfloat16)
    returned = exchange(other_out, "row", 2)
    return residual.astype(jnp.float32) + own_out + returned.astype(jnp.float32)


def routed_experts(residual, normed, routing, combine, up_weight, down_weight):
    n_tokens, width = normed.shape
    top_count = routing.shape[-1]
    experts = lax.axis_size("row") // 2
    capacity = n_tokens * top_count // experts
    flat_route = routing.reshape(-1)
    one_hot = (flat_route[:, None] == jnp.arange(experts, dtype=jnp.int32)[None, :]).astype(jnp.int32)
    earlier = jnp.cumsum(one_hot, axis=0) - one_hot
    slot_index = flat_route * capacity + jnp.sum(earlier * one_hot, axis=1)
    token_of = jnp.arange(n_tokens * top_count, dtype=jnp.int32) // top_count
    source_row = jnp.zeros((experts * capacity,), jnp.int32).at[slot_index].set(token_of)
    send_rows = normed[source_row].reshape(experts, capacity, width)
    partner_up, partner_down = exchange((up_weight, down_weight), "row", 1)
    up_full = jnp.concatenate([up_weight[0], partner_up[0]], axis=1)
    down_full = jnp.concatenate([down_weight[0], partner_down[0]], axis=0)
    outgoing = send_rows.reshape(experts * 2, capacity // 2, width)
    arrived = lax.all_to_all(outgoing, "row", split_axis=0, concat_axis=0, tiled=True)
    hidden = jax.nn.gelu(mxu(arrived.reshape(-1, width), up_full), approximate=True).astype(jnp.bfloat16)
    partial_out = mxu(hidden, down_full).reshape(arrived.shape).astype(jnp.bfloat16)
    returned = lax.all_to_all(partial_out, "row", split_axis=0, concat_axis=0, tiled=True)
    gathered = returned.reshape(-1, width)[slot_index].reshape(n_tokens, top_count, width)
    scaled = gathered.astype(jnp.float32) * combine.reshape(n_tokens, top_count, 1)
    return residual.astype(jnp.float32) + jnp.sum(scaled, axis=1)


def complex_weight(weight):
    real, imag = weight[0], weight[1]
    return jnp.concatenate(
        [jnp.concatenate([real, imag], axis=2), jnp.concatenate([-imag, real], axis=2)], axis=1
    )


def per_device(
    tokens,
    ln_first,
    spec_first,
    spec_second,
    spec_bias,
    ln_second,
    routing,
    combine,
    up_weight,
    down_weight,
):
    _, rows_local, grid_len, width = tokens.shape
    axes = ("row", "expert")
    n_dev = lax.axis_size(axes)
    n_blocks = spec_first.shape[1]
    forward_cols, inverse_cols = column_tables(grid_len, n_dev, rows_local)
    forward_rows, inverse_rows = row_tables(grid_len)
    first_device = lax.axis_index(axes) == 0
    pick = lambda table: jnp.stack([jnp.where(first_device, table[0], table[1]), table[1]])
    flat_tokens = tokens.reshape(-1, width)

    spectra = column_spectra(flat_tokens, ln_first.reshape(1, width), jnp.asarray(forward_cols))
    by_column = lax.all_to_all(
        spectra.reshape(n_dev, -1, spectra.shape[1]), axes, split_axis=0, concat_axis=0, tiled=True
    )
    bias = spec_bias.reshape(2, n_blocks, -1).transpose(1, 0, 2).reshape(n_blocks, -1)
    mixed = mix_modes(
        by_column.reshape(spectra.shape),
        pick(forward_rows),
        complex_weight(spec_first),
        complex_weight(spec_second),
        bias,
        pick(inverse_rows),
        width,
    )
    by_row = lax.all_to_all(
        mixed.reshape(n_dev, -1, mixed.shape[1]), axes, split_axis=0, concat_axis=0, tiled=True
    )
    residual, normed = add_mixing(
        by_row.reshape(mixed.shape), jnp.asarray(inverse_cols), flat_tokens, ln_second.reshape(1, width)
    )
    pairs = lax.axis_size("group") == 2 and lax.axis_size("expert") == 2
    every_expert = lax.axis_size("row") == 2 * routing.shape[-1] and routing.shape[-1] == 4
    moe = all_experts if pairs and every_expert else routed_experts
    final = moe(residual, normed, routing, combine, up_weight, down_weight)
    return final.astype(jnp.bfloat16).reshape(tokens.shape)


def solution(mesh):
    placed = (
        P("group", ("row", "expert"), None, None),
        P(),
        P(),
        P(),
        P(),
        P(),
        P("group", ("row", "expert"), None, None),
        P("group", ("row", "expert"), None, None),
        P("row", None, None),
        P("row", None, None),
    )
    return jax.shard_map(
        per_device,
        mesh=mesh,
        in_specs=placed,
        out_specs=P("group", ("row", "expert"), None, None),
        check_vma=False,
    )
```

time: 801 us -> 375 us (0.47)
  waiting for transfers between devices: 499 us -> 204 us
  Pallas kernels: 0 us -> 97.1 us
  matrix products: 96.5 us -> 0 us
  local copies, waits for them, and re-layouts: 109 us -> 21.4 us
  other arithmetic: 35.4 us -> 12.4 us
  starting transfers between devices: 54.6 us -> 38 us
    all_to_all x4 -> x2, waiting for transfers between devices: 340 us -> 35.8 us  [the longest x1 35.8 us: per_device(): lax.all_to_all(spectra.reshape(n_dev, -1, spectra.shape[1]), axes, split_...]
    pallas_call x0 -> x5, Pallas kernels: none -> 97.1 us  [the longest x2 81.8 us: run_experts(): pl.pallas_call(functools.partial(experts_kernel, n_blocks, n_parts, tile,...]
    dot_general x14 -> x0, matrix products: 96.5 us -> none  [the longest x1 45.2 us: run_expert(): jnp.dot(arrived.reshape(-1, width), up_full, preferred_element_type=jnp.f...]
    gather x2 -> x0, local copies, waits for them, and re-layouts: 46.4 us -> none  [the longest x1 28.1 us: per_device(): results.reshape(-1, width)[slot_index].reshape(n_tokens, top_count, width)]
    all_to_all x4 -> x2, starting transfers between devices: 52.5 us -> 18.9 us  [the longest x1 11.4 us: per_device(): lax.all_to_all(mixed.reshape(n_dev, -1, mixed.shape[1]), axes, split_axis...]
    reshape x1 -> x0, local copies, waits for them, and re-layouts: 19 us -> none  [per_device(): results.reshape(-1, width)[slot_index].reshape(n_tokens, top_count, width)]
    reduce_sum x5 -> x1, other arithmetic: 18.6 us -> 0.05 us  [expert_weights(): jnp.sum(jnp.where(routing == expert, combine, 0.0), axis=-1)]
    ppermute x2 -> x27, starting transfers between devices: 2.09 us -> 19.1 us  [exchange(): return lax.ppermute(value, axis, pairs)]
  transfers between devices with their start and end apart: 6 -> 29, of which waited for: 5 -> 13; matrix products, arithmetic and copies ran while one was open for 8% -> 2% of each run, Pallas kernels for 0% -> 12%
where the time goes in v1:
time: 375 us; the launch traced here: 374 us
  waiting for transfers between devices  204 us (54%)
  Pallas kernels  97.1 us (26%)
  starting transfers between devices  38 us (10%)
  local copies, waits for them, and re-layouts  21.4 us (6%)
  other arithmetic  12.4 us (3%)
    ppermute x27, waiting for transfers between devices, exchange(): return lax.ppermute(value, axis, pairs)  169 us
    pallas_call x2, Pallas kernels, run_experts(): pl.pallas_call(functools.partial(experts_kernel, n_blocks, n_parts, tile,...  81.8 us
    all_to_all x1, waiting for transfers between devices, per_device(): lax.all_to_all(spectra.reshape(n_dev, -1, spectra.shape[1]), axes, split_...  35.8 us
    ppermute x27, starting transfers between devices, exchange(): return lax.ppermute(value, axis, pairs)  19.1 us
    unnamed x67, local copies, waits for them, and re-layouts  17.7 us
    all_to_all x1, starting transfers between devices, per_device(): lax.all_to_all(mixed.reshape(n_dev, -1, mixed.shape[1]), axes, split_axis...  11.4 us
    all_to_all x1, starting transfers between devices, per_device(): lax.all_to_all(spectra.reshape(n_dev, -1, spectra.shape[1]), axes, split_...  7.52 us
  transfers between devices with their start and end apart: 29, of which 13 were waited for; matrix products, arithmetic and copies ran while one was open for 2% of the time, Pallas kernels for 12%

profile of v1, /device:TPU:0, one launch (start us, length us, event | category | flops | bytes accessed | tf_op | source)
XLA Modules:
  0.0 373.7 jit_solution(9513110970262849069)
XLA Ops:
  3.9 4.4 %column_spectra.1 = bf16[256,4096]{1,0:T(8,128)(2,1)S(1)} custom-call(bf16[1024,1024]{1,0:T(8,128)(2,1)S(1)} %bitcast.50, f32[1,1024]{1,0:T(1,128)S(1)} %bitcast.52, bf16[4,256,1024]{2,1,0:T(8,128)(2,1)S(1)} %copy-done.12), custom_call_target="tpu_custom_call" | custom-call | flops 2147483648 | bytes 6291456 | tf_op jit(solution)/shard_map/column_spectra/pallas_call | solution.py:88
  9.6 7.5 %all-to-all-start = ((bf16[16,16,4096]{2,1,0:T(8,128)(2,1)}), bf16[16,16,4096]{2,1,0:T(8,128)(2,1)S(1)}, u32[]{:S(2)}, u32[]{:S(2)}) async-start(bf16[16,16,4096]{2,1,0:T(8,128)(2,1)} %bitcast.48), calls=%async_computation | async-start | bytes 4194304 | tf_op jit(solution)/shard_map/all_to_all | solution.py:372
  18.3 1.8 pad_maximum_fusion.forward
  22.4 35.8 %all-to-all-done = bf16[16,16,4096]{2,1,0:T(8,128)(2,1)S(1)} async-done(((bf16[16,16,4096]{2,1,0:T(8,128)(2,1)}), bf16[16,16,4096]{2,1,0:T(8,128)(2,1)S(1)}, u32[]{:S(2)}, u32[]{:S(2)}) %all-to-all-start) | async-done | bytes 2097184 | tf_op jit(solution)/shard_map/all_to_all | solution.py:372
  61.5 5.9 %mix_modes.1 = bf16[256,4096]{1,0:T(8,128)(2,1)S(1)} custom-call(bf16[256,4096]{1,0:T(8,128)(2,1)S(1)} %bitcast.47, bf16[2,512,256]{2,1,0:T(8,128)(2,1)S(1)} %copy-done.5, bf16[8,256,256]{2,1,0:T(8,128)(2,1)S(1)} %get-tuple-element.17.first, bf16[8,256,256]{2,1,0:T(8,128)(2,1)S(1)} %copy-done.4, f32[8,256]{1,0:T(8,128)S(1)} %bitcast.49, ...), custom_call_target="tpu_custom_call" | custom-call | flops 4294967296 | bytes 6291456 | tf_op jit(solution)/shard_map/mix_modes/pallas_call | solution.py:139
  68.8 11.4 %all-to-all-start.1 = ((bf16[16,16,4096]{2,1,0:T(8,128)(2,1)}), bf16[16,16,4096]{2,1,0:T(8,128)(2,1)S(1)}, u32[]{:S(2)}, u32[]{:S(2)}) async-start(bf16[16,16,4096]{2,1,0:T(8,128)(2,1)} %bitcast.46), calls=%async_computation.1 | async-start | bytes 4194304 | tf_op jit(solution)/shard_map/all_to_all | solution.py:385
  81.4 2.0 collective-permute-start
  83.4 2.4 collective-permute-start.4
  89.9 31.5 %collective-permute-done.refs_1_ = bf16[1024,384]{1,0:T(8,128)(2,1)} collective-permute-done((bf16[1024,384]{1,0:T(8,128)(2,1)S(1)}, bf16[1024,384]{1,0:T(8,128)(2,1)}, u32[]{:S(2)}, u32[]{:S(2)}) %collective-permute-start) | collective-permute-done | bytes 786464 | tf_op jit(solution)/shard_map/ppermute | solution.py:18
  123.0 20.6 %collective-permute-done.25 = f32[2,1024]{0,1:T(8,128)S(1)} collective-permute-done((f32[2,1024]{0,1:T(8,128)S(1)}, f32[2,1024]{0,1:T(8,128)S(1)}, u32[]{:S(2)}, u32[]{:S(2)}) %collective-permute-start.25) | collective-permute-done | bytes 8224 | tf_op jit(solution)/shard_map/ppermute | solution.py:18
  143.5 36.8 %collective-permute-done.4.refs_5_ = bf16[1024,384]{1,0:T(8,128)(2,1)} collective-permute-done((bf16[1024,384]{1,0:T(8,128)(2,1)S(1)}, bf16[1024,384]{1,0:T(8,128)(2,1)}, u32[]{:S(2)}, u32[]{:S(2)}) %collective-permute-start.4) | collective-permute-done | bytes 786464 | tf_op jit(solution)/shard_map/ppermute | solution.py:18
  181.9 14.9 %collective-permute-done.16.refs_18_ = bf16[384,1024]{1,0:T(8,128)(2,1)} collective-permute-done((bf16[384,1024]{1,0:T(8,128)(2,1)S(1)}, bf16[384,1024]{1,0:T(8,128)(2,1)}, u32[]{:S(2)}, u32[]{:S(2)}) %collective-permute-start.16) | collective-permute-done | bytes 786464 | tf_op jit(solution)/shard_map/ppermute | solution.py:18
  196.8 1.6 collective-permute-start.8
  200.7 15.3 %collective-permute-done.8.refs_9_ = bf16[1024,384]{1,0:T(8,128)(2,1)S(1)} collective-permute-done((bf16[1024,384]{1,0:T(8,128)(2,1)}, bf16[1024,384]{1,0:T(8,128)(2,1)S(1)}, u32[]{:S(2)}, u32[]{:S(2)}) %collective-permute-start.8) | collective-permute-done | bytes 786464 | tf_op jit(solution)/shard_map/ppermute | solution.py:18
  226.8 5.0 %add_mixing.1 = (bf16[1024,1024]{1,0:T(8,128)(2,1)S(1)}, bf16[1024,1024]{1,0:T(8,128)(2,1)}) custom-call(bf16[256,4096]{1,0:T(8,128)(2,1)S(1)} %bitcast.45, bf16[4,1024,256]{2,1,0:T(8,128)(2,1)S(1)} %copy-done.11, bf16[1024,1024]{1,0:T(8,128)(2,1)S(1)} %bitcast.51, f32[1,1024]{1,0:T(1,128)S(1)} %bitcast.53), custom_call_target="tpu_custom_call" | custom-call | flops 2147483648 | bytes 10485760 | tf_op jit(solution)/shard_map/add_mixing/pallas_call | solution.py:181
  231.8 2.3 collective-permute-done.17.refs_19_
  236.8 18.0 %collective-permute-done.9.refs_10_ = bf16[1024,384]{1,0:T(8,128)(2,1)} collective-permute-done((bf16[1024,384]{1,0:T(8,128)(2,1)S(1)}, bf16[1024,384]{1,0:T(8,128)(2,1)}, u32[]{:S(2)}, u32[]{:S(2)}) %collective-permute-start.9) | collective-permute-done | bytes 786464 | tf_op jit(solution)/shard_map/ppermute | solution.py:18
  255.4 13.6 %collective-permute-done.21.refs_23_ = bf16[384,1024]{1,0:T(8,128)(2,1)} collective-permute-done((bf16[384,1024]{1,0:T(8,128)(2,1)}, bf16[384,1024]{1,0:T(8,128)(2,1)}, u32[]{:S(2)}, u32[]{:S(2)}) %collective-permute-start.21) | collective-permute-done | bytes 786464 | tf_op jit(solution)/shard_map/ppermute | solution.py:18
  271.7 8.7 %collective-permute-done.24.normed = bf16[1024,1024]{1,0:T(8,128)(2,1)} collective-permute-done((bf16[1024,1024]{1,0:T(8,128)(2,1)}, bf16[1024,1024]{1,0:T(8,128)(2,1)}, u32[]{:S(2)}, u32[]{:S(2)}) %collective-permute-start.24) | collective-permute-done | bytes 2097184 | tf_op jit(solution)/shard_map/ppermute | solution.py:18
  280.4 40.9 %experts.3 = f32[1024,1024]{1,0:T(8,128)} custom-call(bf16[1024,1024]{1,0:T(8,128)(2,1)} %collective-permute-done.24.normed, f32[1024,2]{1,0:T(8,128)} %bitcast.64, bf16[1024,1536]{1,0:T(8,128)(2,1)} %bitcast.55, bf16[1024,384]{1,0:T(8,128)(2,1)} %collective-permute-done.refs_1_, bf16[1024,384]{1,0:T(8,128)(2,1)} %collective-permute-done.1.refs_2_, ...), custom_call_target="tpu_custom_call" | custom-call | flops 25769803776 | bytes 33554432 | tf_op jit(solution)/shard_map/experts/pallas_call | solution.py:259
  321.3 2.5 convert_element_type.13
  324.2 40.9 %experts.2 = f32[1024,1024]{1,0:T(8,128)} custom-call(bf16[1024,1024]{1,0:T(8,128)(2,1)} %get-tuple-element.8.normed, f32[1024,2]{1,0:T(8,128)} %copy.23.weights, bf16[1024,1536]{1,0:T(8,128)(2,1)} %bitcast.56, bf16[1024,384]{1,0:T(8,128)(2,1)} %collective-permute-done.refs_1_, bf16[1024,384]{1,0:T(8,128)(2,1)} %collective-permute-done.1.refs_2_, ...), custom_call_target="tpu_custom_call" | custom-call | flops 25769803776 | bytes 33554432 | tf_op jit(solution)/shard_map/experts/pallas_call | solution.py:259
  365.1 3.9 %collective-permute-done.26 = bf16[1024,1024]{1,0:T(8,128)(2,1)S(1)} collective-permute-done((bf16[1024,1024]{1,0:T(8,128)(2,1)S(1)}, bf16[1024,1024]{1,0:T(8,128)(2,1)S(1)}, u32[]{:S(2)}, u32[]{:S(2)}) %collective-permute-start.26) | collective-permute-done | bytes 2097184 | tf_op jit(solution)/shard_map/ppermute | solution.py:18
  369.0 4.7 %add_convert_fusion = bf16[1024,1024]{1,0:T(8,128)(2,1)} fusion(bf16[1024,1024]{1,0:T(8,128)(2,1)S(1)} %collective-permute-done.26, f32[1024,1024]{1,0:T(8,128)} %experts.2, bf16[1024,1024]{1,0:T(8,128)(2,1)S(1)} %get-tuple-element.7), kind=kLoop, calls=%fused_computation | loop fusion | flops 5242880 | bytes 10485760 | tf_op jit(solution)/shard_map/convert_element_type | solution.py:395
  (124 shorter events, 40.7 us)
Async XLA Ops:
  9.6 48.6 %all-to-all-start = ((bf16[16,16,4096]{2,1,0:T(8,128)(2,1)}), bf16[16,16,4096]{2,1,0:T(8,128)(2,1)S(1)}, u32[]{:S(2)}, u32[]{:S(2)}) async-start(bf16[16,16,4096]{2,1,0:T(8,128)(2,1)} %bitcast.48), calls=%async_computation | async-start | bytes 4194304 | tf_op jit(solution)/shard_map/all_to_all | solution.py:372
  68.8 151.9 %all-to-all-start.1 = ((bf16[16,16,4096]{2,1,0:T(8,128)(2,1)}), bf16[16,16,4096]{2,1,0:T(8,128)(2,1)S(1)}, u32[]{:S(2)}, u32[]{:S(2)}) async-start(bf16[16,16,4096]{2,1,0:T(8,128)(2,1)} %bitcast.46), calls=%async_computation.1 | async-start | bytes 4194304 | tf_op jit(solution)/shard_map/all_to_all | solution.py:385
  81.4 40.1 %collective-permute-start = (bf16[1024,384]{1,0:T(8,128)(2,1)S(1)}, bf16[1024,384]{1,0:T(8,128)(2,1)}, u32[]{:S(2)}, u32[]{:S(2)}) collective-permute-start(bf16[1024,384]{1,0:T(8,128)(2,1)S(1)} %dynamic-slice_bitcast_fusion.1), channel_id=1, source_target_pairs={{0,2},{2,0},{4,6},{6,4},{8,10},{10,8},{12,14},{14,12},{1,3},{3,1},... | collective-permute-start | bytes 2359304 | tf_op jit(solution)/shard_map/ppermute | solution.py:18
  83.4 97.0 %collective-permute-start.4 = (bf16[1024,384]{1,0:T(8,128)(2,1)S(1)}, bf16[1024,384]{1,0:T(8,128)(2,1)}, u32[]{:S(2)}, u32[]{:S(2)}) collective-permute-start(bf16[1024,384]{1,0:T(8,128)(2,1)S(1)} %dynamic-slice_bitcast_fusion.1), channel_id=1, source_target_pairs={{0,8},{2,10},{4,12},{6,14},{8,0},{10,2},{12,4},{14,6},{1,9},{3,11}... | collective-permute-start | bytes 2359304 | tf_op jit(solution)/shard_map/ppermute | solution.py:18
  86.0 57.5 %collective-permute-start.25 = (f32[2,1024]{0,1:T(8,128)S(1)}, f32[2,1024]{0,1:T(8,128)S(1)}, u32[]{:S(2)}, u32[]{:S(2)}) collective-permute-start(f32[2,1024]{0,1:T(8,128)S(1)} %bitcast.54), channel_id=1, source_target_pairs={{0,4},{2,6},{4,0},{6,2},{8,12},{10,14},{12,8},{14,10},{1,5},{3,7},... | collective-permute-start | bytes 24584 | tf_op jit(solution)/shard_map/ppermute | solution.py:18
  88.7 93.1 %collective-permute-start.12 = (bf16[384,1024]{1,0:T(8,128)(2,1)S(1)}, bf16[384,1024]{1,0:T(8,128)(2,1)S(1)}, u32[]{:S(2)}, u32[]{:S(2)}) collective-permute-start(bf16[384,1024]{1,0:T(8,128)(2,1)S(1)} %dynamic-slice_bitcast_fusion), channel_id=1, source_target_pairs={{0,2},{2,0},{4,6},{6,4},{8,10},{10,8},{12,14},{14,12},{1,3},{3,1},... | collective-permute-start | bytes 2359304 | tf_op jit(solution)/shard_map/ppermute | solution.py:18
  89.4 107.4 %collective-permute-start.16 = (bf16[384,1024]{1,0:T(8,128)(2,1)S(1)}, bf16[384,1024]{1,0:T(8,128)(2,1)}, u32[]{:S(2)}, u32[]{:S(2)}) collective-permute-start(bf16[384,1024]{1,0:T(8,128)(2,1)S(1)} %dynamic-slice_bitcast_fusion), channel_id=1, source_target_pairs={{0,8},{2,10},{4,12},{6,14},{8,0},{10,2},{12,4},{14,6},{1,9},{3,11}... | collective-permute-start | bytes 2359304 | tf_op jit(solution)/shard_map/ppermute | solution.py:18
  121.5 76.9 %collective-permute-start.1 = (bf16[1024,384]{1,0:T(8,128)(2,1)}, bf16[1024,384]{1,0:T(8,128)(2,1)}, u32[]{:S(2)}, u32[]{:S(2)}) collective-permute-start(bf16[1024,384]{1,0:T(8,128)(2,1)} %collective-permute-done.refs_1_), channel_id=1, source_target_pairs={{0,16},{16,0},{1,17},{17,1},{2,18},{18,2},{3,19},{19,3},{4,20},{20... | collective-permute-start | bytes 2359304 | tf_op jit(solution)/shard_map/ppermute | solution.py:18
  143.5 56.3 %collective-permute-start.2 = (bf16[1024,384]{1,0:T(8,128)(2,1)}, bf16[1024,384]{1,0:T(8,128)(2,1)S(1)}, u32[]{:S(2)}, u32[]{:S(2)}) collective-permute-start(bf16[1024,384]{1,0:T(8,128)(2,1)} %collective-permute-done.refs_1_), channel_id=1, source_target_pairs={{0,1},{1,0},{2,3},{3,2},{4,5},{5,4},{6,7},{7,6},{8,9},{9,8},{10,11... | collective-permute-start | bytes 2359304 | tf_op jit(solution)/shard_map/ppermute | solution.py:18
  180.4 19.5 %collective-permute-start.5 = (bf16[1024,384]{1,0:T(8,128)(2,1)}, bf16[1024,384]{1,0:T(8,128)(2,1)S(1)}, u32[]{:S(2)}, u32[]{:S(2)}) collective-permute-start(bf16[1024,384]{1,0:T(8,128)(2,1)} %collective-permute-done.4.refs_5_), channel_id=1, source_target_pairs={{0,16},{16,0},{1,17},{17,1},{2,18},{18,2},{3,19},{19,3},{4,20},{20... | collective-permute-start | bytes 2359304 | tf_op jit(solution)/shard_map/ppermute | solution.py:18
  181.9 18.8 %collective-permute-start.6 = (bf16[1024,384]{1,0:T(8,128)(2,1)}, bf16[1024,384]{1,0:T(8,128)(2,1)S(1)}, u32[]{:S(2)}, u32[]{:S(2)}) collective-permute-start(bf16[1024,384]{1,0:T(8,128)(2,1)} %collective-permute-done.4.refs_5_), channel_id=1, source_target_pairs={{0,1},{1,0},{2,3},{3,2},{4,5},{5,4},{6,7},{7,6},{8,9},{9,8},{10,11... | collective-permute-start | bytes 2359304 | tf_op jit(solution)/shard_map/ppermute | solution.py:18
  196.8 19.3 %collective-permute-start.8 = (bf16[1024,384]{1,0:T(8,128)(2,1)}, bf16[1024,384]{1,0:T(8,128)(2,1)S(1)}, u32[]{:S(2)}, u32[]{:S(2)}) collective-permute-start(bf16[1024,384]{1,0:T(8,128)(2,1)} %collective-permute-done.4.refs_5_), channel_id=1, source_target_pairs={{0,2},{2,0},{4,6},{6,4},{8,10},{10,8},{12,14},{14,12},{1,3},{3,1},... | collective-permute-start | bytes 2359304 | tf_op jit(solution)/shard_map/ppermute | solution.py:18
  198.4 20.5 %collective-permute-start.13 = (bf16[384,1024]{1,0:T(8,128)(2,1)S(1)}, bf16[384,1024]{1,0:T(8,128)(2,1)S(1)}, u32[]{:S(2)}, u32[]{:S(2)}) collective-permute-start(bf16[384,1024]{1,0:T(8,128)(2,1)S(1)} %collective-permute-done.12.refs_14_), channel_id=1, source_target_pairs={{0,16},{16,0},{1,17},{17,1},{2,18},{18,2},{3,19},{19,3},{4,20},{20... | collective-permute-start | bytes 2359304 | tf_op jit(solution)/shard_map/ppermute | solution.py:18
  199.9 19.0 %collective-permute-start.14 = (bf16[384,1024]{1,0:T(8,128)(2,1)S(1)}, bf16[384,1024]{1,0:T(8,128)(2,1)S(1)}, u32[]{:S(2)}, u32[]{:S(2)}) collective-permute-start(bf16[384,1024]{1,0:T(8,128)(2,1)S(1)} %collective-permute-done.12.refs_14_), channel_id=1, source_target_pairs={{0,1},{1,0},{2,3},{3,2},{4,5},{5,4},{6,7},{7,6},{8,9},{9,8},{10,11... | collective-permute-start | bytes 2359304 | tf_op jit(solution)/shard_map/ppermute | solution.py:18
  199.9 34.2 %collective-permute-start.17 = (bf16[384,1024]{1,0:T(8,128)(2,1)}, bf16[384,1024]{1,0:T(8,128)(2,1)}, u32[]{:S(2)}, u32[]{:S(2)}) collective-permute-start(bf16[384,1024]{1,0:T(8,128)(2,1)} %collective-permute-done.16.refs_18_), channel_id=1, source_target_pairs={{0,16},{16,0},{1,17},{17,1},{2,18},{18,2},{3,19},{19,3},{4,20},{20... | collective-permute-start | bytes 2359304 | tf_op jit(solution)/shard_map/ppermute | solution.py:18
  200.7 33.4 %collective-permute-start.18 = (bf16[384,1024]{1,0:T(8,128)(2,1)}, bf16[384,1024]{1,0:T(8,128)(2,1)}, u32[]{:S(2)}, u32[]{:S(2)}) collective-permute-start(bf16[384,1024]{1,0:T(8,128)(2,1)} %collective-permute-done.16.refs_18_), channel_id=1, source_target_pairs={{0,1},{1,0},{2,3},{3,2},{4,5},{5,4},{6,7},{7,6},{8,9},{9,8},{10,11... | collective-permute-start | bytes 2359304 | tf_op jit(solution)/shard_map/ppermute | solution.py:18
  216.1 19.6 %collective-permute-start.20 = (bf16[384,1024]{1,0:T(8,128)(2,1)}, bf16[384,1024]{1,0:T(8,128)(2,1)}, u32[]{:S(2)}, u32[]{:S(2)}) collective-permute-start(bf16[384,1024]{1,0:T(8,128)(2,1)} %collective-permute-done.16.refs_18_), channel_id=1, source_target_pairs={{0,2},{2,0},{4,6},{6,4},{8,10},{10,8},{12,14},{14,12},{1,3},{3,1},... | collective-permute-start | bytes 2359304 | tf_op jit(solution)/shard_map/ppermute | solution.py:18
  218.8 16.9 %collective-permute-start.3 = (bf16[1024,384]{1,0:T(8,128)(2,1)}, bf16[1024,384]{1,0:T(8,128)(2,1)}, u32[]{:S(2)}, u32[]{:S(2)}) collective-permute-start(bf16[1024,384]{1,0:T(8,128)(2,1)} %collective-permute-done.1.refs_2_), channel_id=1, source_target_pairs={{0,1},{1,0},{2,3},{3,2},{4,5},{5,4},{6,7},{7,6},{8,9},{9,8},{10,11... | collective-permute-start | bytes 2359304 | tf_op jit(solution)/shard_map/ppermute | solution.py:18
  234.1 46.3 %collective-permute-start.24 = (bf16[1024,1024]{1,0:T(8,128)(2,1)}, bf16[1024,1024]{1,0:T(8,128)(2,1)}, u32[]{:S(2)}, u32[]{:S(2)}) collective-permute-start(bf16[1024,1024]{1,0:T(8,128)(2,1)} %get-tuple-element.8.normed), channel_id=1, source_target_pairs={{0,4},{2,6},{4,0},{6,2},{8,12},{10,14},{12,8},{14,10},{1,5},{3,7},... | collective-permute-start | bytes 6291464 | tf_op jit(solution)/shard_map/ppermute | solution.py:18
  234.1 20.6 %collective-permute-start.9 = (bf16[1024,384]{1,0:T(8,128)(2,1)S(1)}, bf16[1024,384]{1,0:T(8,128)(2,1)}, u32[]{:S(2)}, u32[]{:S(2)}) collective-permute-start(bf16[1024,384]{1,0:T(8,128)(2,1)S(1)} %copy-done.26), channel_id=1, source_target_pairs={{0,16},{16,0},{1,17},{17,1},{2,18},{18,2},{3,19},{19,3},{4,20},{20... | collective-permute-start | bytes 2359304 | tf_op jit(solution)/shard_map/ppermute | solution.py:18
  235.7 19.1 %collective-permute-start.10 = (bf16[1024,384]{1,0:T(8,128)(2,1)S(1)}, bf16[1024,384]{1,0:T(8,128)(2,1)S(1)}, u32[]{:S(2)}, u32[]{:S(2)}) collective-permute-start(bf16[1024,384]{1,0:T(8,128)(2,1)S(1)} %copy-done.26), channel_id=1, source_target_pairs={{0,1},{1,0},{2,3},{3,2},{4,5},{5,4},{6,7},{7,6},{8,9},{9,8},{10,11... | collective-permute-start | bytes 2359304 | tf_op jit(solution)/shard_map/ppermute | solution.py:18
  235.7 19.6 %collective-permute-start.15 = (bf16[384,1024]{1,0:T(8,128)(2,1)S(1)}, bf16[384,1024]{1,0:T(8,128)(2,1)S(1)}, u32[]{:S(2)}, u32[]{:S(2)}) collective-permute-start(bf16[384,1024]{1,0:T(8,128)(2,1)S(1)} %copy-done.28), channel_id=1, source_target_pairs={{0,1},{1,0},{2,3},{3,2},{4,5},{5,4},{6,7},{7,6},{8,9},{9,8},{10,11... | collective-permute-start | bytes 2359304 | tf_op jit(solution)/shard_map/ppermute | solution.py:18
  236.2 32.8 %collective-permute-start.21 = (bf16[384,1024]{1,0:T(8,128)(2,1)}, bf16[384,1024]{1,0:T(8,128)(2,1)}, u32[]{:S(2)}, u32[]{:S(2)}) collective-permute-start(bf16[384,1024]{1,0:T(8,128)(2,1)} %collective-permute-done.20.refs_22_), channel_id=1, source_target_pairs={{0,16},{16,0},{1,17},{17,1},{2,18},{18,2},{3,19},{19,3},{4,20},{20... | collective-permute-start | bytes 2359304 | tf_op jit(solution)/shard_map/ppermute | solution.py:18
  323.9 45.1 %collective-permute-start.26 = (bf16[1024,1024]{1,0:T(8,128)(2,1)S(1)}, bf16[1024,1024]{1,0:T(8,128)(2,1)S(1)}, u32[]{:S(2)}, u32[]{:S(2)}) collective-permute-start(bf16[1024,1024]{1,0:T(8,128)(2,1)S(1)} %convert_element_type.13), channel_id=1, source_target_pairs={{0,4},{2,6},{4,0},{6,2},{8,12},{10,14},{12,8},{14,10},{1,5},{3,7},... | collective-permute-start | bytes 6291464 | tf_op jit(solution)/shard_map/ppermute | solution.py:18
  (38 other events, 573.6 us)

commit v2 on v1

--- a/solution.py
+++ b/solution.py
@@ -51,7 +51,7 @@
     return forward.astype(ml_dtypes.bfloat16), inverse.astype(ml_dtypes.bfloat16)
 
 
-def row_tables(grid_len):
+def row_tables(grid_len, rows_local, n_halves):
     c, s = trig(grid_len)
     z = np.zeros_like(c)
 
@@ -64,7 +64,9 @@
     plain_inv = assemble([[[c, s], [-s, c]], [[c, -s], [-s, -c]]]).T
     first_inv = assemble([[[c, z], [-s, z]], [[z, c], [z, -s]]]).T
     kinds = lambda first, plain: np.stack([first, plain]).astype(ml_dtypes.bfloat16)
-    return kinds(first_fwd, plain_fwd), kinds(first_inv, plain_inv)
+    inverse = kinds(first_inv, plain_inv)
+    inverse = inverse.reshape(2, -1, n_halves, 2 * rows_local // n_halves, 4 * grid_len).transpose(0, 2, 1, 3, 4)
+    return kinds(first_fwd, plain_fwd), inverse.reshape(2, 2 * grid_len, 4 * grid_len)
 
 
 def spectra_kernel(tokens, gain, table, out, normed):
@@ -101,7 +103,8 @@
     )(tokens, gain, table)
 
 
-def modes_kernel(spectra, forward, first, second, bias, inverse, out, mixed):
+def modes_kernel(spectra, forward, first, second, bias, inverse, *refs):
+    outs, mixed = refs[:-1], refs[-1]
     n_blocks, pair, _ = first.shape
     block = pair // 2
     grid_len = spectra.shape[0] // 2
@@ -127,11 +130,15 @@
                 mixed[base : base + grid_len, lanes] = result[
                     sign * grid_len : (sign + 1) * grid_len, part * block : (part + 1) * block
                 ]
-    out[...] = mxu(inverse[0], mixed[...]).astype(out.dtype)
-
-
-def mix_modes(spectra, forward, first, second, bias, inverse, width):
+    back = mxu(inverse[0], mixed[...]).astype(jnp.bfloat16)
+    rows = outs[0].shape[0]
+    for index, out in enumerate(outs):
+        out[...] = back[index * rows : (index + 1) * rows, :]
+
+
+def mix_modes(spectra, forward, first, second, bias, inverse, width, n_halves):
     rows, lanes = spectra.shape
+    rows_out = rows // n_halves
     per_dev = lanes // width
     modes_rows = forward.shape[1]
     kind = lambda k: (jnp.minimum(k, 1), 0, 0)
@@ -139,7 +146,7 @@
     return pl.pallas_call(
         modes_kernel,
         grid=(per_dev,),
-        out_shape=jax.ShapeDtypeStruct((rows, lanes), jnp.bfloat16),
+        out_shape=[jax.ShapeDtypeStruct((rows_out, lanes), jnp.bfloat16)] * n_halves,
         in_specs=[
             pl.BlockSpec((rows, width), lambda k: (0, k)),
             pl.BlockSpec((1,) + forward.shape[1:], kind),
@@ -148,7 +155,7 @@
             pl.BlockSpec(bias.shape, lambda k: (0, 0)),
             pl.BlockSpec((1,) + inverse.shape[1:], kind),
         ],
-        out_specs=pl.BlockSpec((rows, width), lambda k: (0, k)),
+        out_specs=[pl.BlockSpec((rows_out, width), lambda k: (0, k))] * n_halves,
         scratch_shapes=[pltpu.VMEM((modes_rows, width), jnp.bfloat16)],
         compiler_params=pltpu.CompilerParams(vmem_limit_bytes=32 * MIB),
         cost_estimate=pl.CostEstimate(
@@ -172,12 +179,13 @@
     normed[...] = normalize(rounded.astype(jnp.float32), gain[...]).astype(jnp.bfloat16)
 
 
-def add_mixing(spectra, table, tokens, gain):
+def add_mixing(spectra, table, tokens, gain, half):
     per_dev, rows_out, rows_in = table.shape
     width = tokens.shape[1]
     tile = math.gcd(rows_out, 256)
     out = jax.ShapeDtypeStruct((rows_out, width), jnp.bfloat16)
     row_tile = pl.BlockSpec((tile, width), lambda i: (i, 0))
+    base = half * (rows_out // tile)
     return pl.pallas_call(
         residual_kernel,
         grid=(rows_out // tile,),
@@ -185,7 +193,7 @@
         in_specs=[
             pl.BlockSpec(spectra.shape, lambda i: (0, 0)),
             pl.BlockSpec((per_dev, tile, rows_in), lambda i: (0, i, 0)),
-            row_tile,
+            pl.BlockSpec((tile, width), lambda i: (i + base, 0)),
             pl.BlockSpec(gain.shape, lambda i: (0, 0)),
         ],
         out_specs=(row_tile, row_tile),
@@ -199,119 +207,150 @@
     )(spectra, table, tokens, gain)
 
 
-def experts_kernel(n_blocks, n_parts, tile, chunk, normed, weights, *refs):
-    per_block = [1] + [n_parts] * (n_blocks - 1)
-    n_pieces = sum(per_block)
-    ups, downs = refs[:n_pieces], refs[n_pieces : 2 * n_pieces]
-    out, up_all, down_all, up_sem, down_sem = refs[2 * n_pieces :]
-    hidden = up_all.shape[2]
-    copies = []
+def gelu_twice(values):
+    scale = math.sqrt(2.0 / math.pi)
+    return values * jnp.tanh(values * (values * values * (0.044715 * scale) + scale)) + values
+
+
+def experts_kernel(pieces, n_sets, n_totals, chunk, weights, *refs):
+    n_pieces = sum(pieces)
+    take = iter(refs)
+    sets = [next(take) for _ in range(n_sets)]
+    totals = [next(take) for _ in range(n_totals)]
+    ups = [next(take) for _ in range(n_pieces)]
+    downs = [next(take) for _ in range(n_pieces)]
+    outs = [next(take) for _ in range(n_sets)]
+    values, total, up_all, down_all, set_sem, total_sem, up_sem, down_sem = take
+    n_blocks, _, hidden = up_all.shape
+    tile = values.shape[0] // n_sets
+    loads = []
+    for index, ref in enumerate(sets):
+        loads.append(pltpu.make_async_copy(ref, values.at[pl.ds(index * tile, tile)], set_sem.at[index]))
+    total_loads = []
+    for index, ref in enumerate(totals):
+        total_loads.append(pltpu.make_async_copy(ref, total.at[pl.ds(index * tile, tile)], total_sem.at[index]))
+    blocks = []
     piece = 0
-    for block, parts in enumerate(per_block):
+    for block, parts in enumerate(pieces):
         size = hidden // parts
+        copies = []
         for part in range(parts):
             units = pl.ds(part * size, size)
-            copies.append(
-                (
-                    block,
-                    pltpu.make_async_copy(ups[piece], up_all.at[block, :, units], up_sem.at[piece]),
-                    pltpu.make_async_copy(downs[piece], down_all.at[block, units, :], down_sem.at[piece]),
-                )
-            )
+            copies.append(pltpu.make_async_copy(ups[piece], up_all.at[block, :, units], up_sem.at[piece]))
+            copies.append(pltpu.make_async_copy(downs[piece], down_all.at[block, units, :], down_sem.at[piece]))
             piece += 1
-    for _, up_copy, down_copy in copies:
-        up_copy.start()
-        down_copy.start()
-    for block in range(n_blocks):
-        for owner, up_copy, down_copy in copies:
-            if owner == block:
-                up_copy.wait()
-                down_copy.wait()
-
-        def token_tile(index, carry, block=block):
-            rows = pl.ds(pl.multiple_of(index * tile, tile), tile)
-            values = normed[rows, :]
-            total = None
-            for start in range(0, hidden, chunk):
-                units = slice(start, start + chunk)
-                act = jax.nn.gelu(mxu(values, up_all[block, :, units]), approximate=True)
-                term = mxu(act.astype(jnp.bfloat16), down_all[block, units, :])
-                total = term if total is None else total + term
-            column = block // 2
-            total = total * weights[rows, column : column + 1]
-            if block > 0:
-                total = total + out[rows, :]
-            out[rows, :] = total
-            return carry
-
-        lax.fori_loop(0, normed.shape[0] // tile, token_tile, 0)
-
-
-def run_experts(normed, weights, blocks, tile=256, chunk=512):
-    rows, width = normed.shape
+        blocks.append(copies)
+    for copy in loads + [copy for copies in blocks for copy in copies] + total_loads:
+        copy.start()
+    for copy in loads:
+        copy.wait()
+
+    def step(index, carry):
+        block = index // n_sets
+        rows = pl.ds(pl.multiple_of((index % n_sets) * tile, tile), tile)
+        for number in range(n_blocks):
+
+            @pl.when(index == number * n_sets)
+            def _(number=number):
+                for copy in blocks[number]:
+                    copy.wait()
+
+        if n_totals:
+
+            @pl.when(index == 0)
+            def _():
+                for copy in total_loads:
+                    copy.wait()
+
+        given = values[rows, :]
+        acts = [
+            gelu_twice(mxu(given, up_all[block, :, start : start + chunk])).astype(jnp.bfloat16)
+            for start in range(0, hidden, chunk)
+        ]
+        term = mxu(jnp.concatenate(acts, axis=1), down_all[block])
+        scale = weights[rows, 0:1]
+        for number in range(1, n_blocks):
+            scale = jnp.where(block == number, weights[rows, number : number + 1], scale)
+        term = term * (0.5 * scale)
+        if n_totals:
+            total[rows, :] = total[rows, :] + term
+        else:
+
+            @pl.when(block == 0)
+            def _():
+                total[rows, :] = term
+
+            @pl.when(block > 0)
+            def _():
+                total[rows, :] = total[rows, :] + term
+
+        return carry
+
+    lax.fori_loop(0, n_blocks * n_sets, step, 0)
+    for index, out in enumerate(outs):
+        out[...] = total[index * tile : (index + 1) * tile, :].astype(out.dtype)
+
+
+def run_experts(sets, weights, blocks, totals=(), dtype=jnp.float32, chunk=256):
+    rows, width = sets[0].shape
     ups = [up for block in blocks for up, _ in block]
     downs = [down for block in blocks for _, down in block]
+    pieces = tuple(len(block) for block in blocks)
     n_blocks = len(blocks)
-    hidden = blocks[0][0][0].shape[1]
+    hidden = sum(up.shape[1] for up, _ in blocks[0])
     chunk = math.gcd(chunk, hidden)
-    n_parts = len(blocks[-1])
+    n_rows = rows * len(sets)
     vmem = pl.BlockSpec(memory_space=pltpu.VMEM)
+    anywhere = pl.BlockSpec(memory_space=pl.ANY)
     return pl.pallas_call(
-        functools.partial(experts_kernel, n_blocks, n_parts, tile, chunk),
-        out_shape=jax.ShapeDtypeStruct((rows, width), jnp.float32),
-        in_specs=[vmem, vmem] + [pl.BlockSpec(memory_space=pl.ANY)] * (2 * len(ups)),
-        out_specs=vmem,
+        functools.partial(experts_kernel, pieces, len(sets), len(totals), chunk),
+        out_shape=[jax.ShapeDtypeStruct((rows, width), dtype)] * len(sets),
+        in_specs=[vmem] + [anywhere] * (len(sets) + len(totals) + 2 * len(ups)),
+        out_specs=[vmem] * len(sets),
         scratch_shapes=[
+            pltpu.VMEM((n_rows, width), jnp.bfloat16),
+            pltpu.VMEM((n_rows, width), jnp.float32),
             pltpu.VMEM((n_blocks, width, hidden), jnp.bfloat16),
             pltpu.VMEM((n_blocks, hidden, width), jnp.bfloat16),
+            pltpu.SemaphoreType.DMA((len(sets),)),
+            pltpu.SemaphoreType.DMA((max(len(totals), 1),)),
             pltpu.SemaphoreType.DMA((len(ups),)),
             pltpu.SemaphoreType.DMA((len(ups),)),
         ],
         compiler_params=pltpu.CompilerParams(vmem_limit_bytes=56 * MIB),
         cost_estimate=pl.CostEstimate(
-            flops=4 * rows * width * hidden * n_blocks,
-            bytes_accessed=4 * width * hidden * n_blocks + 8 * rows * width,
-            transcendentals=rows * hidden * n_blocks,
+            flops=4 * n_rows * width * hidden * n_blocks,
+            bytes_accessed=4 * width * hidden * n_blocks + 8 * n_rows * width,
+            transcendentals=n_rows * hidden * n_blocks,
         ),
         name="experts",
-    )(normed, weights, *ups, *downs)
-
-
-def expert_weights(routing, combine, experts):
-    return jnp.stack(
-        [jnp.sum(jnp.where(routing == expert, combine, 0.0), axis=-1) for expert in experts], axis=-1
-    )
-
-
-def gather_blocks(up, down):
-    n_parts = lax.axis_size("group") * lax.axis_size("expert")
-    part = lax.axis_index("group") * lax.axis_size("expert") + lax.axis_index("expert")
-    size = up.shape[1] // n_parts
-    mine = (
-        lax.dynamic_slice_in_dim(up, part * size, size, axis=1),
-        lax.dynamic_slice_in_dim(down, part * size, size, axis=0),
-    )
-    far = exchange(mine, "row", 4)
-    near = exchange(mine, "row", 1)
-    far_near = exchange(far, "row", 1)
-    blocks = [[(up, down)]]
-    for piece in (near, far, far_near):
+    )(weights, *sets, *totals, *ups, *downs)
+
+
+def expert_weights(routing, combine, n_experts):
+    route, weight = (value.reshape(-1, value.shape[-1]) for value in (routing, combine))
+    return jnp.stack([jnp.sum(jnp.where(route == e, weight, 0.0), axis=-1) for e in range(n_experts)])
+
+
+def after(value, *others):
+    return lax.optimization_barrier((value,) + others)[0]
+
+
+class Weights:
+    def __init__(self, up, down):
+        n_parts = lax.axis_size("group") * lax.axis_size("expert")
+        part = lax.axis_index("group") * lax.axis_size("expert") + lax.axis_index("expert")
+        size = up.shape[1] // n_parts
+        self.own = [(up, down)]
+        self.part = (
+            lax.dynamic_slice_in_dim(up, part * size, size, axis=1),
+            lax.dynamic_slice_in_dim(down, part * size, size, axis=0),
+        )
+
+    @staticmethod
+    def spread(piece):
         other = exchange(piece, "group", 1)
-        blocks.append([piece, other, exchange(piece, "expert", 1), exchange(other, "expert", 1)])
-    return blocks
-
-
-def all_experts(residual, normed, routing, combine, up_weight, down_weight):
-    mine = lax.axis_index("row") // 2
-    flat = lambda value: value.reshape(-1, value.shape[-1])
-    weights = lambda first: expert_weights(flat(routing), flat(combine), (first, first ^ 2))
-    other_weights = exchange(weights(mine ^ 1).T, "row", 2).T
-    blocks = gather_blocks(up_weight[0], down_weight[0])
-    other = exchange(normed, "row", 2)
-    own_out = run_experts(normed, weights(mine), blocks)
-    other_out = run_experts(other, other_weights, blocks).astype(jnp.bfloat16)
-    returned = exchange(other_out, "row", 2)
-    return residual.astype(jnp.float32) + own_out + returned.astype(jnp.float32)
+        return [piece, other, exchange(piece, "expert", 1), exchange(other, "expert", 1)]
 
 
 def routed_experts(residual, normed, routing, combine, up_weight, down_weight):
@@ -362,8 +401,10 @@
     axes = ("row", "expert")
     n_dev = lax.axis_size(axes)
     n_blocks = spec_first.shape[1]
-    forward_cols, inverse_cols = column_tables(grid_len, n_dev, rows_local)
-    forward_rows, inverse_rows = row_tables(grid_len)
+    n_halves = math.gcd(2, rows_local)
+    forward_cols, _ = column_tables(grid_len, n_dev, rows_local)
+    _, inverse_cols = column_tables(grid_len, n_dev, rows_local // n_halves)
+    forward_rows, inverse_rows = row_tables(grid_len, rows_local, n_halves)
     first_device = lax.axis_index(axes) == 0
     pick = lambda table: jnp.stack([jnp.where(first_device, table[0], table[1]), table[1]])
     flat_tokens = tokens.reshape(-1, width)
@@ -373,6 +414,16 @@
         spectra.reshape(n_dev, -1, spectra.shape[1]), axes, split_axis=0, concat_axis=0, tiled=True
     )
     bias = spec_bias.reshape(2, n_blocks, -1).transpose(1, 0, 2).reshape(n_blocks, -1)
+    pairs = lax.axis_size("group") == 2 and lax.axis_size("expert") == 2
+    every_expert = lax.axis_size("row") == 2 * routing.shape[-1] and routing.shape[-1] == 4
+    dense = pairs and every_expert and n_halves == 2
+    if dense:
+        weights = Weights(up_weight[0], down_weight[0])
+        table = expert_weights(routing, combine, routing.shape[-1])
+        arriving = (exchange(table[:, : table.shape[1] // 2], "row", 1), exchange(table[:, table.shape[1] // 2 :], "row", 2))
+        near = exchange(weights.part, "row", 3)
+        far_up = exchange(weights.part[0], "row", 4)
+        by_column, near, far_up, arriving = lax.optimization_barrier((by_column, near, far_up, arriving))
     mixed = mix_modes(
         by_column.reshape(spectra.shape),
         pick(forward_rows),
@@ -381,18 +432,61 @@
         bias,
         pick(inverse_rows),
         width,
+        n_halves,
     )
-    by_row = lax.all_to_all(
-        mixed.reshape(n_dev, -1, mixed.shape[1]), axes, split_axis=0, concat_axis=0, tiled=True
+    by_row = [
+        lax.all_to_all(half.reshape(n_dev, -1, half.shape[1]), axes, split_axis=0, concat_axis=0, tiled=True)
+        for half in mixed
+    ]
+    if dense:
+        near_all = Weights.spread(near)
+        far_down = exchange(after(weights.part[1], by_column), "row", 4)
+        far_near_up = exchange(far_up, "row", 3)
+        by_row[0], near_all, far_down, far_near_up = lax.optimization_barrier(
+            (by_row[0], near_all, far_down, far_near_up)
+        )
+    sides = []
+    for half, spectrum in enumerate(by_row):
+        sides.append(
+            add_mixing(
+                spectrum.reshape(mixed[0].shape),
+                jnp.asarray(inverse_cols),
+                flat_tokens,
+                ln_second.reshape(1, width),
+                half,
+            )
+        )
+    if not dense:
+        residual, normed = (jnp.concatenate(parts) for parts in zip(*sides))
+        final = routed_experts(residual, normed, routing, combine, up_weight, down_weight)
+        return final.astype(jnp.bfloat16).reshape(tokens.shape)
+
+    far_near_down = exchange(far_down, "row", 3)
+    far_all = Weights.spread((far_up, far_down))
+    far_near_all = Weights.spread((far_near_up, far_near_down))
+    expert = lax.axis_index("row") // 2
+    half_size = table.shape[1] // 2
+    pick_two = lambda columns, first: jnp.stack(
+        [lax.dynamic_index_in_dim(columns, expert ^ (first + k), 0, keepdims=False) for k in range(2)], axis=1
     )
-    residual, normed = add_mixing(
-        by_row.reshape(mixed.shape), jnp.asarray(inverse_cols), flat_tokens, ln_second.reshape(1, width)
-    )
-    pairs = lax.axis_size("group") == 2 and lax.axis_size("expert") == 2
-    every_expert = lax.axis_size("row") == 2 * routing.shape[-1] and routing.shape[-1] == 4
-    moe = all_experts if pairs and every_expert else routed_experts
-    final = moe(residual, normed, routing, combine, up_weight, down_weight)
-    return final.astype(jnp.bfloat16).reshape(tokens.shape)
+    (res_a, norm_a), (res_b, norm_b) = sides
+    from_y = exchange(norm_a, "row", 1)
+    from_z = exchange(norm_b, "row", 2)
+    table_a, table_b = table[:, :half_size], table[:, half_size:]
+    table_in = jnp.concatenate(arriving, axis=1)
+    lower, upper = [weights.own, near_all], [far_all, far_near_all]
+    own_a = run_experts([norm_a], pick_two(table_a, 0), lower)[0]
+    own_b = run_experts([norm_b], pick_two(table_b, 0), lower)[0]
+    others = run_experts([from_y, from_z], pick_two(table_in, 0), lower)
+    back_y, back_z = run_experts([from_y, from_z], pick_two(table_in, 2), upper, others, jnp.bfloat16)
+    back_a = exchange(back_y, "row", 1)
+    back_b = exchange(back_z, "row", 2)
+    own_a, own_b = run_experts([norm_a, norm_b], pick_two(table, 2), upper, [own_a, own_b])
+    final = [
+        (residual.astype(jnp.float32) + own + back.astype(jnp.float32)).astype(jnp.bfloat16)
+        for residual, own, back in ((res_a, own_a, back_a), (res_b, own_b, back_b))
+    ]
+    return jnp.concatenate(final).reshape(tokens.shape)
 
 
 def solution(mesh):

time: 375 us -> 350 us (0.933)
  waiting for transfers between devices: 204 us -> 139 us
  starting transfers between devices: 38 us -> 64.6 us
  Pallas kernels: 97.1 us -> 114 us
  other arithmetic: 12.4 us -> 8.58 us
    ppermute x27 -> x30, waiting for transfers between devices: 169 us -> 122 us  [exchange(): return lax.ppermute(value, axis, pairs)]
    all_to_all x1, waiting for transfers between devices: 35.8 us -> 0.01 us  [per_device(): lax.all_to_all(spectra.reshape(n_dev, -1, spectra.shape[1]), axes, split_...]
    all_to_all x1 -> x2, starting transfers between devices: 11.4 us -> 30.3 us  [per_device(): lax.all_to_all(half.reshape(n_dev, -1, half.shape[1]), axes, split_axis=0...]
    pallas_call x3 -> x6, Pallas kernels: 87.8 us -> 105 us  [the longest x5 98.9 us: run_experts(): pl.pallas_call(functools.partial(experts_kernel, pieces, len(sets), len(t...]
    all_to_all x1 -> x2, waiting for transfers between devices: 0.01 us -> 16.2 us  [per_device(): lax.all_to_all(half.reshape(n_dev, -1, half.shape[1]), axes, split_axis=0...]
    ppermute x27 -> x30, starting transfers between devices: 19.1 us -> 26.8 us  [exchange(): return lax.ppermute(value, axis, pairs)]
    unnamed x67 -> x62, local copies, waits for them, and re-layouts: 17.7 us -> 12.8 us
    convert_element_type x2, other arithmetic: 7.23 us -> 2.83 us  [per_device(): (residual.astype(jnp.float32) + own + back.astype(jnp.float32)).astype(jn...]
  transfers between devices with their start and end apart: 29 -> 33, of which waited for: 13 -> 6; matrix products, arithmetic and copies ran while one was open for 2% -> 5% of each run, Pallas kernels for 12% -> 23%
where the time goes in v2:
time: 350 us; the launch traced here: 349 us
  waiting for transfers between devices  139 us (40%)
  Pallas kernels  114 us (33%)
  starting transfers between devices  64.6 us (18%)
  local copies, waits for them, and re-layouts  22 us (6%)
  other arithmetic  8.58 us (2%)
    ppermute x30, waiting for transfers between devices, exchange(): return lax.ppermute(value, axis, pairs)  122 us
    pallas_call x5, Pallas kernels, run_experts(): pl.pallas_call(functools.partial(experts_kernel, pieces, len(sets), len(t...  98.9 us
    all_to_all x2, starting transfers between devices, per_device(): lax.all_to_all(half.reshape(n_dev, -1, half.shape[1]), axes, split_axis=0...  30.3 us
    ppermute x30, starting transfers between devices, exchange(): return lax.ppermute(value, axis, pairs)  26.8 us
    all_to_all x2, waiting for transfers between devices, per_device(): lax.all_to_all(half.reshape(n_dev, -1, half.shape[1]), axes, split_axis=0...  16.2 us
    unnamed x62, local copies, waits for them, and re-layouts  12.8 us
    all_to_all x1, starting transfers between devices, per_device(): lax.all_to_all(spectra.reshape(n_dev, -1, spectra.shape[1]), axes, split_...  7.38 us
  transfers between devices with their start and end apart: 33, of which 6 were waited for; matrix products, arithmetic and copies ran while one was open for 5% of the time, Pallas kernels for 23%

profile of v2, /device:TPU:0, one launch (start us, length us, event | category | flops | bytes accessed | tf_op | source)
XLA Modules:
  0.0 348.8 jit_solution(8568045651846308877)
XLA Ops:
  3.9 4.4 %column_spectra.1 = bf16[256,4096]{1,0:T(8,128)(2,1)S(1)} custom-call(bf16[1024,1024]{1,0:T(8,128)(2,1)S(1)} %bitcast.65, f32[1,1024]{1,0:T(1,128)S(1)} %bitcast.76, bf16[4,256,1024]{2,1,0:T(8,128)(2,1)S(1)} %copy-done.13), custom_call_target="tpu_custom_call" | custom-call | flops 2147483648 | bytes 6291456 | tf_op jit(solution)/shard_map/column_spectra/pallas_call | solution.py:90
  9.6 7.4 %all-to-all-start = ((bf16[16,16,4096]{2,1,0:T(8,128)(2,1)}), bf16[16,16,4096]{2,1,0:T(8,128)(2,1)S(1)}, u32[]{:S(2)}, u32[]{:S(2)}) async-start(bf16[16,16,4096]{2,1,0:T(8,128)(2,1)} %bitcast.70), calls=%async_computation | async-start | bytes 4194304 | tf_op jit(solution)/shard_map/all_to_all | solution.py:413
  17.0 2.2 dynamic-slice_bitcast_fusion.1
  19.2 2.8 collective-permute-start
  22.0 2.4 collective-permute-start.2
  24.4 2.1 dynamic-slice_bitcast_fusion
  34.4 72.0 %collective-permute-done.4 = f32[4,512]{1,0:T(4,128)S(1)} collective-permute-done((f32[4,512]{1,0:T(4,128)S(1)}, f32[4,512]{1,0:T(4,128)S(1)}, u32[]{:S(2)}, u32[]{:S(2)}) %collective-permute-start.4) | collective-permute-done | bytes 8224 | tf_op jit(solution)/shard_map/ppermute | solution.py:18
  109.8 5.8 %mix_modes.1 = (bf16[128,4096]{1,0:T(8,128)(2,1)S(1)}, bf16[128,4096]{1,0:T(8,128)(2,1)S(1)}) custom-call(bf16[256,4096]{1,0:T(8,128)(2,1)S(1)} %bitcast.69, bf16[2,512,256]{2,1,0:T(8,128)(2,1)S(1)} %copy-done.7, bf16[8,256,256]{2,1,0:T(8,128)(2,1)S(1)} %get-tuple-element.87.first, bf16[8,256,256]{2,1,0:T(8,128)(2,1)S(1)} %copy-done.4, ...), custom_call_target="tpu_custom_call" | custom-call | flops 4294967296 | bytes 6291456 | tf_op jit(solution)/shard_map/mix_modes/pallas_call | solution.py:146
  117.6 5.9 %all-to-all-start.1 = ((bf16[16,8,4096]{2,1,0:T(8,128)(2,1)}), bf16[16,8,4096]{2,1,0:T(8,128)(2,1)S(1)}, u32[]{:S(2)}, u32[]{:S(2)}) async-start(bf16[16,8,4096]{2,1,0:T(8,128)(2,1)} %bitcast.72), calls=%async_computation.1 | async-start | bytes 2097152 | tf_op jit(solution)/shard_map/all_to_all | solution.py:438
  123.4 2.8 collective-permute-start.11
  126.3 2.4 collective-permute-start.12
  130.7 16.2 %all-to-all-done.1 = bf16[16,8,4096]{2,1,0:T(8,128)(2,1)S(1)} async-done(((bf16[16,8,4096]{2,1,0:T(8,128)(2,1)}), bf16[16,8,4096]{2,1,0:T(8,128)(2,1)S(1)}, u32[]{:S(2)}, u32[]{:S(2)}) %all-to-all-start.1) | async-done | bytes 1048608 | tf_op jit(solution)/shard_map/all_to_all | solution.py:438
  146.9 24.5 %all-to-all-start.2 = ((bf16[16,8,4096]{2,1,0:T(8,128)(2,1)}), bf16[16,8,4096]{2,1,0:T(8,128)(2,1)}, u32[]{:S(2)}, u32[]{:S(2)}) async-start(bf16[16,8,4096]{2,1,0:T(8,128)(2,1)} %bitcast.71), calls=%async_computation.2 | async-start | bytes 2097152 | tf_op jit(solution)/shard_map/all_to_all | solution.py:438
  171.8 23.8 %collective-permute-done.11.refs_12_ = bf16[384,1024]{1,0:T(8,128)(2,1)} collective-permute-done((bf16[384,1024]{1,0:T(8,128)(2,1)}, bf16[384,1024]{1,0:T(8,128)(2,1)}, u32[]{:S(2)}, u32[]{:S(2)}) %collective-permute-start.11) | collective-permute-done | bytes 786464 | tf_op jit(solution)/shard_map/ppermute | solution.py:18
  198.0 17.9 %collective-permute-done.13.refs_5_ = bf16[1024,384]{1,0:T(8,128)(2,1)} collective-permute-done((bf16[1024,384]{1,0:T(8,128)(2,1)}, bf16[1024,384]{1,0:T(8,128)(2,1)}, u32[]{:S(2)}, u32[]{:S(2)}) %collective-permute-start.13) | collective-permute-done | bytes 786464 | tf_op jit(solution)/shard_map/ppermute | solution.py:18
  224.1 3.3 add_mixing.3
  229.7 7.5 %collective-permute-done.22.refs_16_ = bf16[384,1024]{1,0:T(8,128)(2,1)} collective-permute-done((bf16[384,1024]{1,0:T(8,128)(2,1)}, bf16[384,1024]{1,0:T(8,128)(2,1)}, u32[]{:S(2)}, u32[]{:S(2)}) %collective-permute-start.22) | collective-permute-done | bytes 786464 | tf_op jit(solution)/shard_map/ppermute | solution.py:18
  238.7 14.4 %experts.6.refs_3_ = f32[512,1024]{1,0:T(8,128)} custom-call(f32[512,2]{1,0:T(8,128)} %copy.30.weights, bf16[512,1024]{1,0:T(8,128)(2,1)} %copy-done.10, bf16[1024,1536]{1,0:T(8,128)(2,1)} %bitcast.77, bf16[1024,384]{1,0:T(8,128)(2,1)} %collective-permute-done.refs_2_.refs_3_, bf16[1024,384]{1,0:T(8,128)(2,1)} %collective-permute-done.5.refs_3_.refs_4_, ...), custom_call_target="tpu_custom_call" | custom-call | flops 6442450944 | bytes 16777216 | tf_op jit(solution)/shard_map/experts/pallas_call | solution.py:305
  253.2 14.4 %experts.5.refs_2_ = f32[512,1024]{1,0:T(8,128)} custom-call(f32[512,2]{1,0:T(8,128)} %copy.29.weights, bf16[512,1024]{1,0:T(8,128)(2,1)} %copy-done.11, bf16[1024,1536]{1,0:T(8,128)(2,1)} %bitcast.78, bf16[1024,384]{1,0:T(8,128)(2,1)} %collective-permute-done.refs_2_.refs_3_, bf16[1024,384]{1,0:T(8,128)(2,1)} %collective-permute-done.5.refs_3_.refs_4_, ...), custom_call_target="tpu_custom_call" | custom-call | flops 6442450944 | bytes 16777216 | tf_op jit(solution)/shard_map/experts/pallas_call | solution.py:305
  269.9 23.1 %experts.8 = (f32[512,1024]{1,0:T(8,128)}, f32[512,1024]{1,0:T(8,128)}) custom-call(f32[1024,2]{1,0:T(8,128)} %copy.32.weights, bf16[512,1024]{1,0:T(8,128)(2,1)} %copy-done.24, bf16[512,1024]{1,0:T(8,128)(2,1)} %copy-done.25, bf16[1024,1536]{1,0:T(8,128)(2,1)} %bitcast.79, bf16[1024,384]{1,0:T(8,128)(2,1)} %collective-permute-done.refs_2_.refs_3_, ...), custom_call_target="tpu_custom_call" | custom-call | flops 12884901888 | bytes 20971520 | tf_op jit(solution)/shard_map/experts/pallas_call | solution.py:305
  294.3 23.0 %experts.9 = (bf16[512,1024]{1,0:T(8,128)(2,1)}, bf16[512,1024]{1,0:T(8,128)(2,1)}) custom-call(f32[1024,2]{1,0:T(8,128)} %copy.33.weights, bf16[512,1024]{1,0:T(8,128)(2,1)} %copy-done.24, bf16[512,1024]{1,0:T(8,128)(2,1)} %copy-done.25, f32[512,1024]{1,0:T(8,128)} %get-tuple-element.59.refs_2_, f32[512,1024]{1,0:T(8,128)} %get-tuple-element.60.refs_3_, ...), custom_call_target="tpu_custom_call" | custom-call | flops 12884901888 | bytes 20971520 | tf_op jit(solution)/shard_map/experts/pallas_call | solution.py:305
  317.7 2.9 collective-permute-start.29
  320.5 23.9 %experts.7 = (f32[512,1024]{1,0:T(8,128)}, f32[512,1024]{1,0:T(8,128)}) custom-call(f32[1024,2]{1,0:T(8,128)} %copy.31.weights, bf16[512,1024]{1,0:T(8,128)(2,1)} %copy-done.11, bf16[512,1024]{1,0:T(8,128)(2,1)} %copy-done.10, f32[512,1024]{1,0:T(8,128)} %experts.5.refs_2_, f32[512,1024]{1,0:T(8,128)} %experts.6.refs_3_, ...), custom_call_target="tpu_custom_call" | custom-call | flops 12884901888 | bytes 20971520 | tf_op jit(solution)/shard_map/experts/pallas_call | solution.py:305
  344.5 2.2 add_convert_fusion.1
  (144 shorter events, 41.0 us)
Async XLA Ops:
  9.6 96.9 %all-to-all-start = ((bf16[16,16,4096]{2,1,0:T(8,128)(2,1)}), bf16[16,16,4096]{2,1,0:T(8,128)(2,1)S(1)}, u32[]{:S(2)}, u32[]{:S(2)}) async-start(bf16[16,16,4096]{2,1,0:T(8,128)(2,1)} %bitcast.70), calls=%async_computation | async-start | bytes 4194304 | tf_op jit(solution)/shard_map/all_to_all | solution.py:413
  19.2 87.3 %collective-permute-start = (bf16[1024,384]{1,0:T(8,128)(2,1)}, bf16[1024,384]{1,0:T(8,128)(2,1)}, u32[]{:S(2)}, u32[]{:S(2)}) collective-permute-start(bf16[1024,384]{1,0:T(8,128)(2,1)} %dynamic-slice_bitcast_fusion.1), channel_id=1, source_target_pairs={{0,6},{2,4},{4,2},{6,0},{8,14},{10,12},{12,10},{14,8},{1,7},{3,5},... | collective-permute-start | bytes 2359304 | tf_op jit(solution)/shard_map/ppermute | solution.py:18
  22.0 84.4 %collective-permute-start.2 = (bf16[1024,384]{1,0:T(8,128)(2,1)}, bf16[1024,384]{1,0:T(8,128)(2,1)}, u32[]{:S(2)}, u32[]{:S(2)}) collective-permute-start(bf16[1024,384]{1,0:T(8,128)(2,1)} %dynamic-slice_bitcast_fusion.1), channel_id=1, source_target_pairs={{0,8},{2,10},{4,12},{6,14},{8,0},{10,2},{12,4},{14,6},{1,9},{3,11}... | collective-permute-start | bytes 2359304 | tf_op jit(solution)/shard_map/ppermute | solution.py:18
  26.4 80.0 %collective-permute-start.1 = (bf16[384,1024]{1,0:T(8,128)(2,1)}, bf16[384,1024]{1,0:T(8,128)(2,1)}, u32[]{:S(2)}, u32[]{:S(2)}) collective-permute-start(bf16[384,1024]{1,0:T(8,128)(2,1)} %dynamic-slice_bitcast_fusion), channel_id=1, source_target_pairs={{0,6},{2,4},{4,2},{6,0},{8,14},{10,12},{12,10},{14,8},{1,7},{3,5},... | collective-permute-start | bytes 2359304 | tf_op jit(solution)/shard_map/ppermute | solution.py:18
  28.6 77.8 %collective-permute-start.4 = (f32[4,512]{1,0:T(4,128)S(1)}, f32[4,512]{1,0:T(4,128)S(1)}, u32[]{:S(2)}, u32[]{:S(2)}) collective-permute-start(f32[4,512]{1,0:T(4,128)S(1)} %get-tuple-element.79), channel_id=1, source_target_pairs={{0,4},{2,6},{4,0},{6,2},{8,12},{10,14},{12,8},{14,10},{1,5},{3,7},... | collective-permute-start | bytes 24584 | tf_op jit(solution)/shard_map/ppermute | solution.py:18
  117.6 29.3 %all-to-all-start.1 = ((bf16[16,8,4096]{2,1,0:T(8,128)(2,1)}), bf16[16,8,4096]{2,1,0:T(8,128)(2,1)S(1)}, u32[]{:S(2)}, u32[]{:S(2)}) async-start(bf16[16,8,4096]{2,1,0:T(8,128)(2,1)} %bitcast.72), calls=%async_computation.1 | async-start | bytes 2097152 | tf_op jit(solution)/shard_map/all_to_all | solution.py:438
  123.4 72.2 %collective-permute-start.11 = (bf16[384,1024]{1,0:T(8,128)(2,1)}, bf16[384,1024]{1,0:T(8,128)(2,1)}, u32[]{:S(2)}, u32[]{:S(2)}) collective-permute-start(bf16[384,1024]{1,0:T(8,128)(2,1)} %dynamic-slice_bitcast_fusion), channel_id=1, source_target_pairs={{0,8},{2,10},{4,12},{6,14},{8,0},{10,2},{12,4},{14,6},{1,9},{3,11}... | collective-permute-start | bytes 2359304 | tf_op jit(solution)/shard_map/ppermute | solution.py:18
  126.3 69.3 %collective-permute-start.12 = (bf16[1024,384]{1,0:T(8,128)(2,1)}, bf16[1024,384]{1,0:T(8,128)(2,1)}, u32[]{:S(2)}, u32[]{:S(2)}) collective-permute-start(bf16[1024,384]{1,0:T(8,128)(2,1)} %collective-permute-done.2.refs_4_), channel_id=1, source_target_pairs={{0,6},{2,4},{4,2},{6,0},{8,14},{10,12},{12,10},{14,8},{1,7},{3,5},... | collective-permute-start | bytes 2359304 | tf_op jit(solution)/shard_map/ppermute | solution.py:18
  128.6 68.5 %collective-permute-start.6 = (bf16[384,1024]{1,0:T(8,128)(2,1)}, bf16[384,1024]{1,0:T(8,128)(2,1)}, u32[]{:S(2)}, u32[]{:S(2)}) collective-permute-start(bf16[384,1024]{1,0:T(8,128)(2,1)} %collective-permute-done.1.refs_7_.refs_8_), channel_id=1, source_target_pairs={{0,16},{16,0},{1,17},{17,1},{2,18},{18,2},{3,19},{19,3},{4,20},{20... | collective-permute-start | bytes 2359304 | tf_op jit(solution)/shard_map/ppermute | solution.py:18
  130.1 67.2 %collective-permute-start.5 = (bf16[1024,384]{1,0:T(8,128)(2,1)}, bf16[1024,384]{1,0:T(8,128)(2,1)}, u32[]{:S(2)}, u32[]{:S(2)}) collective-permute-start(bf16[1024,384]{1,0:T(8,128)(2,1)} %collective-permute-done.refs_2_.refs_3_), channel_id=1, source_target_pairs={{0,16},{16,0},{1,17},{17,1},{2,18},{18,2},{3,19},{19,3},{4,20},{20... | collective-permute-start | bytes 2359304 | tf_op jit(solution)/shard_map/ppermute | solution.py:18
  146.9 76.1 %all-to-all-start.2 = ((bf16[16,8,4096]{2,1,0:T(8,128)(2,1)}), bf16[16,8,4096]{2,1,0:T(8,128)(2,1)}, u32[]{:S(2)}, u32[]{:S(2)}) async-start(bf16[16,8,4096]{2,1,0:T(8,128)(2,1)} %bitcast.71), calls=%async_computation.2 | async-start | bytes 2097152 | tf_op jit(solution)/shard_map/all_to_all | solution.py:438
  171.4 26.3 %collective-permute-start.7 = (bf16[1024,384]{1,0:T(8,128)(2,1)}, bf16[1024,384]{1,0:T(8,128)(2,1)}, u32[]{:S(2)}, u32[]{:S(2)}) collective-permute-start(bf16[1024,384]{1,0:T(8,128)(2,1)} %collective-permute-done.refs_2_.refs_3_), channel_id=1, source_target_pairs={{0,1},{1,0},{2,3},{3,2},{4,5},{5,4},{6,7},{7,6},{8,9},{9,8},{10,11... | collective-permute-start | bytes 2359304 | tf_op jit(solution)/shard_map/ppermute | solution.py:18
  197.7 31.8 %collective-permute-start.14 = (bf16[1024,384]{1,0:T(8,128)(2,1)}, bf16[1024,384]{1,0:T(8,128)(2,1)}, u32[]{:S(2)}, u32[]{:S(2)}) collective-permute-start(bf16[1024,384]{1,0:T(8,128)(2,1)} %collective-permute-done.2.refs_4_), channel_id=1, source_target_pairs={{0,1},{1,0},{2,3},{3,2},{4,5},{5,4},{6,7},{7,6},{8,9},{9,8},{10,11... | collective-permute-start | bytes 2359304 | tf_op jit(solution)/shard_map/ppermute | solution.py:18
  222.5 45.1 %collective-permute-start.19 = (bf16[384,1024]{1,0:T(8,128)(2,1)}, bf16[384,1024]{1,0:T(8,128)(2,1)}, u32[]{:S(2)}, u32[]{:S(2)}) collective-permute-start(bf16[384,1024]{1,0:T(8,128)(2,1)} %collective-permute-done.11.refs_12_), channel_id=1, source_target_pairs={{0,16},{16,0},{1,17},{17,1},{2,18},{18,2},{3,19},{19,3},{4,20},{20... | collective-permute-start | bytes 2359304 | tf_op jit(solution)/shard_map/ppermute | solution.py:18
  229.5 38.3 %collective-permute-start.17 = (bf16[1024,384]{1,0:T(8,128)(2,1)}, bf16[1024,384]{1,0:T(8,128)(2,1)S(1)}, u32[]{:S(2)}, u32[]{:S(2)}) collective-permute-start(bf16[1024,384]{1,0:T(8,128)(2,1)} %collective-permute-done.12.refs_8_), channel_id=1, source_target_pairs={{0,1},{1,0},{2,3},{3,2},{4,5},{5,4},{6,7},{7,6},{8,9},{9,8},{10,11... | collective-permute-start | bytes 2359304 | tf_op jit(solution)/shard_map/ppermute | solution.py:18
  229.5 38.7 %collective-permute-start.26 = (bf16[512,1024]{1,0:T(8,128)(2,1)S(1)}, bf16[512,1024]{1,0:T(8,128)(2,1)S(1)}, u32[]{:S(2)}, u32[]{:S(2)}) collective-permute-start(bf16[512,1024]{1,0:T(8,128)(2,1)S(1)} %get-tuple-element.43.refs_0_), channel_id=1, source_target_pairs={{0,2},{2,0},{4,6},{6,4},{8,10},{10,8},{12,14},{14,12},{1,3},{3,1},... | collective-permute-start | bytes 3145736 | tf_op jit(solution)/shard_map/ppermute | solution.py:18
  237.2 31.1 %collective-permute-start.27 = (bf16[512,1024]{1,0:T(8,128)(2,1)S(1)}, bf16[512,1024]{1,0:T(8,128)(2,1)S(1)}, u32[]{:S(2)}, u32[]{:S(2)}) collective-permute-start(bf16[512,1024]{1,0:T(8,128)(2,1)S(1)} %get-tuple-element.45.refs_0_.refs_1_), channel_id=1, source_target_pairs={{0,4},{2,6},{4,0},{6,2},{8,12},{10,14},{12,8},{14,10},{1,5},{3,7},... | collective-permute-start | bytes 3145736 | tf_op jit(solution)/shard_map/ppermute | solution.py:18
  237.2 32.7 %collective-permute-start.23 = (bf16[384,1024]{1,0:T(8,128)(2,1)}, bf16[384,1024]{1,0:T(8,128)(2,1)S(1)}, u32[]{:S(2)}, u32[]{:S(2)}) collective-permute-start(bf16[384,1024]{1,0:T(8,128)(2,1)} %collective-permute-done.22.refs_16_), channel_id=1, source_target_pairs={{0,16},{16,0},{1,17},{17,1},{2,18},{18,2},{3,19},{19,3},{4,20},{20... | collective-permute-start | bytes 2359304 | tf_op jit(solution)/shard_map/ppermute | solution.py:18
  267.6 25.4 %collective-permute-start.20 = (bf16[384,1024]{1,0:T(8,128)(2,1)}, bf16[384,1024]{1,0:T(8,128)(2,1)}, u32[]{:S(2)}, u32[]{:S(2)}) collective-permute-start(bf16[384,1024]{1,0:T(8,128)(2,1)} %collective-permute-done.11.refs_12_), channel_id=1, source_target_pairs={{0,1},{1,0},{2,3},{3,2},{4,5},{5,4},{6,7},{7,6},{8,9},{9,8},{10,11... | collective-permute-start | bytes 2359304 | tf_op jit(solution)/shard_map/ppermute | solution.py:18
  267.7 25.4 %collective-permute-start.24 = (bf16[384,1024]{1,0:T(8,128)(2,1)}, bf16[384,1024]{1,0:T(8,128)(2,1)}, u32[]{:S(2)}, u32[]{:S(2)}) collective-permute-start(bf16[384,1024]{1,0:T(8,128)(2,1)} %collective-permute-done.22.refs_16_), channel_id=1, source_target_pairs={{0,1},{1,0},{2,3},{3,2},{4,5},{5,4},{6,7},{7,6},{8,9},{9,8},{10,11... | collective-permute-start | bytes 2359304 | tf_op jit(solution)/shard_map/ppermute | solution.py:18
  268.2 24.8 %collective-permute-start.18 = (bf16[1024,384]{1,0:T(8,128)(2,1)}, bf16[1024,384]{1,0:T(8,128)(2,1)S(1)}, u32[]{:S(2)}, u32[]{:S(2)}) collective-permute-start(bf16[1024,384]{1,0:T(8,128)(2,1)} %collective-permute-done.16.refs_9_), channel_id=1, source_target_pairs={{0,1},{1,0},{2,3},{3,2},{4,5},{5,4},{6,7},{7,6},{8,9},{9,8},{10,11... | collective-permute-start | bytes 2359304 | tf_op jit(solution)/shard_map/ppermute | solution.py:18
  268.3 24.7 %collective-permute-start.21 = (bf16[384,1024]{1,0:T(8,128)(2,1)}, bf16[384,1024]{1,0:T(8,128)(2,1)S(1)}, u32[]{:S(2)}, u32[]{:S(2)}) collective-permute-start(bf16[384,1024]{1,0:T(8,128)(2,1)} %collective-permute-done.19.refs_13_), channel_id=1, source_target_pairs={{0,1},{1,0},{2,3},{3,2},{4,5},{5,4},{6,7},{7,6},{8,9},{9,8},{10,11... | collective-permute-start | bytes 2359304 | tf_op jit(solution)/shard_map/ppermute | solution.py:18
  317.3 27.1 %collective-permute-start.28 = (bf16[512,1024]{1,0:T(8,128)(2,1)}, bf16[512,1024]{1,0:T(8,128)(2,1)S(1)}, u32[]{:S(2)}, u32[]{:S(2)}) collective-permute-start(bf16[512,1024]{1,0:T(8,128)(2,1)} %get-tuple-element.61), channel_id=1, source_target_pairs={{0,2},{2,0},{4,6},{6,4},{8,10},{10,8},{12,14},{14,12},{1,3},{3,1},... | collective-permute-start | bytes 3145736 | tf_op jit(solution)/shard_map/ppermute | solution.py:18
  317.7 29.1 %collective-permute-start.29 = (bf16[512,1024]{1,0:T(8,128)(2,1)}, bf16[512,1024]{1,0:T(8,128)(2,1)S(1)}, u32[]{:S(2)}, u32[]{:S(2)}) collective-permute-start(bf16[512,1024]{1,0:T(8,128)(2,1)} %get-tuple-element.64), channel_id=1, source_target_pairs={{0,4},{2,6},{4,0},{6,2},{8,12},{10,14},{12,8},{14,10},{1,5},{3,7},... | collective-permute-start | bytes 3145736 | tf_op jit(solution)/shard_map/ppermute | solution.py:18
  (39 other events, 478.7 us)

commit v3 on v1

--- a/solution.py
+++ b/solution.py
@@ -91,7 +91,7 @@
         in_specs=[pl.BlockSpec(memory_space=pltpu.VMEM)] * 3,
         out_specs=pl.BlockSpec(memory_space=pltpu.VMEM),
         scratch_shapes=[pltpu.VMEM((rows_in, width), jnp.bfloat16)],
-        compiler_params=pltpu.CompilerParams(vmem_limit_bytes=32 * MIB),
+        compiler_params=pltpu.CompilerParams(vmem_limit_bytes=60 * MIB),
         cost_estimate=pl.CostEstimate(
             flops=2 * per_dev * rows_out * rows_in * width,
             bytes_accessed=2 * (rows_in * width + rows_out * per_dev * width + table.size),
@@ -150,7 +150,7 @@
         ],
         out_specs=pl.BlockSpec((rows, width), lambda k: (0, k)),
         scratch_shapes=[pltpu.VMEM((modes_rows, width), jnp.bfloat16)],
-        compiler_params=pltpu.CompilerParams(vmem_limit_bytes=32 * MIB),
+        compiler_params=pltpu.CompilerParams(vmem_limit_bytes=60 * MIB),
         cost_estimate=pl.CostEstimate(
             flops=2 * lanes * (2 * rows * modes_rows + modes_rows * 512),
             bytes_accessed=4 * (rows * lanes + first.size),
@@ -160,36 +160,48 @@
     )(spectra, forward, first, second, bias, inverse)
 
 
-def residual_kernel(spectra, table, tokens, gain, residual, normed):
+def residual_kernel(spectra, table, tokens, gain, residual, *halves):
     width = tokens.shape[1]
-    total = tokens[...].astype(jnp.float32)
     mixing = None
     for column in range(table.shape[0]):
         term = mxu(table[column], spectra[:, column * width : (column + 1) * width])
         mixing = term if mixing is None else mixing + term
-    rounded = (total + mixing).astype(jnp.bfloat16)
+    rounded = (tokens[...].astype(jnp.float32) + mixing).astype(jnp.bfloat16)
     residual[...] = rounded
-    normed[...] = normalize(rounded.astype(jnp.float32), gain[...]).astype(jnp.bfloat16)
+    normed = normalize(rounded.astype(jnp.float32), gain[...]).astype(jnp.bfloat16)
+    per_half = pl.num_programs(0) // len(halves)
+    for index, half in enumerate(halves):
+
+        @pl.when(pl.program_id(0) // per_half == index)
+        def _(half=half):
+            half[...] = normed
+
+
+def half_tiles(tile, width, per_half, n_halves):
+    return [
+        pl.BlockSpec((tile, width), lambda i, first=index * per_half: (jnp.clip(i - first, 0, per_half - 1), 0))
+        for index in range(n_halves)
+    ]
 
 
 def add_mixing(spectra, table, tokens, gain):
     per_dev, rows_out, rows_in = table.shape
     width = tokens.shape[1]
-    tile = math.gcd(rows_out, 256)
-    out = jax.ShapeDtypeStruct((rows_out, width), jnp.bfloat16)
+    tile = math.gcd(rows_out // 2, 256)
+    steps = rows_out // tile
     row_tile = pl.BlockSpec((tile, width), lambda i: (i, 0))
     return pl.pallas_call(
         residual_kernel,
-        grid=(rows_out // tile,),
-        out_shape=(out, out),
+        grid=(steps,),
+        out_shape=[jax.ShapeDtypeStruct((rows, width), jnp.bfloat16) for rows in (rows_out, rows_out // 2, rows_out // 2)],
         in_specs=[
             pl.BlockSpec(spectra.shape, lambda i: (0, 0)),
             pl.BlockSpec((per_dev, tile, rows_in), lambda i: (0, i, 0)),
             row_tile,
             pl.BlockSpec(gain.shape, lambda i: (0, 0)),
         ],
-        out_specs=(row_tile, row_tile),
-        compiler_params=pltpu.CompilerParams(vmem_limit_bytes=32 * MIB),
+        out_specs=[row_tile] + half_tiles(tile, width, steps // 2, 2),
+        compiler_params=pltpu.CompilerParams(vmem_limit_bytes=60 * MIB),
         cost_estimate=pl.CostEstimate(
             flops=2 * per_dev * rows_out * rows_in * width,
             bytes_accessed=2 * (3 * rows_out * width + spectra.size + table.size),
@@ -199,119 +211,179 @@
     )(spectra, table, tokens, gain)
 
 
-def experts_kernel(n_blocks, n_parts, tile, chunk, normed, weights, *refs):
-    per_block = [1] + [n_parts] * (n_blocks - 1)
-    n_pieces = sum(per_block)
-    ups, downs = refs[:n_pieces], refs[n_pieces : 2 * n_pieces]
-    out, up_all, down_all, up_sem, down_sem = refs[2 * n_pieces :]
-    hidden = up_all.shape[2]
-    copies = []
+def sum_kernel(residual, own, back_a, back_b, out):
+    total = residual[...].astype(jnp.float32) + own[...]
+    half = pl.num_programs(0) // 2
+    for index, back in enumerate((back_a, back_b)):
+
+        @pl.when(pl.program_id(0) // half == index)
+        def _(back=back):
+            out[...] = (total + back[...].astype(jnp.float32)).astype(out.dtype)
+
+
+def add_outputs(residual, own, back_a, back_b):
+    rows, width = residual.shape
+    tile = math.gcd(rows // 2, 256)
+    row_tile = pl.BlockSpec((tile, width), lambda i: (i, 0))
+    return pl.pallas_call(
+        sum_kernel,
+        grid=(rows // tile,),
+        out_shape=jax.ShapeDtypeStruct(residual.shape, jnp.bfloat16),
+        in_specs=[row_tile, row_tile] + half_tiles(tile, width, rows // tile // 2, 2),
+        out_specs=row_tile,
+        compiler_params=pltpu.CompilerParams(vmem_limit_bytes=32 * MIB),
+        name="add_outputs",
+    )(residual, own, back_a, back_b)
+
+
+def gate(value, *others):
+    anywhere = pl.BlockSpec(memory_space=pl.ANY)
+    return pl.pallas_call(
+        lambda *refs: None,
+        out_shape=jax.ShapeDtypeStruct(value.shape, value.dtype),
+        in_specs=[anywhere] * (1 + len(others)),
+        out_specs=anywhere,
+        input_output_aliases={0: 0},
+        compiler_params=pltpu.CompilerParams(vmem_limit_bytes=60 * MIB),
+        cost_estimate=pl.CostEstimate(flops=10**11, bytes_accessed=10**8, transcendentals=0),
+        name="gate",
+    )(value, *others)
+
+
+def gelu_twice(values):
+    scale = math.sqrt(2.0 / math.pi)
+    return values * jnp.tanh(values * (values * values * (0.044715 * scale) + scale)) + values
+
+
+def experts_kernel(pieces, n_sets, n_outs, n_totals, chunk, weights, *refs):
+    take = iter(refs)
+    sets = [next(take) for _ in range(n_sets)]
+    totals = [next(take) for _ in range(n_totals)]
+    halves = [[next(take) for _ in range(count)] for count in pieces]
+    outs = [next(take) for _ in range(n_outs)]
+    values, up_all, down_all, set_sem, total_sem, piece_sem = (next(take) for _ in range(6))
+    total = outs[0] if n_outs == 1 else next(take)
+    n_blocks, _, hidden = up_all.shape
+    tile = values.shape[0] // n_sets
+    rows_of = lambda index: pl.ds(index * tile, tile)
+    loads = [
+        pltpu.make_async_copy(ref, values.at[rows_of(index)], set_sem.at[index]) for index, ref in enumerate(sets)
+    ]
+    total_loads = [
+        pltpu.make_async_copy(ref, total.at[pl.ds(index * ref.shape[0], ref.shape[0])], total_sem.at[index])
+        for index, ref in enumerate(totals)
+    ]
+    blocks = []
     piece = 0
-    for block, parts in enumerate(per_block):
-        size = hidden // parts
-        for part in range(parts):
-            units = pl.ds(part * size, size)
-            copies.append(
-                (
-                    block,
-                    pltpu.make_async_copy(ups[piece], up_all.at[block, :, units], up_sem.at[piece]),
-                    pltpu.make_async_copy(downs[piece], down_all.at[block, units, :], down_sem.at[piece]),
-                )
-            )
-            piece += 1
-    for _, up_copy, down_copy in copies:
-        up_copy.start()
-        down_copy.start()
     for block in range(n_blocks):
-        for owner, up_copy, down_copy in copies:
-            if owner == block:
-                up_copy.wait()
-                down_copy.wait()
+        copies = []
+        for side in range(2):
+            base = 0
+            for ref in halves[2 * block + side]:
+                size = ref.shape[1 - side]
+                units = pl.ds(base, size)
+                target = down_all.at[block, units, :] if side else up_all.at[block, :, units]
+                copies.append(pltpu.make_async_copy(ref, target, piece_sem.at[piece]))
+                base += size
+                piece += 1
+        blocks.append(copies)
+    for copy in loads + blocks[0] + total_loads + blocks[1]:
+        copy.start()
+    for copy in loads:
+        copy.wait()
+    for block in range(n_blocks):
+        for copy in blocks[block]:
+            copy.wait()
+        if 0 < block < n_blocks - 1:
+            for copy in blocks[block + 1]:
+                copy.start()
+        if block == 0:
+            for copy in total_loads:
+                copy.wait()
 
         def token_tile(index, carry, block=block):
             rows = pl.ds(pl.multiple_of(index * tile, tile), tile)
-            values = normed[rows, :]
-            total = None
-            for start in range(0, hidden, chunk):
-                units = slice(start, start + chunk)
-                act = jax.nn.gelu(mxu(values, up_all[block, :, units]), approximate=True)
-                term = mxu(act.astype(jnp.bfloat16), down_all[block, units, :])
-                total = term if total is None else total + term
-            column = block // 2
-            total = total * weights[rows, column : column + 1]
-            if block > 0:
-                total = total + out[rows, :]
-            out[rows, :] = total
+            given = values[rows, :]
+            acts = [
+                gelu_twice(mxu(given, up_all[block, :, start : start + chunk])).astype(jnp.bfloat16)
+                for start in range(0, hidden, chunk)
+            ]
+            term = mxu(jnp.concatenate(acts, axis=1), down_all[block]) * (0.5 * weights[rows, block : block + 1])
+            if block > 0 or n_totals:
+                term = total[rows, :] + term
+            total[rows, :] = term
             return carry
 
-        lax.fori_loop(0, normed.shape[0] // tile, token_tile, 0)
-
-
-def run_experts(normed, weights, blocks, tile=256, chunk=512):
-    rows, width = normed.shape
-    ups = [up for block in blocks for up, _ in block]
-    downs = [down for block in blocks for _, down in block]
+        lax.fori_loop(0, n_sets, token_tile, 0)
+    if n_outs > 1:
+        for index, out in enumerate(outs):
+            out[...] = total[index * tile : (index + 1) * tile, :].astype(out.dtype)
+
+
+def run_experts(sets, weights, blocks, totals=(), split=False, chunk=256):
+    rows, width = sets[0].shape
+    halves = [half for block in blocks for half in block]
+    weights_in = [piece for half in halves for piece in half]
     n_blocks = len(blocks)
-    hidden = blocks[0][0][0].shape[1]
+    hidden = sum(piece.shape[1] for piece in blocks[0][0])
     chunk = math.gcd(chunk, hidden)
-    n_parts = len(blocks[-1])
+    n_rows = rows * len(sets)
     vmem = pl.BlockSpec(memory_space=pltpu.VMEM)
+    anywhere = pl.BlockSpec(memory_space=pl.ANY)
+    if split:
+        out_shape = [jax.ShapeDtypeStruct((rows, width), jnp.bfloat16)] * len(sets)
+    else:
+        out_shape = [jax.ShapeDtypeStruct((n_rows, width), jnp.float32)]
+    counts = tuple(len(half) for half in halves)
     return pl.pallas_call(
-        functools.partial(experts_kernel, n_blocks, n_parts, tile, chunk),
-        out_shape=jax.ShapeDtypeStruct((rows, width), jnp.float32),
-        in_specs=[vmem, vmem] + [pl.BlockSpec(memory_space=pl.ANY)] * (2 * len(ups)),
-        out_specs=vmem,
+        functools.partial(experts_kernel, counts, len(sets), len(out_shape), len(totals), chunk),
+        out_shape=out_shape,
+        in_specs=[vmem] + [anywhere] * (len(sets) + len(totals) + len(weights_in)),
+        out_specs=[vmem] * len(out_shape),
         scratch_shapes=[
+            pltpu.VMEM((n_rows, width), jnp.bfloat16),
             pltpu.VMEM((n_blocks, width, hidden), jnp.bfloat16),
             pltpu.VMEM((n_blocks, hidden, width), jnp.bfloat16),
-            pltpu.SemaphoreType.DMA((len(ups),)),
-            pltpu.SemaphoreType.DMA((len(ups),)),
-        ],
-        compiler_params=pltpu.CompilerParams(vmem_limit_bytes=56 * MIB),
+            pltpu.SemaphoreType.DMA((len(sets),)),
+            pltpu.SemaphoreType.DMA((len(sets),)),
+            pltpu.SemaphoreType.DMA((len(weights_in),)),
+        ]
+        + ([pltpu.VMEM((n_rows, width), jnp.float32)] if split else []),
+        compiler_params=pltpu.CompilerParams(vmem_limit_bytes=60 * MIB),
         cost_estimate=pl.CostEstimate(
-            flops=4 * rows * width * hidden * n_blocks,
-            bytes_accessed=4 * width * hidden * n_blocks + 8 * rows * width,
-            transcendentals=rows * hidden * n_blocks,
+            flops=4 * n_rows * width * hidden * n_blocks,
+            bytes_accessed=4 * width * hidden * n_blocks + 8 * n_rows * width,
+            transcendentals=n_rows * hidden * n_blocks,
         ),
         name="experts",
-    )(normed, weights, *ups, *downs)
-
-
-def expert_weights(routing, combine, experts):
-    return jnp.stack(
-        [jnp.sum(jnp.where(routing == expert, combine, 0.0), axis=-1) for expert in experts], axis=-1
-    )
-
-
-def gather_blocks(up, down):
-    n_parts = lax.axis_size("group") * lax.axis_size("expert")
-    part = lax.axis_index("group") * lax.axis_size("expert") + lax.axis_index("expert")
-    size = up.shape[1] // n_parts
-    mine = (
-        lax.dynamic_slice_in_dim(up, part * size, size, axis=1),
-        lax.dynamic_slice_in_dim(down, part * size, size, axis=0),
-    )
-    far = exchange(mine, "row", 4)
-    near = exchange(mine, "row", 1)
-    far_near = exchange(far, "row", 1)
-    blocks = [[(up, down)]]
-    for piece in (near, far, far_near):
+    )(weights, *sets, *totals, *weights_in)
+
+
+def expert_weights(routing, combine, n_experts):
+    route, weight = (value.reshape(-1, value.shape[-1]) for value in (routing, combine))
+    return jnp.stack([jnp.sum(jnp.where(route == e, weight, 0.0), axis=-1) for e in range(n_experts)])
+
+
+def tie(value, *others):
+    return lax.optimization_barrier((value, others))[0]
+
+
+class Weights:
+    def __init__(self, up, down):
+        n_parts = lax.axis_size("group") * lax.axis_size("expert")
+        part = lax.axis_index("group") * lax.axis_size("expert") + lax.axis_index("expert")
+        size = up.shape[1] // n_parts
+        self.own = ([up], [down])
+        self.part = (
+            lax.dynamic_slice_in_dim(up, part * size, size, axis=1),
+            lax.dynamic_slice_in_dim(down, part * size, size, axis=0),
+        )
+
+    @staticmethod
+    def spread(piece):
         other = exchange(piece, "group", 1)
-        blocks.append([piece, other, exchange(piece, "expert", 1), exchange(other, "expert", 1)])
-    return blocks
-
-
-def all_experts(residual, normed, routing, combine, up_weight, down_weight):
-    mine = lax.axis_index("row") // 2
-    flat = lambda value: value.reshape(-1, value.shape[-1])
-    weights = lambda first: expert_weights(flat(routing), flat(combine), (first, first ^ 2))
-    other_weights = exchange(weights(mine ^ 1).T, "row", 2).T
-    blocks = gather_blocks(up_weight[0], down_weight[0])
-    other = exchange(normed, "row", 2)
-    own_out = run_experts(normed, weights(mine), blocks)
-    other_out = run_experts(other, other_weights, blocks).astype(jnp.bfloat16)
-    returned = exchange(other_out, "row", 2)
-    return residual.astype(jnp.float32) + own_out + returned.astype(jnp.float32)
+        pieces = [piece, other, exchange(piece, "expert", 1), exchange(other, "expert", 1)]
+        return tuple(list(side) for side in zip(*pieces))
 
 
 def routed_experts(residual, normed, routing, combine, up_weight, down_weight):
@@ -373,6 +445,18 @@
         spectra.reshape(n_dev, -1, spectra.shape[1]), axes, split_axis=0, concat_axis=0, tiled=True
     )
     bias = spec_bias.reshape(2, n_blocks, -1).transpose(1, 0, 2).reshape(n_blocks, -1)
+    gain = ln_second.reshape(1, width)
+    pairs = lax.axis_size("group") == 2 and lax.axis_size("expert") == 2
+    every_expert = lax.axis_size("row") == 2 * routing.shape[-1] and routing.shape[-1] == 4
+    dense = pairs and every_expert
+    if dense:
+        weights = Weights(up_weight[0], down_weight[0])
+        table = expert_weights(routing, combine, routing.shape[-1])
+        half_size = table.shape[1] // 2
+        arriving = [exchange(table[:, :half_size], "row", 1), exchange(table[:, half_size:], "row", 2)]
+        near = exchange(weights.part, "row", 3)
+        far_up = exchange(weights.part[0], "row", 4)
+        bias = gate(bias, far_up, *near, *arriving)
     mixed = mix_modes(
         by_column.reshape(spectra.shape),
         pick(forward_rows),
@@ -385,14 +469,36 @@
     by_row = lax.all_to_all(
         mixed.reshape(n_dev, -1, mixed.shape[1]), axes, split_axis=0, concat_axis=0, tiled=True
     )
-    residual, normed = add_mixing(
-        by_row.reshape(mixed.shape), jnp.asarray(inverse_cols), flat_tokens, ln_second.reshape(1, width)
-    )
-    pairs = lax.axis_size("group") == 2 and lax.axis_size("expert") == 2
-    every_expert = lax.axis_size("row") == 2 * routing.shape[-1] and routing.shape[-1] == 4
-    moe = all_experts if pairs and every_expert else routed_experts
-    final = moe(residual, normed, routing, combine, up_weight, down_weight)
-    return final.astype(jnp.bfloat16).reshape(tokens.shape)
+    if dense:
+        near_all = Weights.spread(near)
+        far_down = exchange(weights.part[1], "row", 4)
+        far_near_up = exchange(far_up, "row", 3)
+        gain = gate(gain, far_down, far_near_up, *near_all[0], *near_all[1])
+    residual, norm_a, norm_b = add_mixing(
+        by_row.reshape(mixed.shape), jnp.asarray(inverse_cols), flat_tokens, gain
+    )
+    if not dense:
+        normed = jnp.concatenate([norm_a, norm_b])
+        final = routed_experts(residual, normed, routing, combine, up_weight, down_weight)
+        return final.astype(jnp.bfloat16).reshape(tokens.shape)
+
+    from_y = exchange(norm_a, "row", 1)
+    from_z = exchange(norm_b, "row", 2)
+    far_near_down = exchange(far_down, "row", 3)
+    far_all = Weights.spread((far_up, far_down))
+    far_near_all = Weights.spread((far_near_up, far_near_down))
+    expert = lax.axis_index("row") // 2
+    pick_weights = lambda columns, numbers: jnp.stack(
+        [lax.dynamic_index_in_dim(columns, expert ^ number, 0, keepdims=False) for number in numbers], axis=1
+    )
+    table_in = jnp.concatenate(arriving, axis=1)
+    lower, upper = [weights.own, near_all], [far_all, far_near_all]
+    (own,) = run_experts([norm_a, norm_b], pick_weights(table, (0, 1)), lower)
+    back_y, back_z = run_experts([from_y, from_z], pick_weights(table_in, (0, 1, 2, 3)), lower + upper, split=True)
+    back_a = exchange(back_y, "row", 1)
+    back_b = exchange(back_z, "row", 2)
+    (own,) = run_experts([norm_a, norm_b], pick_weights(table, (2, 3)), upper, [own])
+    return add_outputs(residual, own, back_a, back_b).reshape(tokens.shape)
 
 
 def solution(mesh):

time: 375 us -> 322 us (0.86)
  waiting for transfers between devices: 204 us -> 140 us
  Pallas kernels: 97.1 us -> 109 us
  starting transfers between devices: 38 us -> 46.1 us
  other arithmetic: 12.4 us -> 8.01 us
  local copies, waits for them, and re-layouts: 21.4 us -> 17.1 us
    ppermute x27 -> x30, waiting for transfers between devices: 169 us -> 102 us  [exchange(): return lax.ppermute(value, axis, pairs)]
    all_to_all x1, waiting for transfers between devices: 0.01 us -> 38.3 us  [per_device(): lax.all_to_all(mixed.reshape(n_dev, -1, mixed.shape[1]), axes, split_axis...]
    all_to_all x1, waiting for transfers between devices: 35.8 us -> 0.01 us  [per_device(): lax.all_to_all(spectra.reshape(n_dev, -1, spectra.shape[1]), axes, split_...]
    ppermute x27 -> x30, starting transfers between devices: 19.1 us -> 34.9 us  [exchange(): return lax.ppermute(value, axis, pairs)]
    unnamed x67 -> x51, local copies, waits for them, and re-layouts: 17.7 us -> 8.11 us
    convert_element_type x2 -> x0, other arithmetic: 7.23 us -> none  [the longest x1 4.72 us: per_device(): return final.astype(jnp.bfloat16).reshape(tokens.shape)]
    pallas_call x3 -> x7, Pallas kernels: 86.9 us -> 92.9 us  [the longest x3 80.8 us: run_experts(): pl.pallas_call(functools.partial(experts_kernel, counts, len(sets), len(o...]
    all_to_all x1, starting transfers between devices: 11.4 us -> 6.18 us  [per_device(): lax.all_to_all(mixed.reshape(n_dev, -1, mixed.shape[1]), axes, split_axis...]
  transfers between devices with their start and end apart: 29 -> 32, of which waited for: 13 -> 6; matrix products, arithmetic and copies ran while one was open for 2% -> 5% of each run, Pallas kernels for 12% -> 22%
where the time goes in v3:
time: 322 us; the launch traced here: 321 us
  waiting for transfers between devices  140 us (43%)
  Pallas kernels  109 us (34%)
  starting transfers between devices  46.1 us (14%)
  local copies, waits for them, and re-layouts  17.1 us (5%)
  other arithmetic  8.01 us (2%)
    ppermute x30, waiting for transfers between devices, exchange(): return lax.ppermute(value, axis, pairs)  102 us
    pallas_call x3, Pallas kernels, run_experts(): pl.pallas_call(functools.partial(experts_kernel, counts, len(sets), len(o...  80.8 us
    all_to_all x1, waiting for transfers between devices, per_device(): lax.all_to_all(mixed.reshape(n_dev, -1, mixed.shape[1]), axes, split_axis...  38.3 us
    ppermute x30, starting transfers between devices, exchange(): return lax.ppermute(value, axis, pairs)  34.9 us
    pallas_call x1, Pallas kernels, mix_modes(): pl.pallas_call(modes_kernel, grid=(per_dev,), out_shape=jax.ShapeDtypeStr...  8.47 us
    unnamed x51, local copies, waits for them, and re-layouts  8.11 us
    pallas_call x1, Pallas kernels, add_mixing(): pl.pallas_call(residual_kernel, grid=(steps,), out_shape=[jax.ShapeDtypeS...  7.96 us
    pallas_call x1, Pallas kernels, column_spectra(): pl.pallas_call(spectra_kernel, out_shape=jax.ShapeDtypeStruct((rows_out,...  7.93 us
  transfers between devices with their start and end apart: 32, of which 6 were waited for; matrix products, arithmetic and copies ran while one was open for 5% of the time, Pallas kernels for 22%

profile of v3, /device:TPU:0, one launch (start us, length us, event | category | flops | bytes accessed | tf_op | source)
XLA Modules:
  0.0 321.3 jit_solution(573613666702723134)
XLA Ops:
  1.3 2.1 dynamic-slice_bitcast_fusion.1
  3.4 4.0 %collective-permute-start.1 = (bf16[1024,384]{1,0:T(8,128)(2,1)}, bf16[1024,384]{1,0:T(8,128)(2,1)}, u32[]{:S(2)}, u32[]{:S(2)}) collective-permute-start(bf16[1024,384]{1,0:T(8,128)(2,1)} %dynamic-slice_bitcast_fusion.1), channel_id=1, source_target_pairs={{0,6},{2,4},{4,2},{6,0},{8,14},{10,12},{12,10},{14,8},{1,7},{3,5},... | collective-permute-start | bytes 2359304 | tf_op jit(solution)/shard_map/ppermute | solution.py:18
  7.4 2.6 collective-permute-start
  10.0 2.1 dynamic-slice_bitcast_fusion
  14.5 7.9 %column_spectra.1 = bf16[256,4096]{1,0:T(8,128)(2,1)} custom-call(bf16[1024,1024]{1,0:T(8,128)(2,1)} %bitcast.74, f32[1,1024]{1,0:T(1,128)} %bitcast.76, bf16[4,256,1024]{2,1,0:T(8,128)(2,1)} %constant.74.clone.table), custom_call_target="tpu_custom_call" | custom-call | flops 2147483648 | bytes 6291456 | tf_op jit(solution)/shard_map/column_spectra/pallas_call | solution.py:88
  22.4 5.1 %all-to-all-start = ((bf16[16,16,4096]{2,1,0:T(8,128)(2,1)}), bf16[16,16,4096]{2,1,0:T(8,128)(2,1)S(1)}, u32[]{:S(2)}, u32[]{:S(2)}) async-start(bf16[16,16,4096]{2,1,0:T(8,128)(2,1)} %bitcast.60), calls=%async_computation | async-start | bytes 4194304 | tf_op jit(solution)/shard_map/all_to_all | solution.py:444
  30.2 46.4 %collective-permute-done.2.refs_3_.refs_7_.refs_8_ = bf16[384,1024]{1,0:T(8,128)(2,1)} collective-permute-done((bf16[384,1024]{1,0:T(8,128)(2,1)}, bf16[384,1024]{1,0:T(8,128)(2,1)}, u32[]{:S(2)}, u32[]{:S(2)}) %collective-permute-start.2) | collective-permute-done | bytes 786464 | tf_op jit(solution)/shard_map/ppermute | solution.py:18
  81.4 27.8 %collective-permute-done.4.refs_5_ = f32[4,512]{1,0:T(4,128)S(1)} collective-permute-done((f32[4,512]{1,0:T(4,128)S(1)}, f32[4,512]{1,0:T(4,128)S(1)}, u32[]{:S(2)}, u32[]{:S(2)}) %collective-permute-start.4) | collective-permute-done | bytes 8224 | tf_op jit(solution)/shard_map/ppermute | solution.py:18
  109.6 2.4 collective-permute-start.6
  119.0 2.7 maximum_maximum_fusion
  122.8 11.7 %collective-permute-done.6.refs_2_.refs_11_.refs_20_ = bf16[1024,384]{1,0:T(8,128)(2,1)} collective-permute-done((bf16[1024,384]{1,0:T(8,128)(2,1)}, bf16[1024,384]{1,0:T(8,128)(2,1)}, u32[]{:S(2)}, u32[]{:S(2)}) %collective-permute-start.6) | collective-permute-done | bytes 786464 | tf_op jit(solution)/shard_map/ppermute | solution.py:18
  136.5 14.8 %collective-permute-done.22.refs_15_.refs_24_ = bf16[384,1024]{1,0:T(8,128)(2,1)} collective-permute-done((bf16[384,1024]{1,0:T(8,128)(2,1)}, bf16[384,1024]{1,0:T(8,128)(2,1)}, u32[]{:S(2)}, u32[]{:S(2)}) %collective-permute-start.22) | collective-permute-done | bytes 786464 | tf_op jit(solution)/shard_map/ppermute | solution.py:18
  153.1 8.5 %mix_modes.1 = bf16[256,4096]{1,0:T(8,128)(2,1)} custom-call(bf16[256,4096]{1,0:T(8,128)(2,1)} %bitcast.59, bf16[2,512,256]{2,1,0:T(8,128)(2,1)} %pad_maximum_fusion.forward, bf16[8,256,256]{2,1,0:T(8,128)(2,1)} %get-tuple-element.33.first, bf16[8,256,256]{2,1,0:T(8,128)(2,1)} %get-tuple-element.34.second, f32[8,256]{1,0:T(8,128)} %gate.2.bias, ...), custom_call_target="tpu_custom_call" | custom-call | flops 4294967296 | bytes 6291456 | tf_op jit(solution)/shard_map/mix_modes/pallas_call | solution.py:139
  161.6 6.2 %all-to-all-start.1 = ((bf16[16,16,4096]{2,1,0:T(8,128)(2,1)}), bf16[16,16,4096]{2,1,0:T(8,128)(2,1)S(1)}, u32[]{:S(2)}, u32[]{:S(2)}) async-start(bf16[16,16,4096]{2,1,0:T(8,128)(2,1)} %bitcast.62), calls=%async_computation.1 | async-start | bytes 4194304 | tf_op jit(solution)/shard_map/all_to_all | solution.py:469
  170.6 38.3 %all-to-all-done.1 = bf16[16,16,4096]{2,1,0:T(8,128)(2,1)S(1)} async-done(((bf16[16,16,4096]{2,1,0:T(8,128)(2,1)}), bf16[16,16,4096]{2,1,0:T(8,128)(2,1)S(1)}, u32[]{:S(2)}, u32[]{:S(2)}) %all-to-all-start.1) | async-done | bytes 2097184 | tf_op jit(solution)/shard_map/all_to_all | solution.py:469
  210.2 8.0 %add_mixing.1 = (bf16[1024,1024]{1,0:T(8,128)(2,1)}, bf16[512,1024]{1,0:T(8,128)(2,1)}, bf16[512,1024]{1,0:T(8,128)(2,1)}) custom-call(bf16[256,4096]{1,0:T(8,128)(2,1)} %bitcast.61, bf16[4,1024,256]{2,1,0:T(8,128)(2,1)} %constant.79.clone.table, bf16[1024,1024]{1,0:T(8,128)(2,1)} %bitcast.75, f32[1,1024]{1,0:T(1,128)} %gate.3.gain), custom_call_target="tpu_custom_call" | custom-call | flops 2147483648 | bytes 10485760 | tf_op jit(solution)/shard_map/add_mixing/pallas_call | solution.py:193
  219.5 3.4 %collective-permute-start.26 = (bf16[512,1024]{1,0:T(8,128)(2,1)}, bf16[512,1024]{1,0:T(8,128)(2,1)S(1)}, u32[]{:S(2)}, u32[]{:S(2)}) collective-permute-start(bf16[512,1024]{1,0:T(8,128)(2,1)} %get-tuple-element.11.refs_0_), channel_id=1, source_target_pairs={{0,2},{2,0},{4,6},{6,4},{8,10},{10,8},{12,14},{14,12},{1,3},{3,1},... | collective-permute-start | bytes 3145736 | tf_op jit(solution)/shard_map/ppermute | solution.py:18
  222.9 5.7 %collective-permute-start.27 = (bf16[512,1024]{1,0:T(8,128)(2,1)}, bf16[512,1024]{1,0:T(8,128)(2,1)S(1)}, u32[]{:S(2)}, u32[]{:S(2)}) collective-permute-start(bf16[512,1024]{1,0:T(8,128)(2,1)} %get-tuple-element.12.refs_1_), channel_id=1, source_target_pairs={{0,4},{2,6},{4,0},{6,2},{8,12},{10,14},{12,8},{14,10},{1,5},{3,7},... | collective-permute-start | bytes 3145736 | tf_op jit(solution)/shard_map/ppermute | solution.py:18
  228.6 21.9 %experts.3.refs_2_ = f32[1024,1024]{1,0:T(8,128)} custom-call(f32[1024,2]{1,0:T(8,128)} %copy.29.weights, bf16[512,1024]{1,0:T(8,128)(2,1)} %get-tuple-element.11.refs_0_, bf16[512,1024]{1,0:T(8,128)(2,1)} %get-tuple-element.12.refs_1_, bf16[1024,1536]{1,0:T(8,128)(2,1)} %bitcast.63, bf16[1536,1024]{1,0:T(8,128)(2,1)} %bitcast.65, ...), custom_call_target="tpu_custom_call" | custom-call | flops 12884901888 | bytes 20971520 | tf_op jit(solution)/shard_map/experts/pallas_call | solution.py:338
  253.1 35.6 %experts.5 = (bf16[512,1024]{1,0:T(8,128)(2,1)}, bf16[512,1024]{1,0:T(8,128)(2,1)}) custom-call(f32[1024,4]{1,0:T(8,128)} %copy.31.weights, bf16[512,1024]{1,0:T(8,128)(2,1)} %copy-done.18, bf16[512,1024]{1,0:T(8,128)(2,1)} %copy-done.19, bf16[1024,1536]{1,0:T(8,128)(2,1)} %bitcast.64, bf16[1536,1024]{1,0:T(8,128)(2,1)} %bitcast.66, ...), custom_call_target="tpu_custom_call" | custom-call | flops 25769803776 | bytes 33554432 | tf_op jit(solution)/shard_map/experts/pallas_call | solution.py:338
  289.1 2.6 collective-permute-start.29
  291.7 23.3 %experts.4.own = f32[1024,1024]{1,0:T(8,128)} custom-call(f32[1024,2]{1,0:T(8,128)} %copy.30.weights, bf16[512,1024]{1,0:T(8,128)(2,1)} %get-tuple-element.11.refs_0_, bf16[512,1024]{1,0:T(8,128)(2,1)} %get-tuple-element.12.refs_1_, f32[1024,1024]{1,0:T(8,128)} %experts.3.refs_2_, bf16[1024,384]{1,0:T(8,128)(2,1)} %collective-permute-done.refs_1_.refs_3_.refs_12_, ...), custom_call_target="tpu_custom_call" | custom-call | flops 12884901888 | bytes 20971520 | tf_op jit(solution)/shard_map/experts/pallas_call | solution.py:338
  315.0 2.2 copy-done
  317.2 4.1 %add_outputs.1 = bf16[1024,1024]{1,0:T(8,128)(2,1)} custom-call(bf16[1024,1024]{1,0:T(8,128)(2,1)S(1)} %copy-done.1, f32[1024,1024]{1,0:T(8,128)S(1)} %copy-done, bf16[512,1024]{1,0:T(8,128)(2,1)S(1)} %collective-permute-done.28.back_a, bf16[512,1024]{1,0:T(8,128)(2,1)} %collective-permute-done.29.back_b), custom_call_target="tpu_custom_call" | custom-call | tf_op jit(solution)/shard_map/add_outputs/pallas_call | solution.py:228
  (123 shorter events, 31.8 us)
Async XLA Ops:
  3.4 75.1 %collective-permute-start.1 = (bf16[1024,384]{1,0:T(8,128)(2,1)}, bf16[1024,384]{1,0:T(8,128)(2,1)}, u32[]{:S(2)}, u32[]{:S(2)}) collective-permute-start(bf16[1024,384]{1,0:T(8,128)(2,1)} %dynamic-slice_bitcast_fusion.1), channel_id=1, source_target_pairs={{0,6},{2,4},{4,2},{6,0},{8,14},{10,12},{12,10},{14,8},{1,7},{3,5},... | collective-permute-start | bytes 2359304 | tf_op jit(solution)/shard_map/ppermute | solution.py:18
  7.4 101.7 %collective-permute-start = (bf16[1024,384]{1,0:T(8,128)(2,1)}, bf16[1024,384]{1,0:T(8,128)(2,1)}, u32[]{:S(2)}, u32[]{:S(2)}) collective-permute-start(bf16[1024,384]{1,0:T(8,128)(2,1)} %dynamic-slice_bitcast_fusion.1), channel_id=1, source_target_pairs={{0,8},{2,10},{4,12},{6,14},{8,0},{10,2},{12,4},{14,6},{1,9},{3,11}... | collective-permute-start | bytes 2359304 | tf_op jit(solution)/shard_map/ppermute | solution.py:18
  12.1 64.5 %collective-permute-start.2 = (bf16[384,1024]{1,0:T(8,128)(2,1)}, bf16[384,1024]{1,0:T(8,128)(2,1)}, u32[]{:S(2)}, u32[]{:S(2)}) collective-permute-start(bf16[384,1024]{1,0:T(8,128)(2,1)} %dynamic-slice_bitcast_fusion), channel_id=1, source_target_pairs={{0,6},{2,4},{4,2},{6,0},{8,14},{10,12},{12,10},{14,8},{1,7},{3,5},... | collective-permute-start | bytes 2359304 | tf_op jit(solution)/shard_map/ppermute | solution.py:18
  12.4 97.2 %collective-permute-start.5 = (bf16[384,1024]{1,0:T(8,128)(2,1)}, bf16[384,1024]{1,0:T(8,128)(2,1)}, u32[]{:S(2)}, u32[]{:S(2)}) collective-permute-start(bf16[384,1024]{1,0:T(8,128)(2,1)} %dynamic-slice_bitcast_fusion), channel_id=1, source_target_pairs={{0,8},{2,10},{4,12},{6,14},{8,0},{10,2},{12,4},{14,6},{1,9},{3,11}... | collective-permute-start | bytes 2359304 | tf_op jit(solution)/shard_map/ppermute | solution.py:18
  12.6 68.5 %collective-permute-start.3 = (f32[4,512]{1,0:T(4,128)S(1)}, f32[4,512]{1,0:T(4,128)S(1)}, u32[]{:S(2)}, u32[]{:S(2)}) collective-permute-start(f32[4,512]{1,0:T(4,128)S(1)} %get-tuple-element.32), channel_id=1, source_target_pairs={{0,2},{2,0},{4,6},{6,4},{8,10},{10,8},{12,14},{14,12},{1,3},{3,1},... | collective-permute-start | bytes 24584 | tf_op jit(solution)/shard_map/ppermute | solution.py:18
  22.4 129.4 %all-to-all-start = ((bf16[16,16,4096]{2,1,0:T(8,128)(2,1)}), bf16[16,16,4096]{2,1,0:T(8,128)(2,1)S(1)}, u32[]{:S(2)}, u32[]{:S(2)}) async-start(bf16[16,16,4096]{2,1,0:T(8,128)(2,1)} %bitcast.60), calls=%async_computation | async-start | bytes 4194304 | tf_op jit(solution)/shard_map/all_to_all | solution.py:444
  76.6 35.5 %collective-permute-start.10 = (bf16[384,1024]{1,0:T(8,128)(2,1)}, bf16[384,1024]{1,0:T(8,128)(2,1)S(1)}, u32[]{:S(2)}, u32[]{:S(2)}) collective-permute-start(bf16[384,1024]{1,0:T(8,128)(2,1)} %collective-permute-done.2.refs_3_.refs_7_.refs_8_), channel_id=1, source_target_pairs={{0,16},{16,0},{1,17},{17,1},{2,18},{18,2},{3,19},{19,3},{4,20},{20... | collective-permute-start | bytes 2359304 | tf_op jit(solution)/shard_map/ppermute | solution.py:18
  78.5 35.0 %collective-permute-start.7 = (bf16[1024,384]{1,0:T(8,128)(2,1)}, bf16[1024,384]{1,0:T(8,128)(2,1)S(1)}, u32[]{:S(2)}, u32[]{:S(2)}) collective-permute-start(bf16[1024,384]{1,0:T(8,128)(2,1)} %collective-permute-done.1.refs_2_.refs_3_.refs_4_), channel_id=1, source_target_pairs={{0,16},{16,0},{1,17},{17,1},{2,18},{18,2},{3,19},{19,3},{4,20},{20... | collective-permute-start | bytes 2359304 | tf_op jit(solution)/shard_map/ppermute | solution.py:18
  112.1 39.3 %collective-permute-start.13 = (bf16[1024,384]{1,0:T(8,128)(2,1)}, bf16[1024,384]{1,0:T(8,128)(2,1)}, u32[]{:S(2)}, u32[]{:S(2)}) collective-permute-start(bf16[1024,384]{1,0:T(8,128)(2,1)} %collective-permute-done.refs_1_.refs_3_.refs_12_), channel_id=1, source_target_pairs={{0,16},{16,0},{1,17},{17,1},{2,18},{18,2},{3,19},{19,3},{4,20},{20... | collective-permute-start | bytes 2359304 | tf_op jit(solution)/shard_map/ppermute | solution.py:18
  113.6 37.7 %collective-permute-start.22 = (bf16[384,1024]{1,0:T(8,128)(2,1)}, bf16[384,1024]{1,0:T(8,128)(2,1)}, u32[]{:S(2)}, u32[]{:S(2)}) collective-permute-start(bf16[384,1024]{1,0:T(8,128)(2,1)} %collective-permute-done.5.refs_1_.refs_7_.refs_16_), channel_id=1, source_target_pairs={{0,6},{2,4},{4,2},{6,0},{8,14},{10,12},{12,10},{14,8},{1,7},{3,5},... | collective-permute-start | bytes 2359304 | tf_op jit(solution)/shard_map/ppermute | solution.py:18
  134.5 33.3 %collective-permute-start.16 = (bf16[384,1024]{1,0:T(8,128)(2,1)}, bf16[384,1024]{1,0:T(8,128)(2,1)S(1)}, u32[]{:S(2)}, u32[]{:S(2)}) collective-permute-start(bf16[384,1024]{1,0:T(8,128)(2,1)} %collective-permute-done.5.refs_1_.refs_7_.refs_16_), channel_id=1, source_target_pairs={{0,16},{16,0},{1,17},{17,1},{2,18},{18,2},{3,19},{19,3},{4,20},{20... | collective-permute-start | bytes 2359304 | tf_op jit(solution)/shard_map/ppermute | solution.py:18
  136.0 33.3 %collective-permute-start.14 = (bf16[1024,384]{1,0:T(8,128)(2,1)}, bf16[1024,384]{1,0:T(8,128)(2,1)}, u32[]{:S(2)}, u32[]{:S(2)}) collective-permute-start(bf16[1024,384]{1,0:T(8,128)(2,1)} %collective-permute-done.refs_1_.refs_3_.refs_12_), channel_id=1, source_target_pairs={{0,1},{1,0},{2,3},{3,2},{4,5},{5,4},{6,7},{7,6},{8,9},{9,8},{10,11... | collective-permute-start | bytes 2359304 | tf_op jit(solution)/shard_map/ppermute | solution.py:18
  136.0 33.5 %collective-permute-start.17 = (bf16[384,1024]{1,0:T(8,128)(2,1)}, bf16[384,1024]{1,0:T(8,128)(2,1)}, u32[]{:S(2)}, u32[]{:S(2)}) collective-permute-start(bf16[384,1024]{1,0:T(8,128)(2,1)} %collective-permute-done.5.refs_1_.refs_7_.refs_16_), channel_id=1, source_target_pairs={{0,1},{1,0},{2,3},{3,2},{4,5},{5,4},{6,7},{7,6},{8,9},{9,8},{10,11... | collective-permute-start | bytes 2359304 | tf_op jit(solution)/shard_map/ppermute | solution.py:18
  161.6 47.3 %all-to-all-start.1 = ((bf16[16,16,4096]{2,1,0:T(8,128)(2,1)}), bf16[16,16,4096]{2,1,0:T(8,128)(2,1)S(1)}, u32[]{:S(2)}, u32[]{:S(2)}) async-start(bf16[16,16,4096]{2,1,0:T(8,128)(2,1)} %bitcast.62), calls=%async_computation.1 | async-start | bytes 4194304 | tf_op jit(solution)/shard_map/all_to_all | solution.py:469
  167.8 50.4 %collective-permute-start.19 = (bf16[1024,384]{1,0:T(8,128)(2,1)}, bf16[1024,384]{1,0:T(8,128)(2,1)}, u32[]{:S(2)}, u32[]{:S(2)}) collective-permute-start(bf16[1024,384]{1,0:T(8,128)(2,1)} %collective-permute-done.6.refs_2_.refs_11_.refs_20_), channel_id=1, source_target_pairs={{0,16},{16,0},{1,17},{17,1},{2,18},{18,2},{3,19},{19,3},{4,20},{20... | collective-permute-start | bytes 2359304 | tf_op jit(solution)/shard_map/ppermute | solution.py:18
  169.4 49.7 %collective-permute-start.20 = (bf16[1024,384]{1,0:T(8,128)(2,1)}, bf16[1024,384]{1,0:T(8,128)(2,1)}, u32[]{:S(2)}, u32[]{:S(2)}) collective-permute-start(bf16[1024,384]{1,0:T(8,128)(2,1)} %collective-permute-done.6.refs_2_.refs_11_.refs_20_), channel_id=1, source_target_pairs={{0,1},{1,0},{2,3},{3,2},{4,5},{5,4},{6,7},{7,6},{8,9},{9,8},{10,11... | collective-permute-start | bytes 2359304 | tf_op jit(solution)/shard_map/ppermute | solution.py:18
  169.5 49.5 %collective-permute-start.23 = (bf16[384,1024]{1,0:T(8,128)(2,1)}, bf16[384,1024]{1,0:T(8,128)(2,1)}, u32[]{:S(2)}, u32[]{:S(2)}) collective-permute-start(bf16[384,1024]{1,0:T(8,128)(2,1)} %collective-permute-done.22.refs_15_.refs_24_), channel_id=1, source_target_pairs={{0,16},{16,0},{1,17},{17,1},{2,18},{18,2},{3,19},{19,3},{4,20},{20... | collective-permute-start | bytes 2359304 | tf_op jit(solution)/shard_map/ppermute | solution.py:18
  170.1 49.5 %collective-permute-start.24 = (bf16[384,1024]{1,0:T(8,128)(2,1)}, bf16[384,1024]{1,0:T(8,128)(2,1)}, u32[]{:S(2)}, u32[]{:S(2)}) collective-permute-start(bf16[384,1024]{1,0:T(8,128)(2,1)} %collective-permute-done.22.refs_15_.refs_24_), channel_id=1, source_target_pairs={{0,1},{1,0},{2,3},{3,2},{4,5},{5,4},{6,7},{7,6},{8,9},{9,8},{10,11... | collective-permute-start | bytes 2359304 | tf_op jit(solution)/shard_map/ppermute | solution.py:18
  170.2 52.8 %collective-permute-start.15 = (bf16[1024,384]{1,0:T(8,128)(2,1)}, bf16[1024,384]{1,0:T(8,128)(2,1)}, u32[]{:S(2)}, u32[]{:S(2)}) collective-permute-start(bf16[1024,384]{1,0:T(8,128)(2,1)} %collective-permute-done.13.refs_4_.refs_13_), channel_id=1, source_target_pairs={{0,1},{1,0},{2,3},{3,2},{4,5},{5,4},{6,7},{7,6},{8,9},{9,8},{10,11... | collective-permute-start | bytes 2359304 | tf_op jit(solution)/shard_map/ppermute | solution.py:18
  218.2 32.4 %collective-permute-start.18 = (bf16[384,1024]{1,0:T(8,128)(2,1)S(1)}, bf16[384,1024]{1,0:T(8,128)(2,1)S(1)}, u32[]{:S(2)}, u32[]{:S(2)}) collective-permute-start(bf16[384,1024]{1,0:T(8,128)(2,1)S(1)} %collective-permute-done.16.refs_8_.refs_17_), channel_id=1, source_target_pairs={{0,1},{1,0},{2,3},{3,2},{4,5},{5,4},{6,7},{7,6},{8,9},{9,8},{10,11... | collective-permute-start | bytes 2359304 | tf_op jit(solution)/shard_map/ppermute | solution.py:18
  219.0 31.6 %collective-permute-start.21 = (bf16[1024,384]{1,0:T(8,128)(2,1)}, bf16[1024,384]{1,0:T(8,128)(2,1)}, u32[]{:S(2)}, u32[]{:S(2)}) collective-permute-start(bf16[1024,384]{1,0:T(8,128)(2,1)} %collective-permute-done.19.refs_12_.refs_21_), channel_id=1, source_target_pairs={{0,1},{1,0},{2,3},{3,2},{4,5},{5,4},{6,7},{7,6},{8,9},{9,8},{10,11... | collective-permute-start | bytes 2359304 | tf_op jit(solution)/shard_map/ppermute | solution.py:18
  219.1 31.5 %collective-permute-start.25 = (bf16[384,1024]{1,0:T(8,128)(2,1)}, bf16[384,1024]{1,0:T(8,128)(2,1)}, u32[]{:S(2)}, u32[]{:S(2)}) collective-permute-start(bf16[384,1024]{1,0:T(8,128)(2,1)} %collective-permute-done.23.refs_16_.refs_25_), channel_id=1, source_target_pairs={{0,1},{1,0},{2,3},{3,2},{4,5},{5,4},{6,7},{7,6},{8,9},{9,8},{10,11... | collective-permute-start | bytes 2359304 | tf_op jit(solution)/shard_map/ppermute | solution.py:18
  219.5 31.1 %collective-permute-start.26 = (bf16[512,1024]{1,0:T(8,128)(2,1)}, bf16[512,1024]{1,0:T(8,128)(2,1)S(1)}, u32[]{:S(2)}, u32[]{:S(2)}) collective-permute-start(bf16[512,1024]{1,0:T(8,128)(2,1)} %get-tuple-element.11.refs_0_), channel_id=1, source_target_pairs={{0,2},{2,0},{4,6},{6,4},{8,10},{10,8},{12,14},{14,12},{1,3},{3,1},... | collective-permute-start | bytes 3145736 | tf_op jit(solution)/shard_map/ppermute | solution.py:18
  222.9 29.2 %collective-permute-start.27 = (bf16[512,1024]{1,0:T(8,128)(2,1)}, bf16[512,1024]{1,0:T(8,128)(2,1)S(1)}, u32[]{:S(2)}, u32[]{:S(2)}) collective-permute-start(bf16[512,1024]{1,0:T(8,128)(2,1)} %get-tuple-element.12.refs_1_), channel_id=1, source_target_pairs={{0,4},{2,6},{4,0},{6,2},{8,12},{10,14},{12,8},{14,10},{1,5},{3,7},... | collective-permute-start | bytes 3145736 | tf_op jit(solution)/shard_map/ppermute | solution.py:18
  (32 other events, 769.5 us)

commit v4 on v3

--- a/solution.py
+++ b/solution.py
@@ -91,7 +91,7 @@
         in_specs=[pl.BlockSpec(memory_space=pltpu.VMEM)] * 3,
         out_specs=pl.BlockSpec(memory_space=pltpu.VMEM),
         scratch_shapes=[pltpu.VMEM((rows_in, width), jnp.bfloat16)],
-        compiler_params=pltpu.CompilerParams(vmem_limit_bytes=60 * MIB),
+        compiler_params=pltpu.CompilerParams(vmem_limit_bytes=20 * MIB),
         cost_estimate=pl.CostEstimate(
             flops=2 * per_dev * rows_out * rows_in * width,
             bytes_accessed=2 * (rows_in * width + rows_out * per_dev * width + table.size),
@@ -150,7 +150,7 @@
         ],
         out_specs=pl.BlockSpec((rows, width), lambda k: (0, k)),
         scratch_shapes=[pltpu.VMEM((modes_rows, width), jnp.bfloat16)],
-        compiler_params=pltpu.CompilerParams(vmem_limit_bytes=60 * MIB),
+        compiler_params=pltpu.CompilerParams(vmem_limit_bytes=20 * MIB),
         cost_estimate=pl.CostEstimate(
             flops=2 * lanes * (2 * rows * modes_rows + modes_rows * 512),
             bytes_accessed=4 * (rows * lanes + first.size),
@@ -177,31 +177,31 @@
             half[...] = normed
 
 
-def half_tiles(tile, width, per_half, n_halves):
+def part_tiles(tile, width, per_part, n_parts):
     return [
-        pl.BlockSpec((tile, width), lambda i, first=index * per_half: (jnp.clip(i - first, 0, per_half - 1), 0))
-        for index in range(n_halves)
+        pl.BlockSpec((tile, width), lambda i, first=index * per_part: (jnp.clip(i - first, 0, per_part - 1), 0))
+        for index in range(n_parts)
     ]
 
 
-def add_mixing(spectra, table, tokens, gain):
+def add_mixing(spectra, table, tokens, gain, n_parts=4):
     per_dev, rows_out, rows_in = table.shape
     width = tokens.shape[1]
-    tile = math.gcd(rows_out // 2, 256)
+    tile = math.gcd(rows_out // n_parts, 256)
     steps = rows_out // tile
     row_tile = pl.BlockSpec((tile, width), lambda i: (i, 0))
     return pl.pallas_call(
         residual_kernel,
         grid=(steps,),
-        out_shape=[jax.ShapeDtypeStruct((rows, width), jnp.bfloat16) for rows in (rows_out, rows_out // 2, rows_out // 2)],
+        out_shape=[jax.ShapeDtypeStruct((rows, width), jnp.bfloat16) for rows in [rows_out] + n_parts * [rows_out // n_parts]],
         in_specs=[
             pl.BlockSpec(spectra.shape, lambda i: (0, 0)),
             pl.BlockSpec((per_dev, tile, rows_in), lambda i: (0, i, 0)),
             row_tile,
             pl.BlockSpec(gain.shape, lambda i: (0, 0)),
         ],
-        out_specs=[row_tile] + half_tiles(tile, width, steps // 2, 2),
-        compiler_params=pltpu.CompilerParams(vmem_limit_bytes=60 * MIB),
+        out_specs=[row_tile] + part_tiles(tile, width, steps // n_parts, n_parts),
+        compiler_params=pltpu.CompilerParams(vmem_limit_bytes=20 * MIB),
         cost_estimate=pl.CostEstimate(
             flops=2 * per_dev * rows_out * rows_in * width,
             bytes_accessed=2 * (3 * rows_out * width + spectra.size + table.size),
@@ -211,29 +211,30 @@
     )(spectra, table, tokens, gain)
 
 
-def sum_kernel(residual, own, back_a, back_b, out):
+def sum_kernel(residual, own, *refs):
+    backs, out = refs[:-1], refs[-1]
     total = residual[...].astype(jnp.float32) + own[...]
-    half = pl.num_programs(0) // 2
-    for index, back in enumerate((back_a, back_b)):
-
-        @pl.when(pl.program_id(0) // half == index)
+    per_part = pl.num_programs(0) // len(backs)
+    for index, back in enumerate(backs):
+
+        @pl.when(pl.program_id(0) // per_part == index)
         def _(back=back):
             out[...] = (total + back[...].astype(jnp.float32)).astype(out.dtype)
 
 
-def add_outputs(residual, own, back_a, back_b):
+def add_outputs(residual, own, backs):
     rows, width = residual.shape
-    tile = math.gcd(rows // 2, 256)
+    tile = math.gcd(rows // len(backs), 256)
     row_tile = pl.BlockSpec((tile, width), lambda i: (i, 0))
     return pl.pallas_call(
         sum_kernel,
         grid=(rows // tile,),
         out_shape=jax.ShapeDtypeStruct(residual.shape, jnp.bfloat16),
-        in_specs=[row_tile, row_tile] + half_tiles(tile, width, rows // tile // 2, 2),
+        in_specs=[row_tile, row_tile] + part_tiles(tile, width, rows // tile // len(backs), len(backs)),
         out_specs=row_tile,
-        compiler_params=pltpu.CompilerParams(vmem_limit_bytes=32 * MIB),
+        compiler_params=pltpu.CompilerParams(vmem_limit_bytes=16 * MIB),
         name="add_outputs",
-    )(residual, own, back_a, back_b)
+    )(residual, own, *backs)
 
 
 def gate(value, *others):
@@ -244,7 +245,7 @@
         in_specs=[anywhere] * (1 + len(others)),
         out_specs=anywhere,
         input_output_aliases={0: 0},
-        compiler_params=pltpu.CompilerParams(vmem_limit_bytes=60 * MIB),
+        compiler_params=pltpu.CompilerParams(vmem_limit_bytes=MIB),
         cost_estimate=pl.CostEstimate(flops=10**11, bytes_accessed=10**8, transcendentals=0),
         name="gate",
     )(value, *others)
@@ -264,8 +265,9 @@
     values, up_all, down_all, set_sem, total_sem, piece_sem = (next(take) for _ in range(6))
     total = outs[0] if n_outs == 1 else next(take)
     n_blocks, _, hidden = up_all.shape
-    tile = values.shape[0] // n_sets
-    rows_of = lambda index: pl.ds(index * tile, tile)
+    tile = math.gcd(values.shape[0], 512)
+    set_size = values.shape[0] // n_sets
+    rows_of = lambda index: pl.ds(index * set_size, set_size)
     loads = [
         pltpu.make_async_copy(ref, values.at[rows_of(index)], set_sem.at[index]) for index, ref in enumerate(sets)
     ]
@@ -314,10 +316,10 @@
             total[rows, :] = term
             return carry
 
-        lax.fori_loop(0, n_sets, token_tile, 0)
+        lax.fori_loop(0, values.shape[0] // tile, token_tile, 0)
     if n_outs > 1:
         for index, out in enumerate(outs):
-            out[...] = total[index * tile : (index + 1) * tile, :].astype(out.dtype)
+            out[...] = total[index * set_size : (index + 1) * set_size, :].astype(out.dtype)
 
 
 def run_experts(sets, weights, blocks, totals=(), split=False, chunk=256):
@@ -335,6 +337,7 @@
     else:
         out_shape = [jax.ShapeDtypeStruct((n_rows, width), jnp.float32)]
     counts = tuple(len(half) for half in halves)
+    used = n_blocks * 4 * width * hidden + 2 * n_rows * width + 4 * n_rows * width + (2 * n_rows * width if split else 0)
     return pl.pallas_call(
         functools.partial(experts_kernel, counts, len(sets), len(out_shape), len(totals), chunk),
         out_shape=out_shape,
@@ -349,7 +352,7 @@
             pltpu.SemaphoreType.DMA((len(weights_in),)),
         ]
         + ([pltpu.VMEM((n_rows, width), jnp.float32)] if split else []),
-        compiler_params=pltpu.CompilerParams(vmem_limit_bytes=60 * MIB),
+        compiler_params=pltpu.CompilerParams(vmem_limit_bytes=used + 4 * MIB),
         cost_estimate=pl.CostEstimate(
             flops=4 * n_rows * width * hidden * n_blocks,
             bytes_accessed=4 * width * hidden * n_blocks + 8 * n_rows * width,
@@ -456,7 +459,7 @@
         arriving = [exchange(table[:, :half_size], "row", 1), exchange(table[:, half_size:], "row", 2)]
         near = exchange(weights.part, "row", 3)
         far_up = exchange(weights.part[0], "row", 4)
-        bias = gate(bias, far_up, *near, *arriving)
+        bias = gate(bias, far_up, *near)
     mixed = mix_modes(
         by_column.reshape(spectra.shape),
         pick(forward_rows),
@@ -473,17 +476,18 @@
         near_all = Weights.spread(near)
         far_down = exchange(weights.part[1], "row", 4)
         far_near_up = exchange(far_up, "row", 3)
-        gain = gate(gain, far_down, far_near_up, *near_all[0], *near_all[1])
-    residual, norm_a, norm_b = add_mixing(
+        gain = gate(gain, far_down, far_near_up, *near_all[0], *near_all[1], *arriving)
+    residual, *norms = add_mixing(
         by_row.reshape(mixed.shape), jnp.asarray(inverse_cols), flat_tokens, gain
     )
     if not dense:
-        normed = jnp.concatenate([norm_a, norm_b])
+        normed = jnp.concatenate(norms)
         final = routed_experts(residual, normed, routing, combine, up_weight, down_weight)
         return final.astype(jnp.bfloat16).reshape(tokens.shape)
 
-    from_y = exchange(norm_a, "row", 1)
-    from_z = exchange(norm_b, "row", 2)
+    per_row = len(norms) // 2
+    rows_of = [1] * per_row + [2] * per_row
+    others = [exchange(norm, "row", mask) for norm, mask in zip(norms, rows_of)]
     far_near_down = exchange(far_down, "row", 3)
     far_all = Weights.spread((far_up, far_down))
     far_near_all = Weights.spread((far_near_up, far_near_down))
@@ -491,14 +495,18 @@
     pick_weights = lambda columns, numbers: jnp.stack(
         [lax.dynamic_index_in_dim(columns, expert ^ number, 0, keepdims=False) for number in numbers], axis=1
     )
-    table_in = jnp.concatenate(arriving, axis=1)
     lower, upper = [weights.own, near_all], [far_all, far_near_all]
-    (own,) = run_experts([norm_a, norm_b], pick_weights(table, (0, 1)), lower)
-    back_y, back_z = run_experts([from_y, from_z], pick_weights(table_in, (0, 1, 2, 3)), lower + upper, split=True)
-    back_a = exchange(back_y, "row", 1)
-    back_b = exchange(back_z, "row", 2)
-    (own,) = run_experts([norm_a, norm_b], pick_weights(table, (2, 3)), upper, [own])
-    return add_outputs(residual, own, back_a, back_b).reshape(tokens.shape)
+    (own,) = run_experts(norms, pick_weights(table, (0, 1)), lower)
+    backs = [None] * len(norms)
+    size = norms[0].shape[0]
+    for index in range(per_row):
+        sets = (index, index + per_row)
+        table_in = jnp.concatenate([side[:, index * size : (index + 1) * size] for side in arriving], axis=1)
+        results = run_experts([others[k] for k in sets], pick_weights(table_in, (0, 1, 2, 3)), lower + upper, split=True)
+        for k, result in zip(sets, results):
+            backs[k] = exchange(result, "row", rows_of[k])
+    (own,) = run_experts(norms, pick_weights(table, (2, 3)), upper, [own])
+    return add_outputs(residual, own, backs).reshape(tokens.shape)
 
 
 def solution(mesh):

time: 322 us -> 315 us (0.978); the launches traced: 321 us -> 309 us
  Pallas kernels: 109 us -> 86.2 us
  local copies, waits for them, and re-layouts: 17.1 us -> 24.2 us
    pallas_call x3 -> x4, Pallas kernels: 80.8 us -> 67.1 us  [run_experts(): pl.pallas_call(functools.partial(experts_kernel, counts, len(sets), len(o...]
    unnamed x51 -> x66, local copies, waits for them, and re-layouts: 8.11 us -> 16.9 us
    pallas_call x1, Pallas kernels: 7.93 us -> 4.41 us  [column_spectra(): pl.pallas_call(spectra_kernel, out_shape=jax.ShapeDtypeStruct((rows_out,...]
    ppermute x30 -> x34, waiting for transfers between devices: 102 us -> 104 us  [exchange(): return lax.ppermute(value, axis, pairs)]
    ppermute x30 -> x34, starting transfers between devices: 34.9 us -> 36.2 us  [exchange(): return lax.ppermute(value, axis, pairs)]
  transfers between devices with their start and end apart: 32 -> 36, of which waited for: 6 -> 5; matrix products, arithmetic and copies ran while one was open for 5% -> 4% of each run, Pallas kernels for 22% -> 27%
where the time goes in v4:
time: 315 us; the launch traced here: 309 us
  waiting for transfers between devices  142 us (45%)
  Pallas kernels  86.2 us (27%)
  starting transfers between devices  47.7 us (15%)
  local copies, waits for them, and re-layouts  24.2 us (8%)
  other arithmetic  7.87 us (2%)
    ppermute x34, waiting for transfers between devices, exchange(): return lax.ppermute(value, axis, pairs)  104 us
    pallas_call x4, Pallas kernels, run_experts(): pl.pallas_call(functools.partial(experts_kernel, counts, len(sets), len(o...  67.1 us
    all_to_all x1, waiting for transfers between devices, per_device(): lax.all_to_all(mixed.reshape(n_dev, -1, mixed.shape[1]), axes, split_axis...  38.3 us
    ppermute x34, starting transfers between devices, exchange(): return lax.ppermute(value, axis, pairs)  36.2 us
    unnamed x66, local copies, waits for them, and re-layouts  16.9 us
    all_to_all x1, starting transfers between devices, per_device(): lax.all_to_all(mixed.reshape(n_dev, -1, mixed.shape[1]), axes, split_axis...  6.39 us
  transfers between devices with their start and end apart: 36, of which 5 were waited for; matrix products, arithmetic and copies ran while one was open for 4% of the time, Pallas kernels for 27%

profile of v4, /device:TPU:0, one launch (start us, length us, event | category | flops | bytes accessed | tf_op | source)
XLA Modules:
  0.0 309.3 jit_solution(15319625418734084083)
XLA Ops:
  0.8 2.1 dynamic-slice_bitcast_fusion.1
  2.9 4.0 %collective-permute-start.1 = (bf16[1024,384]{1,0:T(8,128)(2,1)}, bf16[1024,384]{1,0:T(8,128)(2,1)}, u32[]{:S(2)}, u32[]{:S(2)}) collective-permute-start(bf16[1024,384]{1,0:T(8,128)(2,1)} %dynamic-slice_bitcast_fusion.1), channel_id=1, source_target_pairs={{0,6},{2,4},{4,2},{6,0},{8,14},{10,12},{12,10},{14,8},{1,7},{3,5},... | collective-permute-start | bytes 2359304 | tf_op jit(solution)/shard_map/ppermute | solution.py:18
  6.9 2.6 collective-permute-start
  9.5 2.1 dynamic-slice_bitcast_fusion
  15.6 4.4 %column_spectra.1 = bf16[256,4096]{1,0:T(8,128)(2,1)S(1)} custom-call(bf16[1024,1024]{1,0:T(8,128)(2,1)S(1)} %bitcast.78, f32[1,1024]{1,0:T(1,128)S(1)} %bitcast.80, bf16[4,256,1024]{2,1,0:T(8,128)(2,1)S(1)} %copy-done.23), custom_call_target="tpu_custom_call" | custom-call | flops 2147483648 | bytes 6291456 | tf_op jit(solution)/shard_map/column_spectra/pallas_call | solution.py:88
  21.3 5.1 %all-to-all-start = ((bf16[16,16,4096]{2,1,0:T(8,128)(2,1)}), bf16[16,16,4096]{2,1,0:T(8,128)(2,1)S(1)}, u32[]{:S(2)}, u32[]{:S(2)}) async-start(bf16[16,16,4096]{2,1,0:T(8,128)(2,1)} %bitcast.68), calls=%async_computation | async-start | bytes 4194304 | tf_op jit(solution)/shard_map/all_to_all | solution.py:447
  31.1 45.0 %collective-permute-done.2.refs_3_.refs_7_.refs_10_.refs_8_ = bf16[384,1024]{1,0:T(8,128)(2,1)} collective-permute-done((bf16[384,1024]{1,0:T(8,128)(2,1)}, bf16[384,1024]{1,0:T(8,128)(2,1)}, u32[]{:S(2)}, u32[]{:S(2)}) %collective-permute-start.2) | collective-permute-done | bytes 786464 | tf_op jit(solution)/shard_map/ppermute | solution.py:18
  83.7 24.9 %collective-permute-done.12.refs_12_ = f32[4,512]{1,0:T(4,128)S(1)} collective-permute-done((f32[4,512]{1,0:T(4,128)S(1)}, f32[4,512]{1,0:T(4,128)S(1)}, u32[]{:S(2)}, u32[]{:S(2)}) %collective-permute-start.12) | collective-permute-done | bytes 8224 | tf_op jit(solution)/shard_map/ppermute | solution.py:18
  109.2 2.4 collective-permute-start.4
  114.7 19.3 %collective-permute-done.4.refs_2_.refs_13_.refs_20_ = bf16[1024,384]{1,0:T(8,128)(2,1)} collective-permute-done((bf16[1024,384]{1,0:T(8,128)(2,1)}, bf16[1024,384]{1,0:T(8,128)(2,1)}, u32[]{:S(2)}, u32[]{:S(2)}) %collective-permute-start.4) | collective-permute-done | bytes 786464 | tf_op jit(solution)/shard_map/ppermute | solution.py:18
  136.1 14.8 %collective-permute-done.22.refs_17_.refs_24_ = bf16[384,1024]{1,0:T(8,128)(2,1)} collective-permute-done((bf16[384,1024]{1,0:T(8,128)(2,1)}, bf16[384,1024]{1,0:T(8,128)(2,1)}, u32[]{:S(2)}, u32[]{:S(2)}) %collective-permute-start.22) | collective-permute-done | bytes 786464 | tf_op jit(solution)/shard_map/ppermute | solution.py:18
  154.6 6.0 %mix_modes.1 = bf16[256,4096]{1,0:T(8,128)(2,1)S(1)} custom-call(bf16[256,4096]{1,0:T(8,128)(2,1)S(1)} %bitcast.67, bf16[2,512,256]{2,1,0:T(8,128)(2,1)S(1)} %copy-done.4, bf16[8,256,256]{2,1,0:T(8,128)(2,1)S(1)} %get-tuple-element.49.first, bf16[8,256,256]{2,1,0:T(8,128)(2,1)S(1)} %copy-done.2, f32[8,256]{1,0:T(8,128)S(1)} %gate.2.bias, ...), custom_call_target="tpu_custom_call" | custom-call | flops 4294967296 | bytes 6291456 | tf_op jit(solution)/shard_map/mix_modes/pallas_call | solution.py:139
  161.9 6.4 %all-to-all-start.1 = ((bf16[16,16,4096]{2,1,0:T(8,128)(2,1)}), bf16[16,16,4096]{2,1,0:T(8,128)(2,1)}, u32[]{:S(2)}, u32[]{:S(2)}) async-start(bf16[16,16,4096]{2,1,0:T(8,128)(2,1)} %bitcast.69), calls=%async_computation.1 | async-start | bytes 4194304 | tf_op jit(solution)/shard_map/all_to_all | solution.py:472
  171.2 38.3 %all-to-all-done.1 = bf16[16,16,4096]{2,1,0:T(8,128)(2,1)} async-done(((bf16[16,16,4096]{2,1,0:T(8,128)(2,1)}), bf16[16,16,4096]{2,1,0:T(8,128)(2,1)}, u32[]{:S(2)}, u32[]{:S(2)}) %all-to-all-start.1) | async-done | bytes 2097184 | tf_op jit(solution)/shard_map/all_to_all | solution.py:472
  212.7 6.2 %add_mixing.1 = (bf16[1024,1024]{1,0:T(8,128)(2,1)S(1)}, bf16[256,1024]{1,0:T(8,128)(2,1)S(1)}, bf16[256,1024]{1,0:T(8,128)(2,1)S(1)}, bf16[256,1024]{1,0:T(8,128)(2,1)S(1)}, bf16[256,1024]{1,0:T(8,128)(2,1)S(1)}) custom-call(bf16[256,4096]{1,0:T(8,128)(2,1)} %bitcast.15.spectra, bf16[4,1024,256]{2,1,0:T(8,128)(2,1)S(1)} %copy-done.22, ...), custom_call_target="tpu_custom_call" | custom-call | flops 2147483648 | bytes 10485760 | tf_op jit(solution)/shard_map/add_mixing/pallas_call | solution.py:193
  220.2 3.4 %collective-permute-start.29 = (bf16[256,1024]{1,0:T(8,128)(2,1)S(1)}, bf16[256,1024]{1,0:T(8,128)(2,1)S(1)}, u32[]{:S(2)}, u32[]{:S(2)}) collective-permute-start(bf16[256,1024]{1,0:T(8,128)(2,1)S(1)} %get-tuple-element.16.refs_1_), channel_id=1, source_target_pairs={{0,2},{2,0},{4,6},{6,4},{8,10},{10,8},{12,14},{14,12},{1,3},{3,1},... | collective-permute-start | bytes 1572872 | tf_op jit(solution)/shard_map/ppermute | solution.py:18
  223.6 5.7 %collective-permute-start.30 = (bf16[256,1024]{1,0:T(8,128)(2,1)S(1)}, bf16[256,1024]{1,0:T(8,128)(2,1)S(1)}, u32[]{:S(2)}, u32[]{:S(2)}) collective-permute-start(bf16[256,1024]{1,0:T(8,128)(2,1)S(1)} %get-tuple-element.18.refs_3_), channel_id=1, source_target_pairs={{0,4},{2,6},{4,0},{6,2},{8,12},{10,14},{12,8},{14,10},{1,5},{3,7},... | collective-permute-start | bytes 1572872 | tf_op jit(solution)/shard_map/ppermute | solution.py:18
  229.3 14.7 %experts.4.refs_4_ = f32[1024,1024]{1,0:T(8,128)S(1)} custom-call(f32[1024,2]{1,0:T(8,128)S(1)} %copy-done.5, bf16[256,1024]{1,0:T(8,128)(2,1)S(1)} %get-tuple-element.15.refs_0_, bf16[256,1024]{1,0:T(8,128)(2,1)S(1)} %get-tuple-element.16.refs_1_, bf16[256,1024]{1,0:T(8,128)(2,1)S(1)} %get-tuple-element.17.refs_2_, ...), custom_call_target="tpu_custom_call" | custom-call | flops 12884901888 | bytes 20971520 | tf_op jit(solution)/shard_map/experts/pallas_call | solution.py:341
  246.2 17.6 %experts.7 = (bf16[256,1024]{1,0:T(8,128)(2,1)S(1)}, bf16[256,1024]{1,0:T(8,128)(2,1)S(1)}) custom-call(f32[512,4]{1,0:T(8,128)S(1)} %copy-done.7, bf16[256,1024]{1,0:T(8,128)(2,1)S(1)} %collective-permute-done.29.refs_0_, bf16[256,1024]{1,0:T(8,128)(2,1)S(1)} %collective-permute-done.30.refs_1_, bf16[1024,1536]{1,0:T(8,128)(2,1)} %bitcast.70, ...), custom_call_target="tpu_custom_call" | custom-call | flops 12884901888 | bytes 29360128 | tf_op jit(solution)/shard_map/experts/pallas_call | solution.py:341
  265.8 2.0 collective-permute-start.33
  269.0 17.7 %experts.6 = (bf16[256,1024]{1,0:T(8,128)(2,1)S(1)}, bf16[256,1024]{1,0:T(8,128)(2,1)S(1)}) custom-call(f32[512,4]{1,0:T(8,128)S(1)} %copy.35.weights, bf16[256,1024]{1,0:T(8,128)(2,1)S(1)} %collective-permute-done.26.refs_0_, bf16[256,1024]{1,0:T(8,128)(2,1)S(1)} %collective-permute-done.27.refs_1_, bf16[1024,1536]{1,0:T(8,128)(2,1)} %bitcast.71, ...), custom_call_target="tpu_custom_call" | custom-call | flops 12884901888 | bytes 29360128 | tf_op jit(solution)/shard_map/experts/pallas_call | solution.py:341
  286.9 2.2 copy-done.25
  289.1 17.2 %experts.5.own = f32[1024,1024]{1,0:T(8,128)S(1)} custom-call(f32[1024,2]{1,0:T(8,128)S(1)} %copy-done.3, bf16[256,1024]{1,0:T(8,128)(2,1)S(1)} %get-tuple-element.15.refs_0_, bf16[256,1024]{1,0:T(8,128)(2,1)S(1)} %copy-done.16, bf16[256,1024]{1,0:T(8,128)(2,1)S(1)} %copy-done.18, bf16[256,1024]{1,0:T(8,128)(2,1)S(1)} %copy-done.20, ...), custom_call_target="tpu_custom_call" | custom-call | flops 12884901888 | bytes 20971520 | tf_op jit(solution)/shard_map/experts/pallas_call | solution.py:341
  306.3 2.5 add_outputs.1
  (151 shorter events, 42.0 us)
Async XLA Ops:
  2.9 75.1 %collective-permute-start.1 = (bf16[1024,384]{1,0:T(8,128)(2,1)}, bf16[1024,384]{1,0:T(8,128)(2,1)}, u32[]{:S(2)}, u32[]{:S(2)}) collective-permute-start(bf16[1024,384]{1,0:T(8,128)(2,1)} %dynamic-slice_bitcast_fusion.1), channel_id=1, source_target_pairs={{0,6},{2,4},{4,2},{6,0},{8,14},{10,12},{12,10},{14,8},{1,7},{3,5},... | collective-permute-start | bytes 2359304 | tf_op jit(solution)/shard_map/ppermute | solution.py:18
  6.9 101.7 %collective-permute-start = (bf16[1024,384]{1,0:T(8,128)(2,1)}, bf16[1024,384]{1,0:T(8,128)(2,1)}, u32[]{:S(2)}, u32[]{:S(2)}) collective-permute-start(bf16[1024,384]{1,0:T(8,128)(2,1)} %dynamic-slice_bitcast_fusion.1), channel_id=1, source_target_pairs={{0,8},{2,10},{4,12},{6,14},{8,0},{10,2},{12,4},{14,6},{1,9},{3,11}... | collective-permute-start | bytes 2359304 | tf_op jit(solution)/shard_map/ppermute | solution.py:18
  11.6 64.5 %collective-permute-start.2 = (bf16[384,1024]{1,0:T(8,128)(2,1)}, bf16[384,1024]{1,0:T(8,128)(2,1)}, u32[]{:S(2)}, u32[]{:S(2)}) collective-permute-start(bf16[384,1024]{1,0:T(8,128)(2,1)} %dynamic-slice_bitcast_fusion), channel_id=1, source_target_pairs={{0,6},{2,4},{4,2},{6,0},{8,14},{10,12},{12,10},{14,8},{1,7},{3,5},... | collective-permute-start | bytes 2359304 | tf_op jit(solution)/shard_map/ppermute | solution.py:18
  12.0 97.2 %collective-permute-start.3 = (bf16[384,1024]{1,0:T(8,128)(2,1)}, bf16[384,1024]{1,0:T(8,128)(2,1)}, u32[]{:S(2)}, u32[]{:S(2)}) collective-permute-start(bf16[384,1024]{1,0:T(8,128)(2,1)} %dynamic-slice_bitcast_fusion), channel_id=1, source_target_pairs={{0,8},{2,10},{4,12},{6,14},{8,0},{10,2},{12,4},{14,6},{1,9},{3,11}... | collective-permute-start | bytes 2359304 | tf_op jit(solution)/shard_map/ppermute | solution.py:18
  12.1 69.3 %collective-permute-start.11 = (f32[4,512]{1,0:T(4,128)S(1)}, f32[4,512]{1,0:T(4,128)S(1)}, u32[]{:S(2)}, u32[]{:S(2)}) collective-permute-start(f32[4,512]{1,0:T(4,128)S(1)} %get-tuple-element.36), channel_id=1, source_target_pairs={{0,2},{2,0},{4,6},{6,4},{8,10},{10,8},{12,14},{14,12},{1,3},{3,1},... | collective-permute-start | bytes 24584 | tf_op jit(solution)/shard_map/ppermute | solution.py:18
  21.3 130.0 %all-to-all-start = ((bf16[16,16,4096]{2,1,0:T(8,128)(2,1)}), bf16[16,16,4096]{2,1,0:T(8,128)(2,1)S(1)}, u32[]{:S(2)}, u32[]{:S(2)}) async-start(bf16[16,16,4096]{2,1,0:T(8,128)(2,1)} %bitcast.68), calls=%async_computation | async-start | bytes 4194304 | tf_op jit(solution)/shard_map/all_to_all | solution.py:447
  76.1 35.5 %collective-permute-start.8 = (bf16[384,1024]{1,0:T(8,128)(2,1)}, bf16[384,1024]{1,0:T(8,128)(2,1)}, u32[]{:S(2)}, u32[]{:S(2)}) collective-permute-start(bf16[384,1024]{1,0:T(8,128)(2,1)} %collective-permute-done.2.refs_3_.refs_7_.refs_10_.refs_8_), channel_id=1, source_target_pairs={{0,16},{16,0},{1,17},{17,1},{2,18},{18,2},{3,19},{19,3},{4,20},{20... | collective-permute-start | bytes 2359304 | tf_op jit(solution)/shard_map/ppermute | solution.py:18
  78.1 35.0 %collective-permute-start.5 = (bf16[1024,384]{1,0:T(8,128)(2,1)}, bf16[1024,384]{1,0:T(8,128)(2,1)}, u32[]{:S(2)}, u32[]{:S(2)}) collective-permute-start(bf16[1024,384]{1,0:T(8,128)(2,1)} %collective-permute-done.1.refs_2_.refs_3_.refs_6_.refs_4_), channel_id=1, source_target_pairs={{0,16},{16,0},{1,17},{17,1},{2,18},{18,2},{3,19},{19,3},{4,20},{20... | collective-permute-start | bytes 2359304 | tf_op jit(solution)/shard_map/ppermute | solution.py:18
  81.4 27.3 %collective-permute-start.12 = (f32[4,512]{1,0:T(4,128)S(1)}, f32[4,512]{1,0:T(4,128)S(1)}, u32[]{:S(2)}, u32[]{:S(2)}) collective-permute-start(f32[4,512]{1,0:T(4,128)S(1)} %get-tuple-element.35), channel_id=1, source_target_pairs={{0,4},{2,6},{4,0},{6,2},{8,12},{10,14},{12,8},{14,10},{1,5},{3,7},... | collective-permute-start | bytes 24584 | tf_op jit(solution)/shard_map/ppermute | solution.py:18
  108.7 26.9 %collective-permute-start.6 = (bf16[1024,384]{1,0:T(8,128)(2,1)}, bf16[1024,384]{1,0:T(8,128)(2,1)}, u32[]{:S(2)}, u32[]{:S(2)}) collective-permute-start(bf16[1024,384]{1,0:T(8,128)(2,1)} %collective-permute-done.1.refs_2_.refs_3_.refs_6_.refs_4_), channel_id=1, source_target_pairs={{0,1},{1,0},{2,3},{3,2},{4,5},{5,4},{6,7},{7,6},{8,9},{9,8},{10,11... | collective-permute-start | bytes 2359304 | tf_op jit(solution)/shard_map/ppermute | solution.py:18
  111.6 39.3 %collective-permute-start.13 = (bf16[1024,384]{1,0:T(8,128)(2,1)}, bf16[1024,384]{1,0:T(8,128)(2,1)}, u32[]{:S(2)}, u32[]{:S(2)}) collective-permute-start(bf16[1024,384]{1,0:T(8,128)(2,1)} %collective-permute-done.refs_1_.refs_5_.refs_12_), channel_id=1, source_target_pairs={{0,16},{16,0},{1,17},{17,1},{2,18},{18,2},{3,19},{19,3},{4,20},{20... | collective-permute-start | bytes 2359304 | tf_op jit(solution)/shard_map/ppermute | solution.py:18
  113.1 37.7 %collective-permute-start.22 = (bf16[384,1024]{1,0:T(8,128)(2,1)}, bf16[384,1024]{1,0:T(8,128)(2,1)}, u32[]{:S(2)}, u32[]{:S(2)}) collective-permute-start(bf16[384,1024]{1,0:T(8,128)(2,1)} %collective-permute-done.3.refs_1_.refs_9_.refs_16_), channel_id=1, source_target_pairs={{0,6},{2,4},{4,2},{6,0},{8,14},{10,12},{12,10},{14,8},{1,7},{3,5},... | collective-permute-start | bytes 2359304 | tf_op jit(solution)/shard_map/ppermute | solution.py:18
  134.0 34.3 %collective-permute-start.16 = (bf16[384,1024]{1,0:T(8,128)(2,1)}, bf16[384,1024]{1,0:T(8,128)(2,1)}, u32[]{:S(2)}, u32[]{:S(2)}) collective-permute-start(bf16[384,1024]{1,0:T(8,128)(2,1)} %collective-permute-done.3.refs_1_.refs_9_.refs_16_), channel_id=1, source_target_pairs={{0,16},{16,0},{1,17},{17,1},{2,18},{18,2},{3,19},{19,3},{4,20},{20... | collective-permute-start | bytes 2359304 | tf_op jit(solution)/shard_map/ppermute | solution.py:18
  135.5 34.4 %collective-permute-start.14 = (bf16[1024,384]{1,0:T(8,128)(2,1)}, bf16[1024,384]{1,0:T(8,128)(2,1)}, u32[]{:S(2)}, u32[]{:S(2)}) collective-permute-start(bf16[1024,384]{1,0:T(8,128)(2,1)} %collective-permute-done.refs_1_.refs_5_.refs_12_), channel_id=1, source_target_pairs={{0,1},{1,0},{2,3},{3,2},{4,5},{5,4},{6,7},{7,6},{8,9},{9,8},{10,11... | collective-permute-start | bytes 2359304 | tf_op jit(solution)/shard_map/ppermute | solution.py:18
  135.6 34.6 %collective-permute-start.17 = (bf16[384,1024]{1,0:T(8,128)(2,1)}, bf16[384,1024]{1,0:T(8,128)(2,1)}, u32[]{:S(2)}, u32[]{:S(2)}) collective-permute-start(bf16[384,1024]{1,0:T(8,128)(2,1)} %collective-permute-done.3.refs_1_.refs_9_.refs_16_), channel_id=1, source_target_pairs={{0,1},{1,0},{2,3},{3,2},{4,5},{5,4},{6,7},{7,6},{8,9},{9,8},{10,11... | collective-permute-start | bytes 2359304 | tf_op jit(solution)/shard_map/ppermute | solution.py:18
  161.9 47.5 %all-to-all-start.1 = ((bf16[16,16,4096]{2,1,0:T(8,128)(2,1)}), bf16[16,16,4096]{2,1,0:T(8,128)(2,1)}, u32[]{:S(2)}, u32[]{:S(2)}) async-start(bf16[16,16,4096]{2,1,0:T(8,128)(2,1)} %bitcast.69), calls=%async_computation.1 | async-start | bytes 4194304 | tf_op jit(solution)/shard_map/all_to_all | solution.py:472
  168.3 50.5 %collective-permute-start.19 = (bf16[1024,384]{1,0:T(8,128)(2,1)}, bf16[1024,384]{1,0:T(8,128)(2,1)}, u32[]{:S(2)}, u32[]{:S(2)}) collective-permute-start(bf16[1024,384]{1,0:T(8,128)(2,1)} %collective-permute-done.4.refs_2_.refs_13_.refs_20_), channel_id=1, source_target_pairs={{0,16},{16,0},{1,17},{17,1},{2,18},{18,2},{3,19},{19,3},{4,20},{20... | collective-permute-start | bytes 2359304 | tf_op jit(solution)/shard_map/ppermute | solution.py:18
  169.9 49.9 %collective-permute-start.20 = (bf16[1024,384]{1,0:T(8,128)(2,1)}, bf16[1024,384]{1,0:T(8,128)(2,1)}, u32[]{:S(2)}, u32[]{:S(2)}) collective-permute-start(bf16[1024,384]{1,0:T(8,128)(2,1)} %collective-permute-done.4.refs_2_.refs_13_.refs_20_), channel_id=1, source_target_pairs={{0,1},{1,0},{2,3},{3,2},{4,5},{5,4},{6,7},{7,6},{8,9},{9,8},{10,11... | collective-permute-start | bytes 2359304 | tf_op jit(solution)/shard_map/ppermute | solution.py:18
  170.1 49.6 %collective-permute-start.23 = (bf16[384,1024]{1,0:T(8,128)(2,1)}, bf16[384,1024]{1,0:T(8,128)(2,1)}, u32[]{:S(2)}, u32[]{:S(2)}) collective-permute-start(bf16[384,1024]{1,0:T(8,128)(2,1)} %collective-permute-done.22.refs_17_.refs_24_), channel_id=1, source_target_pairs={{0,16},{16,0},{1,17},{17,1},{2,18},{18,2},{3,19},{19,3},{4,20},{20... | collective-permute-start | bytes 2359304 | tf_op jit(solution)/shard_map/ppermute | solution.py:18
  170.7 49.6 %collective-permute-start.24 = (bf16[384,1024]{1,0:T(8,128)(2,1)}, bf16[384,1024]{1,0:T(8,128)(2,1)}, u32[]{:S(2)}, u32[]{:S(2)}) collective-permute-start(bf16[384,1024]{1,0:T(8,128)(2,1)} %collective-permute-done.22.refs_17_.refs_24_), channel_id=1, source_target_pairs={{0,1},{1,0},{2,3},{3,2},{4,5},{5,4},{6,7},{7,6},{8,9},{9,8},{10,11... | collective-permute-start | bytes 2359304 | tf_op jit(solution)/shard_map/ppermute | solution.py:18
  170.7 52.9 %collective-permute-start.15 = (bf16[1024,384]{1,0:T(8,128)(2,1)}, bf16[1024,384]{1,0:T(8,128)(2,1)}, u32[]{:S(2)}, u32[]{:S(2)}) collective-permute-start(bf16[1024,384]{1,0:T(8,128)(2,1)} %collective-permute-done.13.refs_6_.refs_13_), channel_id=1, source_target_pairs={{0,1},{1,0},{2,3},{3,2},{4,5},{5,4},{6,7},{7,6},{8,9},{9,8},{10,11... | collective-permute-start | bytes 2359304 | tf_op jit(solution)/shard_map/ppermute | solution.py:18
  218.9 27.2 %collective-permute-start.18 = (bf16[384,1024]{1,0:T(8,128)(2,1)}, bf16[384,1024]{1,0:T(8,128)(2,1)S(1)}, u32[]{:S(2)}, u32[]{:S(2)}) collective-permute-start(bf16[384,1024]{1,0:T(8,128)(2,1)} %collective-permute-done.16.refs_10_.refs_17_), channel_id=1, source_target_pairs={{0,1},{1,0},{2,3},{3,2},{4,5},{5,4},{6,7},{7,6},{8,9},{9,8},{10,11... | collective-permute-start | bytes 2359304 | tf_op jit(solution)/shard_map/ppermute | solution.py:18
  263.8 42.5 %collective-permute-start.31 = (bf16[256,1024]{1,0:T(8,128)(2,1)S(1)}, bf16[256,1024]{1,0:T(8,128)(2,1)S(1)}, u32[]{:S(2)}, u32[]{:S(2)}) collective-permute-start(bf16[256,1024]{1,0:T(8,128)(2,1)S(1)} %get-tuple-element.20), channel_id=1, source_target_pairs={{0,2},{2,0},{4,6},{6,4},{8,10},{10,8},{12,14},{14,12},{1,3},{3,1},... | collective-permute-start | bytes 1572872 | tf_op jit(solution)/shard_map/ppermute | solution.py:18
  265.8 40.5 %collective-permute-start.33 = (bf16[256,1024]{1,0:T(8,128)(2,1)S(1)}, bf16[256,1024]{1,0:T(8,128)(2,1)S(1)}, u32[]{:S(2)}, u32[]{:S(2)}) collective-permute-start(bf16[256,1024]{1,0:T(8,128)(2,1)S(1)} %get-tuple-element.22), channel_id=1, source_target_pairs={{0,4},{2,6},{4,0},{6,2},{8,12},{10,14},{12,8},{14,10},{1,5},{3,7},... | collective-permute-start | bytes 1572872 | tf_op jit(solution)/shard_map/ppermute | solution.py:18
  (44 other events, 658.7 us)

commit v5 on v4

--- a/solution.py
+++ b/solution.py
@@ -488,7 +488,7 @@
     per_row = len(norms) // 2
     rows_of = [1] * per_row + [2] * per_row
     others = [exchange(norm, "row", mask) for norm, mask in zip(norms, rows_of)]
-    far_near_down = exchange(far_down, "row", 3)
+    far_near_down = exchange(tie(far_down, mixed), "row", 3)
     far_all = Weights.spread((far_up, far_down))
     far_near_all = Weights.spread((far_near_up, far_near_down))
     expert = lax.axis_index("row") // 2

time: 315 us -> 305 us (0.968)
  starting transfers between devices: 47.7 us -> 40.6 us
  waiting for transfers between devices: 142 us -> 136 us
  local copies, waits for them, and re-layouts: 24.2 us -> 28.9 us
    all_to_all x1, waiting for transfers between devices: 38.3 us -> 21.8 us  [per_device(): lax.all_to_all(mixed.reshape(n_dev, -1, mixed.shape[1]), axes, split_axis...]
    ppermute x34, waiting for transfers between devices: 104 us -> 115 us  [exchange(): return lax.ppermute(value, axis, pairs)]
    ppermute x34, starting transfers between devices: 36.2 us -> 30.4 us  [exchange(): return lax.ppermute(value, axis, pairs)]
    unnamed x66 -> x88, local copies, waits for them, and re-layouts: 16.9 us -> 22.1 us
  transfers between devices with their start and end apart: 36 -> 36, of which waited for: 5 -> 6; matrix products, arithmetic and copies ran while one was open for 4% -> 4% of each run, Pallas kernels for 27% -> 28%
where the time goes in v5:
time: 305 us; the launch traced here: 299 us
  waiting for transfers between devices  136 us (45%)
  Pallas kernels  85.8 us (28%)
  starting transfers between devices  40.6 us (13%)
  local copies, waits for them, and re-layouts  28.9 us (9%)
  other arithmetic  6.24 us (2%)
    ppermute x34, waiting for transfers between devices, exchange(): return lax.ppermute(value, axis, pairs)  115 us
    pallas_call x4, Pallas kernels, run_experts(): pl.pallas_call(functools.partial(experts_kernel, counts, len(sets), len(o...  67.1 us
    ppermute x34, starting transfers between devices, exchange(): return lax.ppermute(value, axis, pairs)  30.4 us
    unnamed x88, local copies, waits for them, and re-layouts  22.1 us
    all_to_all x1, waiting for transfers between devices, per_device(): lax.all_to_all(mixed.reshape(n_dev, -1, mixed.shape[1]), axes, split_axis...  21.8 us
    pallas_call x1, Pallas kernels, add_mixing(): pl.pallas_call(residual_kernel, grid=(steps,), out_shape=[jax.ShapeDtypeS...  6.18 us
  transfers between devices with their start and end apart: 36, of which 6 were waited for; matrix products, arithmetic and copies ran while one was open for 4% of the time, Pallas kernels for 28%

profile of v5, /device:TPU:0, one launch (start us, length us, event | category | flops | bytes accessed | tf_op | source)
XLA Modules:
  0.0 299.0 jit_solution(6849845473443912738)
XLA Ops:
  0.8 2.2 dynamic-slice_bitcast_fusion.1
  3.0 4.0 %collective-permute-start.1 = (bf16[1024,384]{1,0:T(8,128)(2,1)}, bf16[1024,384]{1,0:T(8,128)(2,1)}, u32[]{:S(2)}, u32[]{:S(2)}) collective-permute-start(bf16[1024,384]{1,0:T(8,128)(2,1)} %dynamic-slice_bitcast_fusion.1), channel_id=1, source_target_pairs={{0,6},{2,4},{4,2},{6,0},{8,14},{10,12},{12,10},{14,8},{1,7},{3,5},... | collective-permute-start | bytes 2359304 | tf_op jit(solution)/shard_map/ppermute | solution.py:18
  7.0 2.6 collective-permute-start
  9.6 2.2 dynamic-slice_bitcast_fusion
  15.8 4.4 %column_spectra.1 = bf16[256,4096]{1,0:T(8,128)(2,1)S(1)} custom-call(bf16[1024,1024]{1,0:T(8,128)(2,1)S(1)} %bitcast.78, f32[1,1024]{1,0:T(1,128)S(1)} %bitcast.80, bf16[4,256,1024]{2,1,0:T(8,128)(2,1)S(1)} %copy-done.34), custom_call_target="tpu_custom_call" | custom-call | flops 2147483648 | bytes 6291456 | tf_op jit(solution)/shard_map/column_spectra/pallas_call | solution.py:88
  21.4 5.1 %all-to-all-start = ((bf16[16,16,4096]{2,1,0:T(8,128)(2,1)}), bf16[16,16,4096]{2,1,0:T(8,128)(2,1)S(1)}, u32[]{:S(2)}, u32[]{:S(2)}) async-start(bf16[16,16,4096]{2,1,0:T(8,128)(2,1)} %bitcast.68), calls=%async_computation | async-start | bytes 4194304 | tf_op jit(solution)/shard_map/all_to_all | solution.py:447
  30.6 45.6 %collective-permute-done.2.refs_3_.refs_7_.refs_10_.refs_8_ = bf16[384,1024]{1,0:T(8,128)(2,1)} collective-permute-done((bf16[384,1024]{1,0:T(8,128)(2,1)}, bf16[384,1024]{1,0:T(8,128)(2,1)}, u32[]{:S(2)}, u32[]{:S(2)}) %collective-permute-start.2) | collective-permute-done | bytes 786464 | tf_op jit(solution)/shard_map/ppermute | solution.py:18
  82.9 25.8 %collective-permute-done.12.refs_12_ = f32[4,512]{1,0:T(4,128)S(1)} collective-permute-done((f32[4,512]{1,0:T(4,128)S(1)}, f32[4,512]{1,0:T(4,128)S(1)}, u32[]{:S(2)}, u32[]{:S(2)}) %collective-permute-start.12) | collective-permute-done | bytes 8224 | tf_op jit(solution)/shard_map/ppermute | solution.py:18
  109.2 2.4 collective-permute-start.4
  117.0 5.8 %mix_modes.1 = bf16[256,4096]{1,0:T(8,128)(2,1)S(1)} custom-call(bf16[256,4096]{1,0:T(8,128)(2,1)S(1)} %bitcast.67, bf16[2,512,256]{2,1,0:T(8,128)(2,1)S(1)} %copy-done.5, bf16[8,256,256]{2,1,0:T(8,128)(2,1)S(1)} %get-tuple-element.51.first, bf16[8,256,256]{2,1,0:T(8,128)(2,1)S(1)} %copy-done.2, f32[8,256]{1,0:T(8,128)S(1)} %gate.2.bias, ...), custom_call_target="tpu_custom_call" | custom-call | flops 4294967296 | bytes 6291456 | tf_op jit(solution)/shard_map/mix_modes/pallas_call | solution.py:139
  124.2 9.9 %collective-permute-done.4.refs_2_.refs_13_.refs_20_ = bf16[1024,384]{1,0:T(8,128)(2,1)} collective-permute-done((bf16[1024,384]{1,0:T(8,128)(2,1)}, bf16[1024,384]{1,0:T(8,128)(2,1)}, u32[]{:S(2)}, u32[]{:S(2)}) %collective-permute-start.4) | collective-permute-done | bytes 786464 | tf_op jit(solution)/shard_map/ppermute | solution.py:18
  135.1 13.0 %collective-permute-done.16.refs_10_.refs_17_ = bf16[384,1024]{1,0:T(8,128)(2,1)} collective-permute-done((bf16[384,1024]{1,0:T(8,128)(2,1)}, bf16[384,1024]{1,0:T(8,128)(2,1)}, u32[]{:S(2)}, u32[]{:S(2)}) %collective-permute-start.16) | collective-permute-done | bytes 786464 | tf_op jit(solution)/shard_map/ppermute | solution.py:18
  149.0 5.1 %all-to-all-start.1 = ((bf16[16,16,4096]{2,1,0:T(8,128)(2,1)}), bf16[16,16,4096]{2,1,0:T(8,128)(2,1)}, u32[]{:S(2)}, u32[]{:S(2)}) async-start(bf16[16,16,4096]{2,1,0:T(8,128)(2,1)} %bitcast.69), calls=%async_computation.1 | async-start | bytes 4194304 | tf_op jit(solution)/shard_map/all_to_all | solution.py:472
  158.1 20.1 %collective-permute-done.22.refs_17_.refs_24_ = bf16[384,1024]{1,0:T(8,128)(2,1)} collective-permute-done((bf16[384,1024]{1,0:T(8,128)(2,1)}, bf16[384,1024]{1,0:T(8,128)(2,1)}, u32[]{:S(2)}, u32[]{:S(2)}) %collective-permute-start.22) | collective-permute-done | bytes 786464 | tf_op jit(solution)/shard_map/ppermute | solution.py:18
  180.9 21.8 %all-to-all-done.1 = bf16[16,16,4096]{2,1,0:T(8,128)(2,1)} async-done(((bf16[16,16,4096]{2,1,0:T(8,128)(2,1)}), bf16[16,16,4096]{2,1,0:T(8,128)(2,1)}, u32[]{:S(2)}, u32[]{:S(2)}) %all-to-all-start.1) | async-done | bytes 2097184 | tf_op jit(solution)/shard_map/all_to_all | solution.py:472
  205.9 6.2 %add_mixing.1 = (bf16[1024,1024]{1,0:T(8,128)(2,1)S(1)}, bf16[256,1024]{1,0:T(8,128)(2,1)S(1)}, bf16[256,1024]{1,0:T(8,128)(2,1)S(1)}, bf16[256,1024]{1,0:T(8,128)(2,1)S(1)}, bf16[256,1024]{1,0:T(8,128)(2,1)S(1)}) custom-call(bf16[256,4096]{1,0:T(8,128)(2,1)} %bitcast.15.spectra, bf16[4,1024,256]{2,1,0:T(8,128)(2,1)S(1)} %copy-done.33, ...), custom_call_target="tpu_custom_call" | custom-call | flops 2147483648 | bytes 10485760 | tf_op jit(solution)/shard_map/add_mixing/pallas_call | solution.py:193
  212.8 2.9 collective-permute-start.30
  215.7 14.6 %experts.4.refs_4_ = f32[1024,1024]{1,0:T(8,128)S(1)} custom-call(f32[1024,2]{1,0:T(8,128)S(1)} %copy-done.4, bf16[256,1024]{1,0:T(8,128)(2,1)S(1)} %get-tuple-element.16.refs_0_, bf16[256,1024]{1,0:T(8,128)(2,1)S(1)} %get-tuple-element.17.refs_1_, bf16[256,1024]{1,0:T(8,128)(2,1)S(1)} %get-tuple-element.18.refs_2_, ...), custom_call_target="tpu_custom_call" | custom-call | flops 12884901888 | bytes 20971520 | tf_op jit(solution)/shard_map/experts/pallas_call | solution.py:341
  230.4 2.0 copy-done.35
  233.7 17.8 %experts.7 = (bf16[256,1024]{1,0:T(8,128)(2,1)S(1)}, bf16[256,1024]{1,0:T(8,128)(2,1)S(1)}) custom-call(f32[512,4]{1,0:T(8,128)S(1)} %copy.36.weights, bf16[256,1024]{1,0:T(8,128)(2,1)S(1)} %collective-permute-done.29.refs_0_, bf16[256,1024]{1,0:T(8,128)(2,1)S(1)} %collective-permute-done.30.refs_1_, bf16[1024,1536]{1,0:T(8,128)(2,1)} %bitcast.70, ...), custom_call_target="tpu_custom_call" | custom-call | flops 12884901888 | bytes 29360128 | tf_op jit(solution)/shard_map/experts/pallas_call | solution.py:341
  258.0 17.8 %experts.6 = (bf16[256,1024]{1,0:T(8,128)(2,1)S(1)}, bf16[256,1024]{1,0:T(8,128)(2,1)S(1)}) custom-call(f32[512,4]{1,0:T(8,128)S(1)} %copy.35.weights, bf16[256,1024]{1,0:T(8,128)(2,1)S(1)} %collective-permute-done.26.refs_0_, bf16[256,1024]{1,0:T(8,128)(2,1)S(1)} %collective-permute-done.27.refs_1_, bf16[1024,1536]{1,0:T(8,128)(2,1)} %bitcast.71, ...), custom_call_target="tpu_custom_call" | custom-call | flops 12884901888 | bytes 29360128 | tf_op jit(solution)/shard_map/experts/pallas_call | solution.py:341
  277.0 2.2 copy-done.36
  279.2 16.8 %experts.5.own = f32[1024,1024]{1,0:T(8,128)S(1)} custom-call(f32[1024,2]{1,0:T(8,128)S(1)} %copy-done.3, bf16[256,1024]{1,0:T(8,128)(2,1)S(1)} %get-tuple-element.16.refs_0_, bf16[256,1024]{1,0:T(8,128)(2,1)S(1)} %copy-done.27, bf16[256,1024]{1,0:T(8,128)(2,1)S(1)} %copy-done.29, bf16[256,1024]{1,0:T(8,128)(2,1)S(1)} %copy-done.31, ...), custom_call_target="tpu_custom_call" | custom-call | flops 12884901888 | bytes 20971520 | tf_op jit(solution)/shard_map/experts/pallas_call | solution.py:341
  296.1 2.3 add_outputs.1
  (173 shorter events, 45.3 us)
Async XLA Ops:
  3.0 75.1 %collective-permute-start.1 = (bf16[1024,384]{1,0:T(8,128)(2,1)}, bf16[1024,384]{1,0:T(8,128)(2,1)}, u32[]{:S(2)}, u32[]{:S(2)}) collective-permute-start(bf16[1024,384]{1,0:T(8,128)(2,1)} %dynamic-slice_bitcast_fusion.1), channel_id=1, source_target_pairs={{0,6},{2,4},{4,2},{6,0},{8,14},{10,12},{12,10},{14,8},{1,7},{3,5},... | collective-permute-start | bytes 2359304 | tf_op jit(solution)/shard_map/ppermute | solution.py:18
  7.0 101.7 %collective-permute-start = (bf16[1024,384]{1,0:T(8,128)(2,1)}, bf16[1024,384]{1,0:T(8,128)(2,1)}, u32[]{:S(2)}, u32[]{:S(2)}) collective-permute-start(bf16[1024,384]{1,0:T(8,128)(2,1)} %dynamic-slice_bitcast_fusion.1), channel_id=1, source_target_pairs={{0,8},{2,10},{4,12},{6,14},{8,0},{10,2},{12,4},{14,6},{1,9},{3,11}... | collective-permute-start | bytes 2359304 | tf_op jit(solution)/shard_map/ppermute | solution.py:18
  11.7 64.4 %collective-permute-start.2 = (bf16[384,1024]{1,0:T(8,128)(2,1)}, bf16[384,1024]{1,0:T(8,128)(2,1)}, u32[]{:S(2)}, u32[]{:S(2)}) collective-permute-start(bf16[384,1024]{1,0:T(8,128)(2,1)} %dynamic-slice_bitcast_fusion), channel_id=1, source_target_pairs={{0,6},{2,4},{4,2},{6,0},{8,14},{10,12},{12,10},{14,8},{1,7},{3,5},... | collective-permute-start | bytes 2359304 | tf_op jit(solution)/shard_map/ppermute | solution.py:18
  12.1 97.1 %collective-permute-start.3 = (bf16[384,1024]{1,0:T(8,128)(2,1)}, bf16[384,1024]{1,0:T(8,128)(2,1)}, u32[]{:S(2)}, u32[]{:S(2)}) collective-permute-start(bf16[384,1024]{1,0:T(8,128)(2,1)} %dynamic-slice_bitcast_fusion), channel_id=1, source_target_pairs={{0,8},{2,10},{4,12},{6,14},{8,0},{10,2},{12,4},{14,6},{1,9},{3,11}... | collective-permute-start | bytes 2359304 | tf_op jit(solution)/shard_map/ppermute | solution.py:18
  12.2 68.2 %collective-permute-start.11 = (f32[4,512]{1,0:T(4,128)S(1)}, f32[4,512]{1,0:T(4,128)S(1)}, u32[]{:S(2)}, u32[]{:S(2)}) collective-permute-start(f32[4,512]{1,0:T(4,128)S(1)} %get-tuple-element.38), channel_id=1, source_target_pairs={{0,2},{2,0},{4,6},{6,4},{8,10},{10,8},{12,14},{14,12},{1,3},{3,1},... | collective-permute-start | bytes 24584 | tf_op jit(solution)/shard_map/ppermute | solution.py:18
  21.4 92.2 %all-to-all-start = ((bf16[16,16,4096]{2,1,0:T(8,128)(2,1)}), bf16[16,16,4096]{2,1,0:T(8,128)(2,1)S(1)}, u32[]{:S(2)}, u32[]{:S(2)}) async-start(bf16[16,16,4096]{2,1,0:T(8,128)(2,1)} %bitcast.68), calls=%async_computation | async-start | bytes 4194304 | tf_op jit(solution)/shard_map/all_to_all | solution.py:447
  76.2 35.5 %collective-permute-start.8 = (bf16[384,1024]{1,0:T(8,128)(2,1)}, bf16[384,1024]{1,0:T(8,128)(2,1)}, u32[]{:S(2)}, u32[]{:S(2)}) collective-permute-start(bf16[384,1024]{1,0:T(8,128)(2,1)} %collective-permute-done.2.refs_3_.refs_7_.refs_10_.refs_8_), channel_id=1, source_target_pairs={{0,16},{16,0},{1,17},{17,1},{2,18},{18,2},{3,19},{19,3},{4,20},{20... | collective-permute-start | bytes 2359304 | tf_op jit(solution)/shard_map/ppermute | solution.py:18
  78.1 35.0 %collective-permute-start.5 = (bf16[1024,384]{1,0:T(8,128)(2,1)}, bf16[1024,384]{1,0:T(8,128)(2,1)}, u32[]{:S(2)}, u32[]{:S(2)}) collective-permute-start(bf16[1024,384]{1,0:T(8,128)(2,1)} %collective-permute-done.1.refs_2_.refs_3_.refs_6_.refs_4_), channel_id=1, source_target_pairs={{0,16},{16,0},{1,17},{17,1},{2,18},{18,2},{3,19},{19,3},{4,20},{20... | collective-permute-start | bytes 2359304 | tf_op jit(solution)/shard_map/ppermute | solution.py:18
  80.5 28.2 %collective-permute-start.12 = (f32[4,512]{1,0:T(4,128)S(1)}, f32[4,512]{1,0:T(4,128)S(1)}, u32[]{:S(2)}, u32[]{:S(2)}) collective-permute-start(f32[4,512]{1,0:T(4,128)S(1)} %get-tuple-element.37), channel_id=1, source_target_pairs={{0,4},{2,6},{4,0},{6,2},{8,12},{10,14},{12,8},{14,10},{1,5},{3,7},... | collective-permute-start | bytes 24584 | tf_op jit(solution)/shard_map/ppermute | solution.py:18
  108.7 25.3 %collective-permute-start.6 = (bf16[1024,384]{1,0:T(8,128)(2,1)}, bf16[1024,384]{1,0:T(8,128)(2,1)}, u32[]{:S(2)}, u32[]{:S(2)}) collective-permute-start(bf16[1024,384]{1,0:T(8,128)(2,1)} %collective-permute-done.1.refs_2_.refs_3_.refs_6_.refs_4_), channel_id=1, source_target_pairs={{0,1},{1,0},{2,3},{3,2},{4,5},{5,4},{6,7},{7,6},{8,9},{9,8},{10,11... | collective-permute-start | bytes 2359304 | tf_op jit(solution)/shard_map/ppermute | solution.py:18
  108.7 25.8 %collective-permute-start.9 = (bf16[384,1024]{1,0:T(8,128)(2,1)}, bf16[384,1024]{1,0:T(8,128)(2,1)}, u32[]{:S(2)}, u32[]{:S(2)}) collective-permute-start(bf16[384,1024]{1,0:T(8,128)(2,1)} %collective-permute-done.2.refs_3_.refs_7_.refs_10_.refs_8_), channel_id=1, source_target_pairs={{0,1},{1,0},{2,3},{3,2},{4,5},{5,4},{6,7},{7,6},{8,9},{9,8},{10,11... | collective-permute-start | bytes 2359304 | tf_op jit(solution)/shard_map/ppermute | solution.py:18
  109.2 24.8 %collective-permute-start.4 = (bf16[1024,384]{1,0:T(8,128)(2,1)}, bf16[1024,384]{1,0:T(8,128)(2,1)}, u32[]{:S(2)}, u32[]{:S(2)}) collective-permute-start(bf16[1024,384]{1,0:T(8,128)(2,1)} %collective-permute-done.refs_1_.refs_5_.refs_12_), channel_id=1, source_target_pairs={{0,6},{2,4},{4,2},{6,0},{8,14},{10,12},{12,10},{14,8},{1,7},{3,5},... | collective-permute-start | bytes 2359304 | tf_op jit(solution)/shard_map/ppermute | solution.py:18
  111.7 23.0 %collective-permute-start.13 = (bf16[1024,384]{1,0:T(8,128)(2,1)}, bf16[1024,384]{1,0:T(8,128)(2,1)}, u32[]{:S(2)}, u32[]{:S(2)}) collective-permute-start(bf16[1024,384]{1,0:T(8,128)(2,1)} %collective-permute-done.refs_1_.refs_5_.refs_12_), channel_id=1, source_target_pairs={{0,16},{16,0},{1,17},{17,1},{2,18},{18,2},{3,19},{19,3},{4,20},{20... | collective-permute-start | bytes 2359304 | tf_op jit(solution)/shard_map/ppermute | solution.py:18
  113.2 34.9 %collective-permute-start.16 = (bf16[384,1024]{1,0:T(8,128)(2,1)}, bf16[384,1024]{1,0:T(8,128)(2,1)}, u32[]{:S(2)}, u32[]{:S(2)}) collective-permute-start(bf16[384,1024]{1,0:T(8,128)(2,1)} %collective-permute-done.3.refs_1_.refs_9_.refs_16_), channel_id=1, source_target_pairs={{0,16},{16,0},{1,17},{17,1},{2,18},{18,2},{3,19},{19,3},{4,20},{20... | collective-permute-start | bytes 2359304 | tf_op jit(solution)/shard_map/ppermute | solution.py:18
  134.6 23.3 %collective-permute-start.7 = (bf16[1024,384]{1,0:T(8,128)(2,1)}, bf16[1024,384]{1,0:T(8,128)(2,1)}, u32[]{:S(2)}, u32[]{:S(2)}) collective-permute-start(bf16[1024,384]{1,0:T(8,128)(2,1)} %collective-permute-done.5.refs_4_.refs_7_.refs_5_), channel_id=1, source_target_pairs={{0,1},{1,0},{2,3},{3,2},{4,5},{5,4},{6,7},{7,6},{8,9},{9,8},{10,11... | collective-permute-start | bytes 2359304 | tf_op jit(solution)/shard_map/ppermute | solution.py:18
  148.1 30.2 %collective-permute-start.22 = (bf16[384,1024]{1,0:T(8,128)(2,1)}, bf16[384,1024]{1,0:T(8,128)(2,1)}, u32[]{:S(2)}, u32[]{:S(2)}) collective-permute-start(bf16[384,1024]{1,0:T(8,128)(2,1)} %collective-permute-done.3.refs_1_.refs_9_.refs_16_), channel_id=1, source_target_pairs={{0,6},{2,4},{4,2},{6,0},{8,14},{10,12},{12,10},{14,8},{1,7},{3,5},... | collective-permute-start | bytes 2359304 | tf_op jit(solution)/shard_map/ppermute | solution.py:18
  149.0 53.7 %all-to-all-start.1 = ((bf16[16,16,4096]{2,1,0:T(8,128)(2,1)}), bf16[16,16,4096]{2,1,0:T(8,128)(2,1)}, u32[]{:S(2)}, u32[]{:S(2)}) async-start(bf16[16,16,4096]{2,1,0:T(8,128)(2,1)} %bitcast.69), calls=%async_computation.1 | async-start | bytes 4194304 | tf_op jit(solution)/shard_map/all_to_all | solution.py:472
  154.1 58.0 %collective-permute-start.19 = (bf16[1024,384]{1,0:T(8,128)(2,1)}, bf16[1024,384]{1,0:T(8,128)(2,1)}, u32[]{:S(2)}, u32[]{:S(2)}) collective-permute-start(bf16[1024,384]{1,0:T(8,128)(2,1)} %collective-permute-done.4.refs_2_.refs_13_.refs_20_), channel_id=1, source_target_pairs={{0,16},{16,0},{1,17},{17,1},{2,18},{18,2},{3,19},{19,3},{4,20},{20... | collective-permute-start | bytes 2359304 | tf_op jit(solution)/shard_map/ppermute | solution.py:18
  156.5 55.7 %collective-permute-start.20 = (bf16[1024,384]{1,0:T(8,128)(2,1)}, bf16[1024,384]{1,0:T(8,128)(2,1)}, u32[]{:S(2)}, u32[]{:S(2)}) collective-permute-start(bf16[1024,384]{1,0:T(8,128)(2,1)} %collective-permute-done.4.refs_2_.refs_13_.refs_20_), channel_id=1, source_target_pairs={{0,1},{1,0},{2,3},{3,2},{4,5},{5,4},{6,7},{7,6},{8,9},{9,8},{10,11... | collective-permute-start | bytes 2359304 | tf_op jit(solution)/shard_map/ppermute | solution.py:18
  157.6 55.2 %collective-permute-start.15 = (bf16[1024,384]{1,0:T(8,128)(2,1)}, bf16[1024,384]{1,0:T(8,128)(2,1)}, u32[]{:S(2)}, u32[]{:S(2)}) collective-permute-start(bf16[1024,384]{1,0:T(8,128)(2,1)} %collective-permute-done.13.refs_6_.refs_13_), channel_id=1, source_target_pairs={{0,1},{1,0},{2,3},{3,2},{4,5},{5,4},{6,7},{7,6},{8,9},{9,8},{10,11... | collective-permute-start | bytes 2359304 | tf_op jit(solution)/shard_map/ppermute | solution.py:18
  157.9 54.9 %collective-permute-start.18 = (bf16[384,1024]{1,0:T(8,128)(2,1)}, bf16[384,1024]{1,0:T(8,128)(2,1)}, u32[]{:S(2)}, u32[]{:S(2)}) collective-permute-start(bf16[384,1024]{1,0:T(8,128)(2,1)} %collective-permute-done.16.refs_10_.refs_17_), channel_id=1, source_target_pairs={{0,1},{1,0},{2,3},{3,2},{4,5},{5,4},{6,7},{7,6},{8,9},{9,8},{10,11... | collective-permute-start | bytes 2359304 | tf_op jit(solution)/shard_map/ppermute | solution.py:18
  178.3 34.4 %collective-permute-start.23 = (bf16[384,1024]{1,0:T(8,128)(2,1)}, bf16[384,1024]{1,0:T(8,128)(2,1)}, u32[]{:S(2)}, u32[]{:S(2)}) collective-permute-start(bf16[384,1024]{1,0:T(8,128)(2,1)} %collective-permute-done.22.refs_17_.refs_24_), channel_id=1, source_target_pairs={{0,16},{16,0},{1,17},{17,1},{2,18},{18,2},{3,19},{19,3},{4,20},{20... | collective-permute-start | bytes 2359304 | tf_op jit(solution)/shard_map/ppermute | solution.py:18
  251.5 44.5 %collective-permute-start.31 = (bf16[256,1024]{1,0:T(8,128)(2,1)S(1)}, bf16[256,1024]{1,0:T(8,128)(2,1)S(1)}, u32[]{:S(2)}, u32[]{:S(2)}) collective-permute-start(bf16[256,1024]{1,0:T(8,128)(2,1)S(1)} %get-tuple-element.22), channel_id=1, source_target_pairs={{0,2},{2,0},{4,6},{6,4},{8,10},{10,8},{12,14},{14,12},{1,3},{3,1},... | collective-permute-start | bytes 1572872 | tf_op jit(solution)/shard_map/ppermute | solution.py:18
  252.7 43.4 %collective-permute-start.33 = (bf16[256,1024]{1,0:T(8,128)(2,1)S(1)}, bf16[256,1024]{1,0:T(8,128)(2,1)S(1)}, u32[]{:S(2)}, u32[]{:S(2)}) collective-permute-start(bf16[256,1024]{1,0:T(8,128)(2,1)S(1)} %get-tuple-element.24), channel_id=1, source_target_pairs={{0,4},{2,6},{4,0},{6,2},{8,12},{10,14},{12,8},{14,10},{1,5},{3,7},... | collective-permute-start | bytes 1572872 | tf_op jit(solution)/shard_map/ppermute | solution.py:18
  (55 other events, 718.1 us)

commit v6 on v5

--- a/solution.py
+++ b/solution.py
@@ -456,7 +456,6 @@
         weights = Weights(up_weight[0], down_weight[0])
         table = expert_weights(routing, combine, routing.shape[-1])
         half_size = table.shape[1] // 2
-        arriving = [exchange(table[:, :half_size], "row", 1), exchange(table[:, half_size:], "row", 2)]
         near = exchange(weights.part, "row", 3)
         far_up = exchange(weights.part[0], "row", 4)
         bias = gate(bias, far_up, *near)
@@ -476,6 +475,8 @@
         near_all = Weights.spread(near)
         far_down = exchange(weights.part[1], "row", 4)
         far_near_up = exchange(far_up, "row", 3)
+        late_table = tie(table, mixed)
+        arriving = [exchange(late_table[:, :half_size], "row", 1), exchange(late_table[:, half_size:], "row", 2)]
         gain = gate(gain, far_down, far_near_up, *near_all[0], *near_all[1], *arriving)
     residual, *norms = add_mixing(
         by_row.reshape(mixed.shape), jnp.asarray(inverse_cols), flat_tokens, gain

time: 305 us -> 306 us (level)
  starting transfers between devices: 40.6 us -> 48.1 us
  local copies, waits for them, and re-layouts: 28.9 us -> 23.3 us
    ppermute x34, waiting for transfers between devices: 115 us -> 137 us  [exchange(): return lax.ppermute(value, axis, pairs)]
    all_to_all x1, waiting for transfers between devices: 21.8 us -> 0.01 us  [per_device(): lax.all_to_all(mixed.reshape(n_dev, -1, mixed.shape[1]), axes, split_axis...]
    unnamed x88 -> x54, local copies, waits for them, and re-layouts: 22.1 us -> 17.6 us
    ppermute x34, starting transfers between devices: 30.4 us -> 34.9 us  [exchange(): return lax.ppermute(value, axis, pairs)]
  transfers between devices with their start and end apart: 36 -> 36, of which waited for: 6 -> 8; matrix products, arithmetic and copies ran while one was open for 4% -> 4% of each run, Pallas kernels for 28% -> 27%
where the time goes in v6:
time: 306 us; the launch traced here: 301 us
  waiting for transfers between devices  137 us (45%)
  Pallas kernels  83.7 us (27%)
  starting transfers between devices  48.1 us (16%)
  local copies, waits for them, and re-layouts  23.3 us (8%)
  other arithmetic  7.21 us (2%)
    ppermute x34, waiting for transfers between devices, exchange(): return lax.ppermute(value, axis, pairs)  137 us
    pallas_call x4, Pallas kernels, run_experts(): pl.pallas_call(functools.partial(experts_kernel, counts, len(sets), len(o...  66.7 us
    ppermute x34, starting transfers between devices, exchange(): return lax.ppermute(value, axis, pairs)  34.9 us
    unnamed x54, local copies, waits for them, and re-layouts  17.6 us
    all_to_all x1, starting transfers between devices, per_device(): lax.all_to_all(mixed.reshape(n_dev, -1, mixed.shape[1]), axes, split_axis...  6.75 us
    all_to_all x1, starting transfers between devices, per_device(): lax.all_to_all(spectra.reshape(n_dev, -1, spectra.shape[1]), axes, split_...  6.4 us
  transfers between devices with their start and end apart: 36, of which 8 were waited for; matrix products, arithmetic and copies ran while one was open for 4% of the time, Pallas kernels for 27%

profile of v6, /device:TPU:0, one launch (start us, length us, event | category | flops | bytes accessed | tf_op | source)
XLA Modules:
  0.0 300.6 jit_solution(7776541558946441186)
XLA Ops:
  3.0 4.0 %collective-permute-start = (bf16[1024,384]{1,0:T(8,128)(2,1)}, bf16[1024,384]{1,0:T(8,128)(2,1)}, u32[]{:S(2)}, u32[]{:S(2)}) collective-permute-start(bf16[1024,384]{1,0:T(8,128)(2,1)} %dynamic-slice_bitcast_fusion.1), channel_id=1, source_target_pairs={{0,8},{2,10},{4,12},{6,14},{8,0},{10,2},{12,4},{14,6},{1,9},{3,11}... | collective-permute-start | bytes 2359304 | tf_op jit(solution)/shard_map/ppermute | solution.py:18
  7.0 2.5 collective-permute-start.1
  13.6 4.4 %column_spectra.1 = bf16[256,4096]{1,0:T(8,128)(2,1)S(1)} custom-call(bf16[1024,1024]{1,0:T(8,128)(2,1)S(1)} %bitcast.79, f32[1,1024]{1,0:T(1,128)S(1)} %bitcast.81, bf16[4,256,1024]{2,1,0:T(8,128)(2,1)S(1)} %copy-done.18), custom_call_target="tpu_custom_call" | custom-call | flops 2147483648 | bytes 6291456 | tf_op jit(solution)/shard_map/column_spectra/pallas_call | solution.py:88
  19.4 6.4 %all-to-all-start = ((bf16[16,16,4096]{2,1,0:T(8,128)(2,1)}), bf16[16,16,4096]{2,1,0:T(8,128)(2,1)S(1)}, u32[]{:S(2)}, u32[]{:S(2)}) async-start(bf16[16,16,4096]{2,1,0:T(8,128)(2,1)} %bitcast.68), calls=%async_computation | async-start | bytes 4194304 | tf_op jit(solution)/shard_map/all_to_all | solution.py:447
  31.7 50.4 %collective-permute-done.2.refs_3_.refs_7_.refs_10_.refs_8_ = bf16[384,1024]{1,0:T(8,128)(2,1)} collective-permute-done((bf16[384,1024]{1,0:T(8,128)(2,1)}, bf16[384,1024]{1,0:T(8,128)(2,1)}, u32[]{:S(2)}, u32[]{:S(2)}) %collective-permute-start.2) | collective-permute-done | bytes 786464 | tf_op jit(solution)/shard_map/ppermute | solution.py:18
  86.1 16.8 %collective-permute-done.8.refs_8_.refs_11_.refs_9_ = bf16[384,1024]{1,0:T(8,128)(2,1)} collective-permute-done((bf16[384,1024]{1,0:T(8,128)(2,1)}, bf16[384,1024]{1,0:T(8,128)(2,1)}, u32[]{:S(2)}, u32[]{:S(2)}) %collective-permute-start.8) | collective-permute-done | bytes 786464 | tf_op jit(solution)/shard_map/ppermute | solution.py:18
  102.9 10.2 %collective-permute-done.5.refs_4_.refs_7_.refs_5_ = bf16[1024,384]{1,0:T(8,128)(2,1)} collective-permute-done((bf16[1024,384]{1,0:T(8,128)(2,1)}, bf16[1024,384]{1,0:T(8,128)(2,1)}, u32[]{:S(2)}, u32[]{:S(2)}) %collective-permute-start.5) | collective-permute-done | bytes 786464 | tf_op jit(solution)/shard_map/ppermute | solution.py:18
  116.4 5.8 %mix_modes.1 = bf16[256,4096]{1,0:T(8,128)(2,1)S(1)} custom-call(bf16[256,4096]{1,0:T(8,128)(2,1)S(1)} %bitcast.67, bf16[2,512,256]{2,1,0:T(8,128)(2,1)S(1)} %copy-done.3, bf16[8,256,256]{2,1,0:T(8,128)(2,1)S(1)} %get-tuple-element.53.first, bf16[8,256,256]{2,1,0:T(8,128)(2,1)S(1)} %copy-done.2, f32[8,256]{1,0:T(8,128)S(1)} %gate.2.bias, ...), custom_call_target="tpu_custom_call" | custom-call | flops 4294967296 | bytes 6291456 | tf_op jit(solution)/shard_map/mix_modes/pallas_call | solution.py:139
  123.6 4.7 %collective-permute-done.4.refs_2_.refs_13_.refs_20_ = bf16[1024,384]{1,0:T(8,128)(2,1)} collective-permute-done((bf16[1024,384]{1,0:T(8,128)(2,1)}, bf16[1024,384]{1,0:T(8,128)(2,1)}, u32[]{:S(2)}, u32[]{:S(2)}) %collective-permute-start.4) | collective-permute-done | bytes 786464 | tf_op jit(solution)/shard_map/ppermute | solution.py:18
  129.8 5.4 %collective-permute-start.12 = (f32[4,512]{1,0:T(4,128)S(1)}, f32[4,512]{1,0:T(4,128)S(1)}, u32[]{:S(2)}, u32[]{:S(2)}) collective-permute-start(f32[4,512]{1,0:T(4,128)S(1)} %get-tuple-element.39), channel_id=1, source_target_pairs={{0,4},{2,6},{4,0},{6,2},{8,12},{10,14},{12,8},{14,10},{1,5},{3,7},... | collective-permute-start | bytes 24584 | tf_op jit(solution)/shard_map/ppermute | solution.py:18
  135.7 6.7 %all-to-all-start.1 = ((bf16[16,16,4096]{2,1,0:T(8,128)(2,1)}), bf16[16,16,4096]{2,1,0:T(8,128)(2,1)S(1)}, u32[]{:S(2)}, u32[]{:S(2)}) async-start(bf16[16,16,4096]{2,1,0:T(8,128)(2,1)} %bitcast.69), calls=%async_computation.1 | async-start | bytes 4194304 | tf_op jit(solution)/shard_map/all_to_all | solution.py:471
  145.1 2.9 collective-permute-start.22
  148.0 15.2 %collective-permute-done.13.refs_6_.refs_13_ = bf16[1024,384]{1,0:T(8,128)(2,1)} collective-permute-done((bf16[1024,384]{1,0:T(8,128)(2,1)}, bf16[1024,384]{1,0:T(8,128)(2,1)}, u32[]{:S(2)}, u32[]{:S(2)}) %collective-permute-start.13) | collective-permute-done | bytes 786464 | tf_op jit(solution)/shard_map/ppermute | solution.py:18
  164.7 15.4 %collective-permute-done.16.refs_10_.refs_17_ = bf16[384,1024]{1,0:T(8,128)(2,1)} collective-permute-done((bf16[384,1024]{1,0:T(8,128)(2,1)}, bf16[384,1024]{1,0:T(8,128)(2,1)}, u32[]{:S(2)}, u32[]{:S(2)}) %collective-permute-start.16) | collective-permute-done | bytes 786464 | tf_op jit(solution)/shard_map/ppermute | solution.py:18
  182.3 15.7 %collective-permute-done.22.refs_17_.refs_24_ = bf16[384,1024]{1,0:T(8,128)(2,1)} collective-permute-done((bf16[384,1024]{1,0:T(8,128)(2,1)}, bf16[384,1024]{1,0:T(8,128)(2,1)}, u32[]{:S(2)}, u32[]{:S(2)}) %collective-permute-start.22) | collective-permute-done | bytes 786464 | tf_op jit(solution)/shard_map/ppermute | solution.py:18
  203.9 4.5 %add_mixing.1 = (bf16[1024,1024]{1,0:T(8,128)(2,1)S(1)}, bf16[256,1024]{1,0:T(8,128)(2,1)S(1)}, bf16[256,1024]{1,0:T(8,128)(2,1)S(1)}, bf16[256,1024]{1,0:T(8,128)(2,1)S(1)}, bf16[256,1024]{1,0:T(8,128)(2,1)S(1)}) custom-call(bf16[256,4096]{1,0:T(8,128)(2,1)S(1)} %bitcast.70, bf16[4,1024,256]{2,1,0:T(8,128)(2,1)S(1)} %copy-done.17, ...), custom_call_target="tpu_custom_call" | custom-call | flops 2147483648 | bytes 10485760 | tf_op jit(solution)/shard_map/add_mixing/pallas_call | solution.py:193
  208.9 8.8 %collective-permute-done.23.refs_18_.refs_25_ = bf16[384,1024]{1,0:T(8,128)(2,1)} collective-permute-done((bf16[384,1024]{1,0:T(8,128)(2,1)}, bf16[384,1024]{1,0:T(8,128)(2,1)}, u32[]{:S(2)}, u32[]{:S(2)}) %collective-permute-start.23) | collective-permute-done | bytes 786464 | tf_op jit(solution)/shard_map/ppermute | solution.py:18
  218.5 3.2 %collective-permute-start.30 = (bf16[256,1024]{1,0:T(8,128)(2,1)S(1)}, bf16[256,1024]{1,0:T(8,128)(2,1)S(1)}, u32[]{:S(2)}, u32[]{:S(2)}) collective-permute-start(bf16[256,1024]{1,0:T(8,128)(2,1)S(1)} %get-tuple-element.21.refs_3_), channel_id=1, source_target_pairs={{0,4},{2,6},{4,0},{6,2},{8,12},{10,14},{12,8},{14,10},{1,5},{3,7},... | collective-permute-start | bytes 1572872 | tf_op jit(solution)/shard_map/ppermute | solution.py:18
  221.7 14.6 %experts.4.refs_4_ = f32[1024,1024]{1,0:T(8,128)S(1)} custom-call(f32[1024,2]{1,0:T(8,128)S(1)} %copy.33.weights, bf16[256,1024]{1,0:T(8,128)(2,1)S(1)} %get-tuple-element.18.refs_0_, bf16[256,1024]{1,0:T(8,128)(2,1)S(1)} %get-tuple-element.19.refs_1_, bf16[256,1024]{1,0:T(8,128)(2,1)S(1)} %get-tuple-element.20.refs_2_, ...), custom_call_target="tpu_custom_call" | custom-call | flops 12884901888 | bytes 20971520 | tf_op jit(solution)/shard_map/experts/pallas_call | solution.py:341
  239.1 17.6 %experts.7 = (bf16[256,1024]{1,0:T(8,128)(2,1)S(1)}, bf16[256,1024]{1,0:T(8,128)(2,1)S(1)}) custom-call(f32[512,4]{1,0:T(8,128)S(1)} %copy-done.5, bf16[256,1024]{1,0:T(8,128)(2,1)S(1)} %collective-permute-done.29.refs_0_, bf16[256,1024]{1,0:T(8,128)(2,1)S(1)} %collective-permute-done.30.refs_1_, bf16[1024,1536]{1,0:T(8,128)(2,1)} %bitcast.71, ...), custom_call_target="tpu_custom_call" | custom-call | flops 12884901888 | bytes 29360128 | tf_op jit(solution)/shard_map/experts/pallas_call | solution.py:341
  260.1 17.6 %experts.6 = (bf16[256,1024]{1,0:T(8,128)(2,1)S(1)}, bf16[256,1024]{1,0:T(8,128)(2,1)S(1)}) custom-call(f32[512,4]{1,0:T(8,128)S(1)} %copy.35.weights, bf16[256,1024]{1,0:T(8,128)(2,1)S(1)} %collective-permute-done.26.refs_0_, bf16[256,1024]{1,0:T(8,128)(2,1)S(1)} %collective-permute-done.27.refs_1_, bf16[1024,1536]{1,0:T(8,128)(2,1)} %bitcast.72, ...), custom_call_target="tpu_custom_call" | custom-call | flops 12884901888 | bytes 29360128 | tf_op jit(solution)/shard_map/experts/pallas_call | solution.py:341
  278.7 2.2 copy-done.20
  280.9 16.8 %experts.5.own = f32[1024,1024]{1,0:T(8,128)S(1)} custom-call(f32[1024,2]{1,0:T(8,128)S(1)} %copy.34.weights, bf16[256,1024]{1,0:T(8,128)(2,1)S(1)} %get-tuple-element.18.refs_0_, bf16[256,1024]{1,0:T(8,128)(2,1)S(1)} %get-tuple-element.19.refs_1_, bf16[256,1024]{1,0:T(8,128)(2,1)S(1)} %get-tuple-element.20.refs_2_, bf16[256,1024]{1,0:T(8,128)(2,1)S(1)} %copy-done.15, ...), custom_call_target="tpu_custom_call" | custom-call | flops 12884901888 | bytes 20971520 | tf_op jit(solution)/shard_map/experts/pallas_call | solution.py:341
  297.8 2.3 add_outputs.1
  (139 shorter events, 45.3 us)
Async XLA Ops:
  3.0 82.6 %collective-permute-start = (bf16[1024,384]{1,0:T(8,128)(2,1)}, bf16[1024,384]{1,0:T(8,128)(2,1)}, u32[]{:S(2)}, u32[]{:S(2)}) collective-permute-start(bf16[1024,384]{1,0:T(8,128)(2,1)} %dynamic-slice_bitcast_fusion.1), channel_id=1, source_target_pairs={{0,8},{2,10},{4,12},{6,14},{8,0},{10,2},{12,4},{14,6},{1,9},{3,11}... | collective-permute-start | bytes 2359304 | tf_op jit(solution)/shard_map/ppermute | solution.py:18
  7.0 76.6 %collective-permute-start.1 = (bf16[1024,384]{1,0:T(8,128)(2,1)}, bf16[1024,384]{1,0:T(8,128)(2,1)}, u32[]{:S(2)}, u32[]{:S(2)}) collective-permute-start(bf16[1024,384]{1,0:T(8,128)(2,1)} %dynamic-slice_bitcast_fusion.1), channel_id=1, source_target_pairs={{0,6},{2,4},{4,2},{6,0},{8,14},{10,12},{12,10},{14,8},{1,7},{3,5},... | collective-permute-start | bytes 2359304 | tf_op jit(solution)/shard_map/ppermute | solution.py:18
  11.6 70.5 %collective-permute-start.2 = (bf16[384,1024]{1,0:T(8,128)(2,1)}, bf16[384,1024]{1,0:T(8,128)(2,1)}, u32[]{:S(2)}, u32[]{:S(2)}) collective-permute-start(bf16[384,1024]{1,0:T(8,128)(2,1)} %dynamic-slice_bitcast_fusion), channel_id=1, source_target_pairs={{0,6},{2,4},{4,2},{6,0},{8,14},{10,12},{12,10},{14,8},{1,7},{3,5},... | collective-permute-start | bytes 2359304 | tf_op jit(solution)/shard_map/ppermute | solution.py:18
  12.0 74.0 %collective-permute-start.3 = (bf16[384,1024]{1,0:T(8,128)(2,1)}, bf16[384,1024]{1,0:T(8,128)(2,1)}, u32[]{:S(2)}, u32[]{:S(2)}) collective-permute-start(bf16[384,1024]{1,0:T(8,128)(2,1)} %dynamic-slice_bitcast_fusion), channel_id=1, source_target_pairs={{0,8},{2,10},{4,12},{6,14},{8,0},{10,2},{12,4},{14,6},{1,9},{3,11}... | collective-permute-start | bytes 2359304 | tf_op jit(solution)/shard_map/ppermute | solution.py:18
  19.4 93.8 %all-to-all-start = ((bf16[16,16,4096]{2,1,0:T(8,128)(2,1)}), bf16[16,16,4096]{2,1,0:T(8,128)(2,1)S(1)}, u32[]{:S(2)}, u32[]{:S(2)}) async-start(bf16[16,16,4096]{2,1,0:T(8,128)(2,1)} %bitcast.68), calls=%async_computation | async-start | bytes 4194304 | tf_op jit(solution)/shard_map/all_to_all | solution.py:447
  83.6 29.5 %collective-permute-start.5 = (bf16[1024,384]{1,0:T(8,128)(2,1)}, bf16[1024,384]{1,0:T(8,128)(2,1)}, u32[]{:S(2)}, u32[]{:S(2)}) collective-permute-start(bf16[1024,384]{1,0:T(8,128)(2,1)} %collective-permute-done.1.refs_2_.refs_3_.refs_6_.refs_4_), channel_id=1, source_target_pairs={{0,16},{16,0},{1,17},{17,1},{2,18},{18,2},{3,19},{19,3},{4,20},{20... | collective-permute-start | bytes 2359304 | tf_op jit(solution)/shard_map/ppermute | solution.py:18
  85.6 44.3 %collective-permute-start.6 = (bf16[1024,384]{1,0:T(8,128)(2,1)}, bf16[1024,384]{1,0:T(8,128)(2,1)}, u32[]{:S(2)}, u32[]{:S(2)}) collective-permute-start(bf16[1024,384]{1,0:T(8,128)(2,1)} %collective-permute-done.1.refs_2_.refs_3_.refs_6_.refs_4_), channel_id=1, source_target_pairs={{0,1},{1,0},{2,3},{3,2},{4,5},{5,4},{6,7},{7,6},{8,9},{9,8},{10,11... | collective-permute-start | bytes 2359304 | tf_op jit(solution)/shard_map/ppermute | solution.py:18
  85.6 56.9 %collective-permute-start.9 = (bf16[384,1024]{1,0:T(8,128)(2,1)}, bf16[384,1024]{1,0:T(8,128)(2,1)}, u32[]{:S(2)}, u32[]{:S(2)}) collective-permute-start(bf16[384,1024]{1,0:T(8,128)(2,1)} %collective-permute-done.2.refs_3_.refs_7_.refs_10_.refs_8_), channel_id=1, source_target_pairs={{0,1},{1,0},{2,3},{3,2},{4,5},{5,4},{6,7},{7,6},{8,9},{9,8},{10,11... | collective-permute-start | bytes 2359304 | tf_op jit(solution)/shard_map/ppermute | solution.py:18
  86.1 42.2 %collective-permute-start.4 = (bf16[1024,384]{1,0:T(8,128)(2,1)}, bf16[1024,384]{1,0:T(8,128)(2,1)}, u32[]{:S(2)}, u32[]{:S(2)}) collective-permute-start(bf16[1024,384]{1,0:T(8,128)(2,1)} %collective-permute-done.refs_1_.refs_5_.refs_12_), channel_id=1, source_target_pairs={{0,6},{2,4},{4,2},{6,0},{8,14},{10,12},{12,10},{14,8},{1,7},{3,5},... | collective-permute-start | bytes 2359304 | tf_op jit(solution)/shard_map/ppermute | solution.py:18
  102.9 41.1 %collective-permute-start.10 = (bf16[384,1024]{1,0:T(8,128)(2,1)}, bf16[384,1024]{1,0:T(8,128)(2,1)}, u32[]{:S(2)}, u32[]{:S(2)}) collective-permute-start(bf16[384,1024]{1,0:T(8,128)(2,1)} %collective-permute-done.8.refs_8_.refs_11_.refs_9_), channel_id=1, source_target_pairs={{0,1},{1,0},{2,3},{3,2},{4,5},{5,4},{6,7},{7,6},{8,9},{9,8},{10,11... | collective-permute-start | bytes 2359304 | tf_op jit(solution)/shard_map/ppermute | solution.py:18
  113.1 31.4 %collective-permute-start.7 = (bf16[1024,384]{1,0:T(8,128)(2,1)}, bf16[1024,384]{1,0:T(8,128)(2,1)}, u32[]{:S(2)}, u32[]{:S(2)}) collective-permute-start(bf16[1024,384]{1,0:T(8,128)(2,1)} %collective-permute-done.5.refs_4_.refs_7_.refs_5_), channel_id=1, source_target_pairs={{0,1},{1,0},{2,3},{3,2},{4,5},{5,4},{6,7},{7,6},{8,9},{9,8},{10,11... | collective-permute-start | bytes 2359304 | tf_op jit(solution)/shard_map/ppermute | solution.py:18
  135.7 65.0 %all-to-all-start.1 = ((bf16[16,16,4096]{2,1,0:T(8,128)(2,1)}), bf16[16,16,4096]{2,1,0:T(8,128)(2,1)S(1)}, u32[]{:S(2)}, u32[]{:S(2)}) async-start(bf16[16,16,4096]{2,1,0:T(8,128)(2,1)} %bitcast.69), calls=%async_computation.1 | async-start | bytes 4194304 | tf_op jit(solution)/shard_map/all_to_all | solution.py:471
  144.0 36.0 %collective-permute-start.16 = (bf16[384,1024]{1,0:T(8,128)(2,1)}, bf16[384,1024]{1,0:T(8,128)(2,1)}, u32[]{:S(2)}, u32[]{:S(2)}) collective-permute-start(bf16[384,1024]{1,0:T(8,128)(2,1)} %collective-permute-done.3.refs_1_.refs_9_.refs_16_), channel_id=1, source_target_pairs={{0,16},{16,0},{1,17},{17,1},{2,18},{18,2},{3,19},{19,3},{4,20},{20... | collective-permute-start | bytes 2359304 | tf_op jit(solution)/shard_map/ppermute | solution.py:18
  144.6 35.5 %collective-permute-start.14 = (bf16[1024,384]{1,0:T(8,128)(2,1)}, bf16[1024,384]{1,0:T(8,128)(2,1)S(1)}, u32[]{:S(2)}, u32[]{:S(2)}) collective-permute-start(bf16[1024,384]{1,0:T(8,128)(2,1)} %collective-permute-done.refs_1_.refs_5_.refs_12_), channel_id=1, source_target_pairs={{0,1},{1,0},{2,3},{3,2},{4,5},{5,4},{6,7},{7,6},{8,9},{9,8},{10,11... | collective-permute-start | bytes 2359304 | tf_op jit(solution)/shard_map/ppermute | solution.py:18
  144.6 36.9 %collective-permute-start.17 = (bf16[384,1024]{1,0:T(8,128)(2,1)}, bf16[384,1024]{1,0:T(8,128)(2,1)S(1)}, u32[]{:S(2)}, u32[]{:S(2)}) collective-permute-start(bf16[384,1024]{1,0:T(8,128)(2,1)} %collective-permute-done.3.refs_1_.refs_9_.refs_16_), channel_id=1, source_target_pairs={{0,1},{1,0},{2,3},{3,2},{4,5},{5,4},{6,7},{7,6},{8,9},{9,8},{10,11... | collective-permute-start | bytes 2359304 | tf_op jit(solution)/shard_map/ppermute | solution.py:18
  145.1 53.0 %collective-permute-start.22 = (bf16[384,1024]{1,0:T(8,128)(2,1)}, bf16[384,1024]{1,0:T(8,128)(2,1)}, u32[]{:S(2)}, u32[]{:S(2)}) collective-permute-start(bf16[384,1024]{1,0:T(8,128)(2,1)} %collective-permute-done.3.refs_1_.refs_9_.refs_16_), channel_id=1, source_target_pairs={{0,6},{2,4},{4,2},{6,0},{8,14},{10,12},{12,10},{14,8},{1,7},{3,5},... | collective-permute-start | bytes 2359304 | tf_op jit(solution)/shard_map/ppermute | solution.py:18
  163.2 45.2 %collective-permute-start.19 = (bf16[1024,384]{1,0:T(8,128)(2,1)}, bf16[1024,384]{1,0:T(8,128)(2,1)}, u32[]{:S(2)}, u32[]{:S(2)}) collective-permute-start(bf16[1024,384]{1,0:T(8,128)(2,1)} %collective-permute-done.4.refs_2_.refs_13_.refs_20_), channel_id=1, source_target_pairs={{0,16},{16,0},{1,17},{17,1},{2,18},{18,2},{3,19},{19,3},{4,20},{20... | collective-permute-start | bytes 2359304 | tf_op jit(solution)/shard_map/ppermute | solution.py:18
  180.0 28.4 %collective-permute-start.20 = (bf16[1024,384]{1,0:T(8,128)(2,1)}, bf16[1024,384]{1,0:T(8,128)(2,1)}, u32[]{:S(2)}, u32[]{:S(2)}) collective-permute-start(bf16[1024,384]{1,0:T(8,128)(2,1)} %collective-permute-done.4.refs_2_.refs_13_.refs_20_), channel_id=1, source_target_pairs={{0,1},{1,0},{2,3},{3,2},{4,5},{5,4},{6,7},{7,6},{8,9},{9,8},{10,11... | collective-permute-start | bytes 2359304 | tf_op jit(solution)/shard_map/ppermute | solution.py:18
  180.9 36.8 %collective-permute-start.15 = (bf16[1024,384]{1,0:T(8,128)(2,1)}, bf16[1024,384]{1,0:T(8,128)(2,1)}, u32[]{:S(2)}, u32[]{:S(2)}) collective-permute-start(bf16[1024,384]{1,0:T(8,128)(2,1)} %collective-permute-done.13.refs_6_.refs_13_), channel_id=1, source_target_pairs={{0,1},{1,0},{2,3},{3,2},{4,5},{5,4},{6,7},{7,6},{8,9},{9,8},{10,11... | collective-permute-start | bytes 2359304 | tf_op jit(solution)/shard_map/ppermute | solution.py:18
  182.3 36.2 %collective-permute-start.18 = (bf16[384,1024]{1,0:T(8,128)(2,1)}, bf16[384,1024]{1,0:T(8,128)(2,1)}, u32[]{:S(2)}, u32[]{:S(2)}) collective-permute-start(bf16[384,1024]{1,0:T(8,128)(2,1)} %collective-permute-done.16.refs_10_.refs_17_), channel_id=1, source_target_pairs={{0,1},{1,0},{2,3},{3,2},{4,5},{5,4},{6,7},{7,6},{8,9},{9,8},{10,11... | collective-permute-start | bytes 2359304 | tf_op jit(solution)/shard_map/ppermute | solution.py:18
  208.3 30.0 %collective-permute-start.21 = (bf16[1024,384]{1,0:T(8,128)(2,1)}, bf16[1024,384]{1,0:T(8,128)(2,1)S(1)}, u32[]{:S(2)}, u32[]{:S(2)}) collective-permute-start(bf16[1024,384]{1,0:T(8,128)(2,1)} %collective-permute-done.19.refs_14_.refs_21_), channel_id=1, source_target_pairs={{0,1},{1,0},{2,3},{3,2},{4,5},{5,4},{6,7},{7,6},{8,9},{9,8},{10,11... | collective-permute-start | bytes 2359304 | tf_op jit(solution)/shard_map/ppermute | solution.py:18
  208.4 30.6 %collective-permute-start.24 = (bf16[384,1024]{1,0:T(8,128)(2,1)}, bf16[384,1024]{1,0:T(8,128)(2,1)S(1)}, u32[]{:S(2)}, u32[]{:S(2)}) collective-permute-start(bf16[384,1024]{1,0:T(8,128)(2,1)} %collective-permute-done.22.refs_17_.refs_24_), channel_id=1, source_target_pairs={{0,1},{1,0},{2,3},{3,2},{4,5},{5,4},{6,7},{7,6},{8,9},{9,8},{10,11... | collective-permute-start | bytes 2359304 | tf_op jit(solution)/shard_map/ppermute | solution.py:18
  256.8 40.9 %collective-permute-start.31 = (bf16[256,1024]{1,0:T(8,128)(2,1)S(1)}, bf16[256,1024]{1,0:T(8,128)(2,1)S(1)}, u32[]{:S(2)}, u32[]{:S(2)}) collective-permute-start(bf16[256,1024]{1,0:T(8,128)(2,1)S(1)} %get-tuple-element.24), channel_id=1, source_target_pairs={{0,2},{2,0},{4,6},{6,4},{8,10},{10,8},{12,14},{14,12},{1,3},{3,1},... | collective-permute-start | bytes 1572872 | tf_op jit(solution)/shard_map/ppermute | solution.py:18
  258.1 39.6 %collective-permute-start.33 = (bf16[256,1024]{1,0:T(8,128)(2,1)S(1)}, bf16[256,1024]{1,0:T(8,128)(2,1)S(1)}, u32[]{:S(2)}, u32[]{:S(2)}) collective-permute-start(bf16[256,1024]{1,0:T(8,128)(2,1)S(1)} %get-tuple-element.26), channel_id=1, source_target_pairs={{0,4},{2,6},{4,0},{6,2},{8,12},{10,14},{12,8},{14,10},{1,5},{3,7},... | collective-permute-start | bytes 1572872 | tf_op jit(solution)/shard_map/ppermute | solution.py:18
  (38 other events, 452.2 us)
